TPU v7x, 32 devices: a whole 2x2x4 slice. The times are simulated.
32 devices in a mesh: row: 8 (over z, x), col: 4 (over y, core).
Axes of the slice: x: 2, y: 2, z: 4, core: 2. Of those that a mesh axis runs over, the one named last changes fastest.
Arguments:
- hidden_in: bfloat16 [6144, 5120], P('row', 'col'), may hold values from -6 to 6
- modulation: bfloat16 [24, 3, 5120], P(None, None, 'col'), may hold values from -3 to 3
- w_qkv: bfloat16 [5120, 12288], P('row', 'col'), may hold values from -0.078125 to 0.078125
- w_out: bfloat16 [4096, 5120], P('row', 'col'), may hold values from -0.09375 to 0.09375
- prefix_cache: bfloat16 [8, 256, 8192], P('row', None, 'col'), may hold values from -48 to 48
- req_group: int32 [24], replicated, may hold values from 0 to 3
- req_len: int32 [24], replicated, may hold values from 1 to 672, 6144 in all
- owner: int32 [4], replicated, may hold values from 0 to 7, as said below
Outputs:
- hidden_out: bfloat16 [6144, 5120], P('row', 'col')
- suffix_keys: bfloat16 [6144, 4096], P('row', 'col')
- suffix_values: bfloat16 [6144, 4096], P('row', 'col')
Inputs may be any that keep to these rules, and one draw needn't show every extreme that they name: `owner`: the 4 slots are distinct; slot 0 and slot 8 - 1 always hold a group.
All inputs are finite; a program needn't handle non-finite values.
Results may differ from a plain program's by a relative error of at most 0.006.
Values may be sent and summed in bfloat16 or wider, within the bound.
No kernel may reach another device: no remote copies, remote signals or barrier semaphores. Data moves between devices by JAX's collectives and lax.ppermute only.
A program may use at most 192 MiB of HBM per device.

v0:
```python
import math

import jax
import jax.numpy as jnp
from jax import lax
from jax.sharding import PartitionSpec as P

HD = 128


neg_fill = -1e30


def with_halo(block, sides, width):
    for axis, dim in sides:
        count = lax.axis_size(axis)
        forward = [(i, i + 1) for i in range(count - 1)]
        backward = [(target, source) for source, target in forward]
        low = lax.ppermute(
            lax.slice_in_dim(block, block.shape[dim] - width, None, axis=dim), axis, forward
        )
        high = lax.ppermute(lax.slice_in_dim(block, 0, width, axis=dim), axis, backward)
        block = jnp.concatenate([low, block, high], axis=dim)
    return block


def request_of(positions, req_len):
    starts = jnp.cumsum(req_len) - req_len
    inside = (starts[None, :] <= positions[:, None]).astype(jnp.int32)
    return jnp.sum(inside, axis=1) - 1


def attend(running, queries, key_block, value_block, allowed):
    largest, denominator, summed = running
    scores = jnp.einsum("thd,khd->thk", queries, key_block, preferred_element_type=jnp.float32)
    scores = scores * (1.0 / math.sqrt(queries.shape[-1]))
    widened = allowed[:, None, :]
    scores = jnp.where(widened, scores, neg_fill)
    new_largest = jnp.maximum(largest, jnp.max(scores, axis=2))
    weights = jnp.where(widened, jnp.exp(scores - new_largest[:, :, None]), 0.0)
    rescale = jnp.exp(largest - new_largest)
    denominator = denominator * rescale + jnp.sum(weights, axis=2)
    summed = summed * rescale[:, :, None] + jnp.einsum(
        "thk,khd->thd",
        weights.astype(jnp.bfloat16),
        value_block,
        preferred_element_type=jnp.float32,
    )
    return (new_largest, denominator, summed)


def shards(hidden_in, modulation, w_qkv, w_out, prefix_cache, req_group, req_len, owner):
    token_rows = hidden_in.shape[0]
    full_hidden, full_modulation = (
        lax.all_gather(hidden_in, "col", axis=1, tiled=True),
        lax.all_gather(modulation, "col", axis=2, tiled=True),
    )
    full_width = full_hidden.shape[1]
    requests = req_len.shape[0]
    row_index = lax.axis_index("row")
    positions = row_index * token_rows + jnp.arange(token_rows, dtype=jnp.int32)
    request_id = request_of(positions, req_len)
    matches = request_id[:, None] == jnp.arange(requests, dtype=jnp.int32)[None, :]
    onehot = matches.astype(jnp.bfloat16)
    per_token = jnp.dot(
        onehot,
        full_modulation.reshape(requests, 3 * full_width),
        preferred_element_type=jnp.float32,
    )
    shift_rows = per_token[:, :full_width]
    scale_rows = per_token[:, full_width : 2 * full_width]
    gate_rows = jnp.dot(onehot, modulation[:, 2, :], preferred_element_type=jnp.float32)
    token_group = jnp.sum(jnp.where(matches, req_group[None, :], 0), axis=1)
    hidden_f = full_hidden.astype(jnp.float32)
    average = jnp.mean(hidden_f, axis=1, keepdims=True)
    centred = hidden_f - average
    variance = jnp.mean(centred * centred, axis=1, keepdims=True)
    modulated = (centred * lax.rsqrt(variance + 1e-06) * (1.0 + scale_rows) + shift_rows).astype(
        jnp.bfloat16
    )
    projected_qkv = jnp.dot(
        modulated,
        lax.all_gather(w_qkv, "row", axis=0, tiled=True),
        preferred_element_type=jnp.float32,
    )
    local_heads = w_qkv.shape[1] // (3 * HD)
    projected_qkv = projected_qkv.astype(jnp.bfloat16).reshape(token_rows, local_heads, 3, HD)
    queries = projected_qkv[:, :, 0]
    new_keys = projected_qkv[:, :, 1]
    new_values = projected_qkv[:, :, 2]
    key_value = projected_qkv[:, :, 1:].reshape(token_rows, local_heads * 2 * HD)
    surrounded = with_halo(key_value, (("row", 0),), token_rows)
    running = (
        jnp.full((token_rows, local_heads), neg_fill, jnp.float32),
        jnp.zeros((token_rows, local_heads), jnp.float32),
        jnp.zeros((token_rows, local_heads, HD), jnp.float32),
    )

    def slot_attend(carried, slot_data, group_number):
        present = token_group == group_number
        arranged = slot_data.reshape(slot_data.shape[0], local_heads, 2, HD)
        allowed = jnp.broadcast_to(present[:, None], (token_rows, slot_data.shape[0]))
        return attend(carried, queries, arranged[:, :, 0], arranged[:, :, 1], allowed)

    group_numbers = jnp.arange(owner.shape[0], dtype=jnp.int32)
    slot_block = lax.all_gather(prefix_cache, "row", axis=0, tiled=True)

    def one_slot(offset, current):
        group_number = jnp.sum(jnp.where(owner == offset, group_numbers + 1, 0)) - 1
        slot_data = lax.dynamic_index_in_dim(slot_block, offset, 0, keepdims=False)
        return slot_attend(current, slot_data, group_number)

    running = lax.fori_loop(0, slot_block.shape[0], one_slot, running)
    near_pairs = surrounded.reshape(3 * token_rows, local_heads, 2, HD)
    key_pos = (row_index - 1) * token_rows + jnp.arange(3 * token_rows, dtype=jnp.int32)
    key_req = request_of(key_pos, req_len)
    inside_range = key_pos < jnp.sum(req_len)
    near_mask = (key_req[None, :] == request_id[:, None]) & inside_range[None, :]
    running = attend(running, queries, near_pairs[:, :, 0], near_pairs[:, :, 1], near_mask)
    largest, denominator, summed = running
    attended = (
        (summed / denominator[:, :, None])
        .astype(jnp.bfloat16)
        .reshape(token_rows, local_heads * HD)
    )
    out_weight = lax.all_gather(w_out, "row", axis=0, tiled=True)
    projected = jnp.dot(
        lax.all_gather(attended, "col", axis=1, tiled=True),
        out_weight,
        preferred_element_type=jnp.float32,
    )
    hidden_out = (hidden_in.astype(jnp.float32) + gate_rows * projected).astype(jnp.bfloat16)
    return (
        hidden_out,
        new_keys.reshape(token_rows, local_heads * HD),
        new_values.reshape(token_rows, local_heads * HD),
    )


def solution(mesh):
    return jax.shard_map(
        shards,
        mesh=mesh,
        in_specs=(
            P("row", "col"),
            P(None, None, "col"),
            P("row", "col"),
            P("row", "col"),
            P("row", None, "col"),
            P(),
            P(),
            P(),
        ),
        out_specs=(P("row", "col"), P("row", "col"), P("row", "col")),
        check_vma=False,
    )
```

profile of v0, /device:TPU:0, one launch (start us, length us, event | category | flops | bytes accessed | tf_op | source)
XLA Modules:
  0.0 1206.1 jit_solution(14722354366863941986)
XLA Ops:
  11.1 9.8 all_gather.20
  21.8 18.4 %fusion.50 = f32[768,15360]{1,0:T(8,128)} fusion(bf16[24,15360]{1,0:T(8,128)(2,1)S(1)} %bitcast.106, s32[768]{0:T(1024)S(1)} %broadcast_add_fusion.1), kind=kOutput, calls=%fused_computation.68 | convolution fusion | flops 566249472 | bytes 47926272 | tf_op jit(solution)/shard_map/dot_general | solution.py:65
  43.0 24.6 %all-gather.8.cloned.1.call-done = bf16[768,5120]{1,0:T(8,128)(2,1)} async-done(((bf16[768,1280]{1,0:T(8,128)(2,1)}), bf16[768,5120]{1,0:T(8,128)(2,1)}) %all-gather.8.cloned.1.call-update) | async-done | bytes 7864336 | tf_op jit(solution)/shard_map/all_gather | solution.py:55
  75.3 592.3 %all-gather.10.cloned.1.call-done = bf16[5120,3072]{1,0:T(8,128)(2,1)} async-done(((bf16[640,3072]{1,0:T(8,128)(2,1)}), bf16[5120,3072]{1,0:T(8,128)(2,1)}) %all-gather.10.cloned.1.call-update) | async-done | bytes 31457296 | tf_op jit(solution)/shard_map/all_gather | solution.py:83
  667.6 44.1 %fusion.39 = bf16[768,3072]{1,0:T(8,128)(2,1)} fusion(bf16[5120,3072]{1,0:T(8,128)(2,1)} %all-gather.10.cloned.1.call-done, bf16[768,5120]{1,0:T(8,128)(2,1)} %all-gather.8.cloned.1.call-done, f32[768,15360]{1,0:T(8,128)} %fusion.50, f32[768]{0:T(1024)S(1)} %add_rsqrt_fusion, f32[768]{0:T(1024)S(1)} %broadcast_multiply_fusion), kind=kOutput, calls=%fused_computation.54 | convolution fusion | flops 24189075456 | bytes 75503616 | tf_op jit(solution)/shard_map/dot_general | solution.py:81
  711.7 6.6 copy.55
  730.9 169.0 %all-gather.6.cloned.1.call-done = bf16[8,256,2048]{2,1,0:T(8,128)(2,1)} async-done(((bf16[1,256,2048]{2,1,0:T(8,128)(2,1)}), bf16[8,256,2048]{2,1,0:T(8,128)(2,1)}) %all-gather.6.cloned.1.call-update) | async-done | bytes 8388624 | tf_op jit(solution)/shard_map/all_gather | solution.py:106
  900.0 147.7 %while.20 = (s32[]{:T(128)}, f32[768,8]{0,1:T(8,128)S(1)}, f32[768,8]{0,1:T(8,128)S(1)}, f32[768,8,128]{0,2,1:T(8,128)}, s32[4]{0:T(128)S(1)}, /*index=5*/s32[76...) while((s32[]{:T(128)}, f32[768,8]{0,1:T(8,128)S(1)}, ...), condition=%wide.region_9.10_spmd.clone, body=%wide.region_5.9_spmd.clone.sunk | while | flops 828144384 | bytes 57548480 | solution.py:113
  908.4 5.2 fusion.76
  930.9 5.3 bitcast_add_fusion.3
  939.5 5.2 bitcast_reduce_fusion.2
  949.3 5.3 bitcast_add_fusion.3
  963.1 5.2 fusion.76
  968.6 5.3 bitcast_add_fusion.3
  986.9 5.3 bitcast_add_fusion.3
  1005.3 5.3 bitcast_add_fusion.3
  1023.9 5.3 bitcast_add_fusion.3
  1042.3 5.3 bitcast_add_fusion.3
  1060.5 6.8 pad_maximum_fusion
  1067.3 23.4 %fusion.22 = (f32[768,8]{0,1:T(8,128)S(1)}, f32[8,2304,768]{2,1,0:T(8,128)}) fusion(pred[768,2304]{0,1:T(8,128)(4,1)S(1)} %copy-done.3, bf16[768,8,3,128]{0,3,2,1:T(8,128)(2,1)} %bitcast.101, bf16[2304,8,2,128]{3,0,1,2:T(8,128)(2,1)} %pad_maximum_fusion), kind=kOutput, calls=%fused_computation.34 | convolution fusion | flops 3666339840 | bytes 64708608 | tf_op jit(solution)/shard_map/thd,khd->thk/dot_general | solution.py:35
  1090.7 18.9 %fusion.23 = f32[768,8]{0,1:T(8,128)S(1)} fusion(f32[8,2304,768]{2,1,0:T(8,128)} %get-tuple-element.310, f32[768,8]{0,1:T(8,128)S(1)} %max.13, pred[768,2304]{0,1:T(8,128)(4,1)S(1)} %copy-done.4), kind=kLoop, calls=%fused_computation.35 | loop fusion | flops 70772736 | bytes 58441728 | tf_op jit(solution)/shard_map/reduce_sum | solution.py:42
  1109.7 26.4 %fusion.46 = bf16[768,8,128]{0,2,1:T(8,128)(2,1)} fusion(f32[768,8,128]{0,2,1:T(8,128)} %get-tuple-element.225, f32[8,2304,768]{2,1,0:T(8,128)} %get-tuple-element.310, f32[768,8]{0,1:T(8,128)S(1)} %max.13, pred[768,2304]{0,1:T(8,128)(4,1)S(1)} %copy-done.4, bf16[2304,8,2,128]{3,0,1,2:T(8,128)(2,1)} %pad_maximum_fusion, ...), kind=kOutput, calls=%fused_computation.63 | convolution fusion | flops 3697803264 | bytes 67903488 | tf_op jit(solution)/shard_map/thk,khd->thd/dot_general | solution.py:43
  1143.0 40.5 %all-gather.12.cloned.1.call-done = bf16[768,4096]{0,1:T(8,128)(2,1)} async-done(((bf16[768,1024]{0,1:T(8,128)(2,1)}), bf16[768,4096]{0,1:T(8,128)(2,1)}) %all-gather.12.cloned.1.call-update) | async-done | bytes 6291472 | tf_op jit(solution)/shard_map/all_gather | solution.py:128
  1183.5 16.0 %fusion.44 = bf16[768,1280]{1,0:T(8,128)(2,1)} fusion(f32[768,1280]{1,0:T(8,128)} %fusion.51, bf16[768,4096]{0,1:T(8,128)(2,1)} %all-gather.12.cloned.1.call-done, bf16[4096,1280]{1,0:T(8,128)(2,1)} %all-gather.14.cloned.1.call-done, bf16[768,1280]{1,0:T(8,128)(2,1)} %param.10), kind=kOutput, calls=%fused_computation.60 | convolution fusion | flops 8056995840 | bytes 24641536 | tf_op jit(solution)/shard_map/dot_general | solution.py:127
  (157 shorter events, 136.5 us)
Async XLA Ops:
  7.2 60.4 %all-gather.8.cloned.1.call-start = ((), (), s32[]{:S(2)}) async-start(), calls=%async_computation.1 | async-start | bytes 9830400 | tf_op jit(solution)/shard_map/all_gather | solution.py:55
  7.9 659.7 %all-gather.10.cloned.1.call-start = ((), (), s32[]{:S(2)}) async-start(), calls=%async_computation.2 | async-start | bytes 35389440 | tf_op jit(solution)/shard_map/all_gather | solution.py:83
  8.7 891.3 %all-gather.6.cloned.1.call-start = ((), (), s32[]{:S(2)}) async-start(), calls=%async_computation | async-start | bytes 9437184 | tf_op jit(solution)/shard_map/all_gather | solution.py:106
  9.4 1133.6 %all-gather.14.cloned.1.call-start = ((), (), s32[]{:S(2)}) async-start(), calls=%async_computation.4 | async-start | bytes 11796480 | tf_op jit(solution)/shard_map/all_gather | solution.py:126
  10.0 1173.6 %all-gather.12.cloned.1.call-start = ((), (), s32[]{:S(2)}) async-start(), calls=%async_computation.3 | async-start | bytes 7864320 | tf_op jit(solution)/shard_map/all_gather | solution.py:128
  11.1 29.2 %copy-start.7 = (s32[768]{0:T(1024)}, s32[768]{0:T(1024)S(1)}, u32[]{:S(2)}) copy-start(s32[768]{0:T(1024)S(1)} %broadcast_add_fusion.1) | copy-start | bytes 9220
  21.8 18.4 %copy-start.11 = (s32[24]{0:T(128)S(1)}, s32[24]{0:T(128)}, u32[]{:S(2)}) copy-start(s32[24]{0:T(128)} %param.15) | copy-start | bytes 292
  67.6 5.5 copy-start.2
  718.3 9.0 copy-start.1
  722.3 177.6 %copy-start.12 = (s32[4]{0:T(128)S(1)}, s32[4]{0:T(128)}, u32[]{:S(2)}) copy-start(s32[4]{0:T(128)} %param.17) | copy-start | bytes 52
  722.3 328.8 %collective-permute-start = (bf16[768,2048]{0,1:T(8,128)(2,1)}, bf16[768,2048]{0,1:T(8,128)(2,1)}, u32[]{:S(2)}, u32[]{:S(2)}) collective-permute-start(bf16[768,2048]{0,1:T(8,128)(2,1)} %bitcast.4), channel_id=1, source_target_pairs={{0,4},{4,8},{8,12},{12,16},{16,20},{20,24},{24,28},{1,5},{5,9},{9,... | collective-permute-start | bytes 9437192 | tf_op jit(solution)/shard_map/ppermute | solution.py:19
  726.0 329.8 %collective-permute-start.1 = (bf16[768,2048]{0,1:T(8,128)(2,1)}, bf16[768,2048]{0,1:T(8,128)(2,1)}, u32[]{:S(2)}, u32[]{:S(2)}) collective-permute-start(bf16[768,2048]{0,1:T(8,128)(2,1)} %bitcast.4), channel_id=1, source_target_pairs={{4,0},{8,4},{12,8},{16,12},{20,16},{24,20},{28,24},{5,1},{9,5},{13... | collective-permute-start | bytes 9437192 | tf_op jit(solution)/shard_map/ppermute | solution.py:22
  908.4 5.9 copy-start
  926.2 4.7 copy-start
  944.7 4.6 copy-start
  963.1 5.5 copy-start
  982.3 4.6 copy-start
  1000.7 4.6 copy-start
  1019.1 4.9 copy-start
  1037.7 4.6 copy-start
  1060.5 6.9 copy-start.3
  1067.3 23.4 %copy-start.4 = (pred[768,2304]{0,1:T(8,128)(4,1)S(1)}, pred[768,2304]{0,1:T(8,128)(4,1)}, u32[]{:S(2)}) copy-start(pred[768,2304]{0,1:T(8,128)(4,1)} %compare_and_fusion) | copy-start | bytes 5308420
  1109.6 26.5 %copy-start.8 = (s32[768]{0:T(1024)S(1)}, s32[768]{0:T(1024)}, u32[]{:S(2)}) copy-start(s32[768]{0:T(1024)} %copy-done.7) | copy-start | bytes 9220
  1136.1 5.3 copy-start.5
  (3 other events, 10.5 us)
Sparse Core Ops, SparseCore 0:
  9.6 58.0 all-gather.7
  69.2 598.3 all-gather.9
  669.7 230.1 all-gather.5
  902.0 151.4 all-gather.13
  1136.2 47.2 all-gather.11
where the time goes:
time: 1210 us
  waiting for transfers between devices  829 us (69%)
  matrix products  214 us (18%)
  other arithmetic  79.8 us (7%)
  local copies, waits for them, and re-layouts  48.2 us (4%)
  between operations  14 us (1%)
    all_gather x1, waiting for transfers between devices, shards(): lax.all_gather(w_qkv, 'row', axis=0, tiled=True)  592 us
    all_gather x1, waiting for transfers between devices, shards(): slot_block = lax.all_gather(prefix_cache, 'row', axis=0, tiled=True)  169 us
    dot_general x9, matrix products, attend(): jnp.einsum('thk,khd->thd', weights.astype(jnp.bfloat16), value_block, pre...  67.1 us
    dot_general x9, matrix products, attend(): jnp.einsum('thd,khd->thk', queries, key_block, preferred_element_type=jnp...  64.9 us
    reduce_sum x9, other arithmetic, attend(): denominator = denominator * rescale + jnp.sum(weights, axis=2)  55.8 us
    dot_general x1, matrix products, shards(): jnp.dot(modulated, lax.all_gather(w_qkv, 'row', axis=0, tiled=True), pref...  44.1 us
    all_gather x1, waiting for transfers between devices, shards(): lax.all_gather(attended, 'col', axis=1, tiled=True)  40.5 us
    all_gather x1, waiting for transfers between devices, shards(): lax.all_gather(hidden_in, 'col', axis=1, tiled=True)  24.6 us
  transfers between devices with their start and end apart: 7, of which 4 were waited for; matrix products, arithmetic and copies ran while one was open for 27% of the time, Pallas kernels for 0%

commit v1 on v0

v1 whole, which is shorter than its diff:
```python
import functools
import math

import jax
import jax.numpy as jnp
from jax import lax
from jax.experimental import pallas as pl
from jax.experimental.pallas import tpu as pltpu
from jax.sharding import PartitionSpec as P

HD = 128
MOST = 672
KT = 256
HALO = -(-MOST // KT) * KT
MASKED = -1e30
LOWEST = -1e28
ONES = 16
VMEM = 56 * 1024 * 1024


def request_of(positions, req_len):
    starts = jnp.cumsum(req_len) - req_len
    inside = (starts[None, :] <= positions[:, None]).astype(jnp.int32)
    return jnp.sum(inside, axis=1) - 1


def tile_rows(rows, most):
    return max(t for t in range(16, most + 1, 16) if rows % t == 0)


def qkv_kernel(planes, count, z_ref, at_ref, *refs):
    blocks, pieces = refs[:count], refs[count : count + 2 * planes - 1]
    out_ref, a_ref, w_ref, sems = refs[count + 2 * planes - 1 :]
    z = z_ref[0]
    depth = pieces[0].shape[0]
    n, m = blocks[0].shape
    t = pl.program_id(0)

    def each_weight(act):
        for i, piece in enumerate(pieces):
            at = z + i - (planes - 1)

            @pl.when(jnp.logical_and(at >= 0, at < planes))
            def _():
                to = w_ref.at[pl.ds(pl.multiple_of(at * depth, depth), depth), :]
                act(pltpu.make_async_copy(piece, to, sems.at[count + i]))

    def each_block(act, tile):
        for i, block in enumerate(blocks):
            row, column = at_ref[i, 0], at_ref[i, 1]

            @pl.when(row == tile)
            def _():
                to = a_ref.at[pl.ds(pl.multiple_of(row * n, n), n), pl.ds(pl.multiple_of(column * m, m), m)]
                act(pltpu.make_async_copy(block, to, sems.at[i]))

    @pl.when(t == 0)
    def _():
        each_weight(lambda copy: copy.start())
        for tile in range(a_ref.shape[0] // n):
            each_block(lambda copy: copy.start(), tile)
        each_weight(lambda copy: copy.wait())

    each_block(lambda copy: copy.wait(), t)
    a = a_ref[pl.ds(pl.multiple_of(t * n, n), n), :]
    out_ref[...] = jnp.dot(a, w_ref[...], preferred_element_type=jnp.float32).astype(out_ref.dtype)


def qkv_call(z, at, blocks, shape, pieces):
    rows, width = shape
    n, m = blocks[0].shape
    if n % 16 or m % HD:
        whole = jnp.zeros(shape, blocks[0].dtype)
        for i, block in enumerate(blocks):
            whole = lax.dynamic_update_slice(whole, block, (at[i, 0] * n, at[i, 1] * m))
        n, m = shape
        blocks, at = [whole], jnp.zeros((1, 2), jnp.int32)
    planes = (len(pieces) + 1) // 2
    columns = pieces[0].shape[1]
    return pl.pallas_call(
        functools.partial(qkv_kernel, planes, len(blocks)),
        out_shape=jax.ShapeDtypeStruct((rows, columns), jnp.bfloat16),
        grid_spec=pltpu.PrefetchScalarGridSpec(
            num_scalar_prefetch=2,
            grid=(rows // n,),
            in_specs=[pl.BlockSpec(memory_space=pl.ANY)] * (len(blocks) + len(pieces)),
            out_specs=pl.BlockSpec((n, columns), lambda i, *_: (i, 0)),
            scratch_shapes=[
                pltpu.VMEM((rows, width), jnp.bfloat16),
                pltpu.VMEM((width, columns), jnp.bfloat16),
                pltpu.SemaphoreType.DMA((len(blocks) + len(pieces),)),
            ],
        ),
        compiler_params=pltpu.CompilerParams(vmem_limit_bytes=VMEM),
        cost_estimate=pl.CostEstimate(
            flops=2 * rows * width * columns,
            bytes_accessed=2 * (rows * width + width * columns + rows * columns),
            transcendentals=0,
        ),
        name="qkv",
    )(z, at, *blocks, *pieces)


def attention_kernel(heads, groups, need_ref, q_ref, own_ref, low_ref, high_ref, prefix_ref, qtag_ref, ktag_ref,
                     out_ref, kv_ref, vt_ref, m_ref, acc_ref):
    t = pl.program_id(0)
    rows = own_ref.shape[0]
    tiles = ktag_ref.shape[0]
    first = groups * KT
    scale = math.log2(math.e) / math.sqrt(HD)

    @pl.when(t == 0)
    def _():
        for h in range(heads):
            there = slice(h * 2 * HD, (h + 1) * 2 * HD)
            kv_ref[h, first : first + HALO - MOST, :] = jnp.zeros((HALO - MOST, 2 * HD), jnp.bfloat16)
            for g in range(groups):
                kv_ref[h, g * KT : (g + 1) * KT, :] = prefix_ref[g, :, there]
            start = first + HALO
            kv_ref[h, start - MOST : start, :] = low_ref[:, there]
            kv_ref[h, start : start + rows, :] = own_ref[:, h * 3 * HD + HD : (h + 1) * 3 * HD]
            kv_ref[h, start + rows : start + rows + MOST, :] = high_ref[:, there]
            kv_ref[h, start + rows + MOST :, :] = jnp.zeros((HALO - MOST, 2 * HD), jnp.bfloat16)

        def turn(kt, _):
            at = pl.ds(pl.multiple_of(kt * KT, KT), KT)
            for h in range(heads):
                vt_ref[h, kt, :HD, :] = kv_ref[h, at, HD:].T
                vt_ref[h, kt, HD:, :] = jnp.ones((ONES, KT), jnp.bfloat16)
            return 0

        lax.fori_loop(0, tiles, turn, 0)

    m_ref[...] = jnp.full(m_ref.shape, LOWEST, jnp.float32)
    acc_ref[...] = jnp.zeros(acc_ref.shape, jnp.float32)

    def step(kt, _):
        @pl.when(need_ref[t, kt] > 0)
        def _():
            which = (kt >= groups).astype(jnp.int32)
            allowed = ktag_ref[kt] == qtag_ref[which]
            at = pl.ds(pl.multiple_of(kt * KT, KT), KT)
            for h in range(heads):
                q = q_ref[:, h * 3 * HD : h * 3 * HD + HD]
                k = kv_ref[h, at, :HD]
                s = lax.dot_general(k, q, (((1,), (1,)), ((), ())), preferred_element_type=jnp.float32)
                s = jnp.where(allowed, s, MASKED)
                old = m_ref[h]
                new = jnp.maximum(old, jnp.max(s, axis=0, keepdims=True))
                m_ref[h] = new
                p = jnp.exp2(s * scale - new * scale).astype(jnp.bfloat16)
                acc_ref[h] = acc_ref[h] * jnp.exp2((old - new) * scale) + jnp.dot(
                    vt_ref[h, kt], p, preferred_element_type=jnp.float32
                )

        return 0

    lax.fori_loop(0, tiles, step, 0)
    for h in range(heads):
        result = acc_ref[h, :HD] / acc_ref[h, HD : HD + 1]
        out_ref[:, h * HD : (h + 1) * HD] = result.T.astype(out_ref.dtype)


def attention_call(need, qkv, low, high, prefix, qtag, ktag):
    rows = qkv.shape[0]
    heads = qkv.shape[1] // (3 * HD)
    groups = prefix.shape[0]
    tile = rows // need.shape[0]
    tiles = ktag.shape[0]
    whole = lambda shape: pl.BlockSpec(shape, lambda t, *_: (0,) * len(shape))
    return pl.pallas_call(
        functools.partial(attention_kernel, heads, groups),
        out_shape=jax.ShapeDtypeStruct((rows, heads * HD), jnp.bfloat16),
        grid_spec=pltpu.PrefetchScalarGridSpec(
            num_scalar_prefetch=1,
            grid=(rows // tile,),
            in_specs=[
                pl.BlockSpec((tile, heads * 3 * HD), lambda t, *_: (t, 0)),
                whole(qkv.shape),
                whole(low.shape),
                whole(high.shape),
                whole(prefix.shape),
                pl.BlockSpec((2, 1, tile), lambda t, *_: (0, 0, t)),
                whole(ktag.shape),
            ],
            out_specs=pl.BlockSpec((tile, heads * HD), lambda t, *_: (t, 0)),
            scratch_shapes=[
                pltpu.VMEM((heads, tiles * KT, 2 * HD), jnp.bfloat16),
                pltpu.VMEM((heads, tiles, HD + ONES, KT), jnp.bfloat16),
                pltpu.VMEM((heads, 1, tile), jnp.float32),
                pltpu.VMEM((heads, HD + ONES, tile), jnp.float32),
            ],
        ),
        compiler_params=pltpu.CompilerParams(vmem_limit_bytes=VMEM),
        cost_estimate=pl.CostEstimate(
            flops=4 * rows * heads * HD * 8 * KT,
            bytes_accessed=2 * rows * heads * HD * 8,
            transcendentals=rows * heads * 8 * KT,
        ),
        name="attention",
    )(need, qkv, qkv, low, high, prefix, qtag, ktag)


def out_kernel(planes, parts, where_ref, at_ref, hidden_ref, gate_ref, *refs):
    count = 2 * (2 * planes - 1)
    pieces, columns = refs[:count], refs[count : count + parts]
    out_ref, w_ref, a_ref, sems = refs[count + parts :]
    z, x = where_ref[0], where_ref[1]
    depth = pieces[0].shape[0]
    tile = hidden_ref.shape[0]
    t = pl.program_id(0)

    @pl.when(t == 0)
    def _():
        def each(act):
            for i, piece in enumerate(columns):
                m = piece.shape[1]
                to = a_ref.at[:, pl.ds(pl.multiple_of(at_ref[i] * m, m), m)]
                act(pltpu.make_async_copy(piece, to, sems.at[count + i]))
            for i, piece in enumerate(pieces):
                plane = z + i // 2 - (planes - 1)
                at = 2 * plane + (x if i % 2 == 0 else 1 - x)

                @pl.when(jnp.logical_and(plane >= 0, plane < planes))
                def _():
                    to = w_ref.at[pl.ds(pl.multiple_of(at * depth, depth), depth), :]
                    act(pltpu.make_async_copy(piece, to, sems.at[i]))

        each(lambda copy: copy.start())
        each(lambda copy: copy.wait())

    a = a_ref[pl.ds(pl.multiple_of(t * tile, tile), tile), :]
    projected = jnp.dot(a, w_ref[...], preferred_element_type=jnp.float32)
    out_ref[...] = (
        hidden_ref[...].astype(jnp.float32) + gate_ref[...].astype(jnp.float32) * projected
    ).astype(out_ref.dtype)


def out_call(where, at, columns, hidden, gate, pieces):
    rows, width = hidden.shape
    depth = sum(piece.shape[1] for piece in columns)
    planes = (len(pieces) // 2 + 1) // 2
    tile = tile_rows(rows, 256)
    block = pl.BlockSpec((tile, width), lambda i, *_: (i, 0))
    return pl.pallas_call(
        functools.partial(out_kernel, planes, len(columns)),
        out_shape=jax.ShapeDtypeStruct((rows, width), jnp.bfloat16),
        grid_spec=pltpu.PrefetchScalarGridSpec(
            num_scalar_prefetch=2,
            grid=(rows // tile,),
            in_specs=[block, block] + [pl.BlockSpec(memory_space=pl.ANY)] * (len(pieces) + len(columns)),
            out_specs=block,
            scratch_shapes=[
                pltpu.VMEM((depth, width), jnp.bfloat16),
                pltpu.VMEM((rows, depth), jnp.bfloat16),
                pltpu.SemaphoreType.DMA((len(pieces) + len(columns),)),
            ],
        ),
        compiler_params=pltpu.CompilerParams(vmem_limit_bytes=VMEM),
        cost_estimate=pl.CostEstimate(
            flops=2 * rows * width * depth,
            bytes_accessed=2 * (rows * depth + width * depth + 3 * rows * width),
            transcendentals=0,
        ),
        name="project",
    )(where, at, hidden, gate, *pieces, *columns)


def shards(rows_n, cols_n, hidden_in, modulation, w_qkv, w_out, prefix_cache, req_group, req_len, owner):
    planes = rows_n // 2
    tokens, width = hidden_in.shape
    local_heads = w_qkv.shape[1] // (3 * HD)
    heads = local_heads // 2
    parts = 2 if heads % 2 == 0 else 1
    hc = heads // parts
    groups = owner.shape[0]
    requests = req_len.shape[0]
    r, c = lax.axis_index("row"), lax.axis_index("col")
    z, x = r // 2, r % 2
    total = rows_n * tokens

    def swap_x(v, valid=lambda plane: True):
        return lax.ppermute(v, "row", [(i, i ^ 1) for i in range(rows_n) if valid(i // 2)])

    def swap_col(v, bit):
        return lax.ppermute(v, "col", [(i, i ^ bit) for i in range(cols_n)])

    def z_move(v, by, sources):
        pairs = [(2 * p + i, 2 * (p + by) + i) for p in sources for i in range(2)]
        return lax.ppermute(v, "row", pairs)

    under_way = []

    def line_step(v, w, step):
        if len(under_way) >= 2:
            v, w, _, _ = lax.optimization_barrier((v, w) + under_way[-2])
        right = z_move(v, 1, range(step - 1, planes - 1))
        left = z_move(w, -1, range(1, planes - step + 1))
        under_way.append((right, left))
        return right, left

    def line_gather(own):
        lows, highs = [], []
        low = high = own
        for step in range(1, planes):
            low, high = line_step(low, high, step)
            lows.append(low)
            highs.append(high)
        return lows[::-1] + [own] + highs

    def by_x(mine, other, axis):
        return jnp.where(
            x == 0,
            jnp.concatenate([mine, other], axis),
            jnp.concatenate([other, mine], axis),
        )

    def columns_of(v, start, size):
        return lax.dynamic_slice_in_dim(v, start, size, v.ndim - 1)

    def plane_weights(part):
        size = hc * 3 * HD
        mine = columns_of(w_qkv, x * heads * 3 * HD + part * size, size)
        other = columns_of(w_qkv, (1 - x) * heads * 3 * HD + part * size, size)
        return by_x(mine, swap_x(other), 0)

    weights = [plane_weights(part) for part in range(parts)]

    kv_width = heads * 2 * HD
    slot = prefix_cache[0]
    mine = columns_of(slot, x * kv_width, kv_width)
    other = columns_of(slot, (1 - x) * kv_width, kv_width)
    here = by_x(mine[None], swap_x(other)[None], 0)
    owner_plane = owner // 2

    def beyond(plane, side):
        inside = (owner_plane - plane) * side > 0
        return inside, jnp.cumsum(inside.astype(jnp.int32)) - 1

    def outgoing(side, held):
        wanted, order = beyond(z - side, side)
        _, held_order = beyond(z, side)
        source = jnp.where(owner_plane == z, owner % 2, 2 + held_order)
        pool = jnp.concatenate([here, held], 0)
        picked = []
        for j in range(groups - 1):
            at = jnp.sum(jnp.where(wanted & (order == j), source, 0))
            picked.append(lax.dynamic_slice_in_dim(pool, at, 1, 0))
        return jnp.concatenate(picked, 0)

    held_low = held_high = jnp.zeros((groups - 1,) + here.shape[1:], here.dtype)
    for step in range(planes - 1):
        came = z_move(outgoing(-1, held_low), 1, [step])
        held_low = jnp.where(z == step + 1, came, held_low)
        came = z_move(outgoing(1, held_high), -1, [planes - 1 - step])
        held_high = jnp.where(z == planes - 2 - step, came, held_high)
    pool = jnp.concatenate([here, held_low, held_high], 0)
    low_order, high_order = beyond(z, -1)[1], beyond(z, 1)[1]
    source = jnp.where(
        owner_plane == z,
        owner % 2,
        jnp.where(owner_plane < z, 2 + low_order, 2 + groups - 1 + high_order),
    )
    prefix = jnp.concatenate(
        [lax.dynamic_slice_in_dim(pool, source[g], 1, 0) for g in range(groups)], 0
    )

    positions = r * tokens + jnp.arange(tokens, dtype=jnp.int32)
    request_id = request_of(positions, req_len)
    onehot = (request_id[:, None] == jnp.arange(requests, dtype=jnp.int32)[None, :]).astype(jnp.bfloat16)
    shift, scale, gate = [
        jnp.dot(onehot, modulation[:, i, :], preferred_element_type=jnp.float32) for i in range(3)
    ]
    hidden_f = hidden_in.astype(jnp.float32)
    local_mean = jnp.mean(hidden_f, axis=1, keepdims=True)
    local_square = jnp.sum((hidden_f - local_mean) ** 2, axis=1, keepdims=True)
    stats = lax.all_gather(jnp.concatenate([local_mean, local_square], 1).T, "col", axis=0, tiled=False)
    mean = jnp.mean(stats[:, 0], axis=0)
    square = jnp.sum(stats[:, 1], axis=0) + width * jnp.sum((stats[:, 0] - mean[None]) ** 2, axis=0)
    variance = square / (width * cols_n)
    modulated = (
        (hidden_f - mean[:, None]) * lax.rsqrt(variance[:, None] + 1e-06) * (1.0 + scale) + shift
    ).astype(jnp.bfloat16)

    half = tokens // 2
    col_bits = [1 << b for b in reversed(range(cols_n.bit_length() - 1))]
    full_pieces, full_at = [], []
    for i in range(2):
        pieces = [(modulated[i * half : (i + 1) * half], 0, 0)]
        order = [0] + col_bits if i == 0 else col_bits[:-1] + [0] + col_bits[-1:]
        for bit in order:
            if bit == 0:
                pieces += [(swap_x(v), 1, cb) for v, _, cb in pieces]
            else:
                pieces += [(swap_col(v, bit), xb, cb ^ bit) for v, xb, cb in pieces]
        for v, xb, cb in pieces:
            full_pieces.append(v)
            full_at.append(jnp.stack([(x ^ xb) * 2 + i, c ^ cb]))
    full_at = jnp.stack(full_at)

    rows = 2 * tokens
    key_pos = z * rows - HALO + jnp.arange(rows + 2 * HALO, dtype=jnp.int32)
    key_req = request_of(key_pos, req_len)
    key_req = jnp.where(key_pos < 0, -1, jnp.where(key_pos >= total, -2, key_req))
    plane_req = key_req[HALO : HALO + rows]
    plane_group = jnp.sum(
        jnp.where(plane_req[:, None] == jnp.arange(requests, dtype=jnp.int32)[None, :], req_group[None, :], 0), axis=1
    )
    group_tag = jnp.repeat(jnp.arange(groups, dtype=jnp.int32), KT)
    ktag = jnp.concatenate([group_tag, key_req]).reshape(-1, KT, 1)
    qtag = jnp.stack([plane_group, plane_req])[:, None, :]
    tile = tile_rows(rows, 256)
    tile_group = plane_group.reshape(-1, tile)
    tile_req = plane_req.reshape(-1, tile)
    need_group = jnp.any(tile_group[:, None, :] == jnp.arange(groups, dtype=jnp.int32)[None, :, None], axis=2)
    key_tiles = key_req.reshape(-1, KT)
    lowest = jnp.min(jnp.where(key_tiles < 0, requests, key_tiles), axis=1)
    highest = jnp.max(key_tiles, axis=1)
    need_near = (lowest[None, :] <= tile_req[:, -1:]) & (highest[None, :] >= tile_req[:, :1])
    need = jnp.concatenate([need_group, need_near], axis=1).astype(jnp.int32)

    keys = jnp.zeros((tokens, local_heads * HD), jnp.bfloat16)
    values = keys
    attended, attended_at = [], []
    for part in range(parts):
        qkv = qkv_call(z[None], full_at, full_pieces, (rows, width * cols_n), line_gather(weights[part]))

        def kv_of(start, size):
            kv = lax.dynamic_slice_in_dim(qkv, start, size, 0)
            return jnp.concatenate([kv[:, (3 * j + 1) * HD : (3 * j + 3) * HD] for j in range(hc)], 1)

        low = z_move(kv_of(rows - MOST, MOST), 1, range(planes - 1))
        high = z_move(kv_of(0, MOST), -1, range(1, planes))
        own_kv = kv_of(x * tokens, tokens)
        other_kv = swap_x(kv_of((1 - x) * tokens, tokens))
        for xb, v in ((0, own_kv), (1, other_kv)):
            at = ((x ^ xb) * heads + part * hc) * HD
            k = jnp.concatenate([v[:, 2 * j * HD : (2 * j + 1) * HD] for j in range(hc)], 1)
            v = jnp.concatenate([v[:, (2 * j + 1) * HD : (2 * j + 2) * HD] for j in range(hc)], 1)
            keys = lax.dynamic_update_slice(keys, k, (0, at))
            values = lax.dynamic_update_slice(values, v, (0, at))
        part_prefix = prefix[:, :, part * hc * 2 * HD : (part + 1) * hc * 2 * HD]
        out = attention_call(need, qkv, low, high, part_prefix, qtag, ktag)
        pieces = [(lax.dynamic_slice_in_dim(out, x * tokens, tokens, 0), 0, 0)]
        pieces.append((swap_x(lax.dynamic_slice_in_dim(out, (1 - x) * tokens, tokens, 0)), 1, 0))
        for bit in col_bits:
            pieces += [(swap_col(v, bit), xb, cb ^ bit) for v, xb, cb in pieces]
        for v, xb, cb in pieces:
            attended.append(v)
            attended_at.append(((c ^ cb) * 2 + (x ^ xb)) * parts + part)

    out_pieces = []
    for i, piece in enumerate(line_gather(w_out)):
        off = i - (planes - 1)
        out_pieces += [piece, swap_x(piece, lambda p: 0 <= p + off < planes)]
    hidden_out = out_call(
        jnp.stack([z, x]), jnp.stack(attended_at), attended, hidden_in, gate.astype(jnp.bfloat16), out_pieces
    )
    return hidden_out, keys, values


def solution(mesh):
    return jax.shard_map(
        functools.partial(shards, mesh.shape["row"], mesh.shape["col"]),
        mesh=mesh,
        in_specs=(
            P("row", "col"),
            P(None, None, "col"),
            P("row", "col"),
            P("row", "col"),
            P("row", None, "col"),
            P(),
            P(),
            P(),
        ),
        out_specs=(P("row", "col"), P("row", "col"), P("row", "col")),
        check_vma=False,
    )
```

time: 1210 us -> 656 us (0.54)
  waiting for transfers between devices: 829 us -> 334 us
  matrix products: 214 us -> 4.49 us
  Pallas kernels: 0 us -> 116 us
  starting transfers between devices: 5.17 us -> 115 us
  other arithmetic: 79.8 us -> 31.9 us
  local copies, waits for them, and re-layouts: 48.2 us -> 26.7 us
    all_gather x5 -> x0, waiting for transfers between devices: 826 us -> none  [the longest x1 592 us: shards(): lax.all_gather(w_qkv, 'row', axis=0, tiled=True)]
    ppermute x2 -> x68, waiting for transfers between devices: 0.01 us -> 334 us  [the longest x28 206 us: z_move(): return lax.ppermute(v, 'row', pairs)]
    dot_general x22 -> x3, matrix products: 214 us -> 4.49 us  [shards(): jnp.dot(onehot, modulation[:, i, :], preferred_element_type=jnp.float32)]
    pallas_call x0 -> x5, Pallas kernels: none -> 116 us  [the longest x2 60 us: attention_call(): pl.pallas_call(functools.partial(attention_kernel, heads, groups), out_sh...]
    ppermute x2 -> x68, starting transfers between devices: 4.98 us -> 115 us  [the longest x28 80.1 us: z_move(): return lax.ppermute(v, 'row', pairs)]
    reduce_sum x21 -> x6, other arithmetic: 68.9 us -> 1.88 us  [the longest x1 0.76 us: outgoing(): at = jnp.sum(jnp.where(wanted & (order == j), source, 0))]
  transfers between devices with their start and end apart: 7 -> 68, of which waited for: 4 -> 22; matrix products, arithmetic and copies ran while one was open for 27% -> 9% of each run, Pallas kernels for 0% -> 15%
where the time goes in v1:
time: 656 us; the launch traced here: 654 us
  waiting for transfers between devices  334 us (51%)
  Pallas kernels  116 us (18%)
  starting transfers between devices  115 us (18%)
  other arithmetic  31.9 us (5%)
  local copies, waits for them, and re-layouts  26.7 us (4%)
  between operations  20.4 us (3%)
    ppermute x28, waiting for transfers between devices, z_move(): return lax.ppermute(v, 'row', pairs)  206 us
    ppermute x17, waiting for transfers between devices, swap_x(): lax.ppermute(v, 'row', [(i, i ^ 1) for i in range(rows_n) if valid(i // 2)])  106 us
    ppermute x28, starting transfers between devices, z_move(): return lax.ppermute(v, 'row', pairs)  80.1 us
    pallas_call x2, Pallas kernels, attention_call(): pl.pallas_call(functools.partial(attention_kernel, heads, groups), out_sh...  60 us
    pallas_call x2, Pallas kernels, qkv_call(): pl.pallas_call(functools.partial(qkv_kernel, planes, len(blocks)), out_sh...  38.6 us
    ppermute x17, starting transfers between devices, swap_x(): lax.ppermute(v, 'row', [(i, i ^ 1) for i in range(rows_n) if valid(i // 2)])  22.4 us
    ppermute x23, waiting for transfers between devices, swap_col(): return lax.ppermute(v, 'col', [(i, i ^ bit) for i in range(cols_n)])  21.7 us
    pallas_call x1, Pallas kernels, out_call(): pl.pallas_call(functools.partial(out_kernel, planes, len(columns)), out_s...  17.8 us
  transfers between devices with their start and end apart: 68, of which 22 were waited for; matrix products, arithmetic and copies ran while one was open for 9% of the time, Pallas kernels for 15%

profile of v1, /device:TPU:0, one launch (start us, length us, event | category | flops | bytes accessed | tf_op | source)
XLA Modules:
  0.0 653.8 jit_solution(4688532107845595920)
XLA Ops:
  15.0 5.3 all-gather.1
  22.7 18.3 %collective-permute-done.43 = bf16[256,1024]{1,0:T(8,128)(2,1)S(1)} collective-permute-done((bf16[256,1024]{1,0:T(8,128)(2,1)}, bf16[256,1024]{1,0:T(8,128)(2,1)S(1)}, u32[]{:S(2)}, u32[]{:S(2)}) %collective-permute-start.43) | collective-permute-done | bytes 524320 | tf_op jit(solution)/shard_map/ppermute | solution.py:283
  68.9 15.0 %collective-permute-done.44 = bf16[3,256,1024]{2,1,0:T(8,128)(2,1)} collective-permute-done((bf16[3,256,1024]{2,1,0:T(8,128)(2,1)}, bf16[3,256,1024]{2,1,0:T(8,128)(2,1)}, u32[]{:S(2)}, u32[]{:S(2)}) %collective-permute-start.44) | collective-permute-done | bytes 1572896 | tf_op jit(solution)/shard_map/ppermute | solution.py:290
  90.7 14.5 %collective-permute-done.34.refs_9_ = bf16[384,1280]{1,0:T(8,128)(2,1)} collective-permute-done((bf16[384,1280]{1,0:T(8,128)(2,1)}, bf16[384,1280]{1,0:T(8,128)(2,1)}, u32[]{:S(2)}, u32[]{:S(2)}) %collective-permute-start.34) | collective-permute-done | bytes 983072 | tf_op jit(solution)/shard_map/ppermute | solution.py:286
  106.6 17.3 %collective-permute-done.2.refs_18_ = bf16[1280,768]{1,0:T(8,128)(2,1)} collective-permute-done((bf16[1280,768]{1,0:T(8,128)(2,1)}, bf16[1280,768]{1,0:T(8,128)(2,1)}, u32[]{:S(2)}, u32[]{:S(2)}) %collective-permute-start.2) | collective-permute-done | bytes 1966112 | tf_op jit(solution)/shard_map/ppermute | solution.py:290
  139.2 12.9 %collective-permute-done = bf16[640,768]{1,0:T(8,128)(2,1)} collective-permute-done((bf16[640,768]{1,0:T(8,128)(2,1)}, bf16[640,768]{1,0:T(8,128)(2,1)}, u32[]{:S(2)}, u32[]{:S(2)}) %collective-permute-start) | collective-permute-done | bytes 983072 | tf_op jit(solution)/shard_map/ppermute | solution.py:283
  153.5 18.6 %collective-permute-done.5.refs_21_ = bf16[1280,768]{1,0:T(8,128)(2,1)} collective-permute-done((bf16[1280,768]{1,0:T(8,128)(2,1)}, bf16[1280,768]{1,0:T(8,128)(2,1)}, u32[]{:S(2)}, u32[]{:S(2)}) %collective-permute-start.5) | collective-permute-done | bytes 1966112 | tf_op jit(solution)/shard_map/ppermute | solution.py:290
  186.2 18.6 %collective-permute-start.6 = (bf16[1280,768]{1,0:T(8,128)(2,1)}, bf16[1280,768]{1,0:T(8,128)(2,1)}, u32[]{:S(2)}, u32[]{:S(2)}) collective-permute-start(bf16[1280,768]{1,0:T(8,128)(2,1)} %maximum_select_fusion.refs_19_), channel_id=1, source_target_pairs={{0,8},{4,12},{8,16},{12,20},{16,24},{20,28},{1,9},{5,13},{9,17},{1... | collective-permute-start | bytes 5898248 | tf_op jit(solution)/shard_map/ppermute | solution.py:290
  218.2 97.9 %collective-permute-done.49 = bf16[3,256,1024]{2,1,0:T(8,128)(2,1)} collective-permute-done((bf16[3,256,1024]{2,1,0:T(8,128)(2,1)}, bf16[3,256,1024]{2,1,0:T(8,128)(2,1)}, u32[]{:S(2)}, u32[]{:S(2)}) %collective-permute-start.49) | collective-permute-done | bytes 1572896 | tf_op jit(solution)/shard_map/ppermute | solution.py:290
  324.6 19.3 %qkv.2.q_ref.own_ref = bf16[1536,768]{1,0:T(8,128)(2,1)} custom-call(s32[1]{0:T(128)} %bitcast.z_ref, s32[16,2]{1,0:T(8,128)} %stack.276.at_ref, bf16[384,1280]{1,0:T(8,128)(2,1)} %get-tuple-element.94.refs_0_, bf16[384,1280]{1,0:T(8,128)(2,1)} %collective-permute-done.27.refs_1_, bf16[384,1280]{1,0:T(8,128)(2,1)} %collective-permute-done.28.refs_2_, ...), custom_call_target="tpu_custom_call" | custom-call | flops 12079595520 | bytes 25952256 | tf_op jit(solution)/shard_map/qkv/pallas_call | solution.py:80
  354.2 16.7 %collective-permute-done.11.refs_21_ = bf16[1280,768]{1,0:T(8,128)(2,1)} collective-permute-done((bf16[1280,768]{1,0:T(8,128)(2,1)}, bf16[1280,768]{1,0:T(8,128)(2,1)}, u32[]{:S(2)}, u32[]{:S(2)}) %collective-permute-start.11) | collective-permute-done | bytes 1966112 | tf_op jit(solution)/shard_map/ppermute | solution.py:290
  374.1 6.9 %collective-permute-start.12 = (bf16[512,1280]{1,0:T(8,128)(2,1)}, bf16[512,1280]{1,0:T(8,128)(2,1)}, u32[]{:S(2)}, u32[]{:S(2)}) collective-permute-start(bf16[512,1280]{1,0:T(8,128)(2,1)} %refs_6_.1), channel_id=1, source_target_pairs={{0,8},{4,12},{8,16},{12,20},{16,24},{20,28},{1,9},{5,13},{9,17},{1... | collective-permute-start | bytes 3932168 | tf_op jit(solution)/shard_map/ppermute | solution.py:290
  386.6 30.0 %attention.2 = bf16[1536,256]{1,0:T(8,128)(2,1)} custom-call(s32[6,16]{1,0:T(8,128)} %add_convert_fusion.need_ref, bf16[1536,768]{1,0:T(8,128)(2,1)} %qkv.2.q_ref.own_ref, bf16[1536,768]{1,0:T(8,128)(2,1)} %qkv.2.q_ref.own_ref, bf16[672,512]{1,0:T(8,128)(2,1)} %copy-done.37, bf16[672,512]{1,0:T(8,128)(2,1)} %copy-done.35, ...), custom_call_target="tpu_custom_call" | custom-call | flops 3221225472 | bytes 6291456 | tf_op jit(solution)/shard_map/attention/pallas_call | solution.py:171
  419.7 8.5 %collective-permute-done.50.refs_15_ = bf16[768,256]{1,0:T(8,128)(2,1)} collective-permute-done((bf16[768,256]{1,0:T(8,128)(2,1)S(1)}, bf16[768,256]{1,0:T(8,128)(2,1)}, u32[]{:S(2)}, u32[]{:S(2)}) %collective-permute-start.50) | collective-permute-done | bytes 393248 | tf_op jit(solution)/shard_map/ppermute | solution.py:283
  430.4 25.0 %collective-permute-done.13.refs_8_ = bf16[512,1280]{1,0:T(8,128)(2,1)} collective-permute-done((bf16[512,1280]{1,0:T(8,128)(2,1)}, bf16[512,1280]{1,0:T(8,128)(2,1)}, u32[]{:S(2)}, u32[]{:S(2)}) %collective-permute-start.13) | collective-permute-done | bytes 1310752 | tf_op jit(solution)/shard_map/ppermute | solution.py:290
  462.0 12.3 %collective-permute-done.66 = bf16[768,512]{1,0:T(8,128)(2,1)S(1)} collective-permute-done((bf16[768,512]{1,0:T(8,128)(2,1)S(1)}, bf16[768,512]{1,0:T(8,128)(2,1)S(1)}, u32[]{:S(2)}, u32[]{:S(2)}) %collective-permute-start.66) | collective-permute-done | bytes 786464 | tf_op jit(solution)/shard_map/ppermute | solution.py:283
  475.7 19.3 %qkv.3.q_ref.own_ref = bf16[1536,768]{1,0:T(8,128)(2,1)} custom-call(s32[1]{0:T(128)} %bitcast.z_ref, s32[16,2]{1,0:T(8,128)} %stack.276.at_ref, bf16[384,1280]{1,0:T(8,128)(2,1)} %get-tuple-element.94.refs_0_, bf16[384,1280]{1,0:T(8,128)(2,1)} %collective-permute-done.27.refs_1_, bf16[384,1280]{1,0:T(8,128)(2,1)} %collective-permute-done.28.refs_2_, ...), custom_call_target="tpu_custom_call" | custom-call | flops 12079595520 | bytes 25952256 | tf_op jit(solution)/shard_map/qkv/pallas_call | solution.py:80
  501.8 9.0 %collective-permute-start.57 = (bf16[672,512]{1,0:T(8,128)(2,1)S(1)}, bf16[672,512]{1,0:T(8,128)(2,1)S(1)}, u32[]{:S(2)}, u32[]{:S(2)}) collective-permute-start(bf16[672,512]{1,0:T(8,128)(2,1)S(1)} %pad_maximum_fusion.12), channel_id=1, source_target_pairs={{0,8},{4,12},{8,16},{12,20},{16,24},{20,28},{1,9},{5,13},{9,17},{1... | collective-permute-start | bytes 2064392 | tf_op jit(solution)/shard_map/ppermute | solution.py:290
  513.1 10.8 %collective-permute-done.58.high_ref = bf16[672,512]{1,0:T(8,128)(2,1)S(1)} collective-permute-done((bf16[672,512]{1,0:T(8,128)(2,1)S(1)}, bf16[672,512]{1,0:T(8,128)(2,1)S(1)}, u32[]{:S(2)}, u32[]{:S(2)}) %collective-permute-start.58) | collective-permute-done | bytes 688160 | tf_op jit(solution)/shard_map/ppermute | solution.py:290
  527.0 29.9 %attention.3 = bf16[1536,256]{1,0:T(8,128)(2,1)} custom-call(s32[6,16]{1,0:T(8,128)} %add_convert_fusion.need_ref, bf16[1536,768]{1,0:T(8,128)(2,1)} %qkv.3.q_ref.own_ref, bf16[1536,768]{1,0:T(8,128)(2,1)} %qkv.3.q_ref.own_ref, bf16[672,512]{1,0:T(8,128)(2,1)} %copy-done.38, bf16[672,512]{1,0:T(8,128)(2,1)} %copy-done.36, ...), custom_call_target="tpu_custom_call" | custom-call | flops 3221225472 | bytes 6291456 | tf_op jit(solution)/shard_map/attention/pallas_call | solution.py:171
  572.7 5.1 collective-permute-done.61.refs_25_
  588.6 23.0 %collective-permute-done.24.refs_11_ = bf16[512,1280]{1,0:T(8,128)(2,1)S(1)} collective-permute-done((bf16[512,1280]{1,0:T(8,128)(2,1)}, bf16[512,1280]{1,0:T(8,128)(2,1)S(1)}, u32[]{:S(2)}, u32[]{:S(2)}) %collective-permute-start.24) | collective-permute-done | bytes 1310752 | tf_op jit(solution)/shard_map/ppermute | solution.py:283
  611.6 24.3 %collective-permute-done.26.refs_13_ = bf16[512,1280]{1,0:T(8,128)(2,1)} collective-permute-done((bf16[512,1280]{1,0:T(8,128)(2,1)}, bf16[512,1280]{1,0:T(8,128)(2,1)}, u32[]{:S(2)}, u32[]{:S(2)}) %collective-permute-start.26) | collective-permute-done | bytes 1310752 | tf_op jit(solution)/shard_map/ppermute | solution.py:283
  635.9 17.8 %project.1 = bf16[768,1280]{1,0:T(8,128)(2,1)} custom-call(s32[2]{0:T(128)} %pad_add_fusion.2.where_ref, s32[16]{0:T(128)} %stack.235.at_ref, bf16[768,1280]{1,0:T(8,128)(2,1)} %hidden_ref.1, bf16[768,1280]{1,0:T(8,128)(2,1)} %convolution_convert_fusion.gate_ref, bf16[512,1280]{1,0:T(8,128)(2,1)} %collective-permute-done.18.refs_0_, ...), custom_call_target="tpu_custom_call" | custom-call | flops 8053063680 | bytes 22675456 | tf_op jit(solution)/shard_map/project/pallas_call | solution.py:245
  (309 shorter events, 157.3 us)
Async XLA Ops:
  4.9 49.5 %collective-permute-start.1 = (bf16[640,768]{1,0:T(8,128)(2,1)}, bf16[640,768]{1,0:T(8,128)(2,1)}, u32[]{:S(2)}, u32[]{:S(2)}) collective-permute-start(bf16[640,768]{1,0:T(8,128)(2,1)} %get-tuple-element.58), channel_id=1, source_target_pairs={{0,4},{4,0},{8,12},{12,8},{16,20},{20,16},{24,28},{28,24},{1,5},{5... | collective-permute-start | bytes 2949128 | tf_op jit(solution)/shard_map/ppermute | solution.py:283
  57.8 66.1 %collective-permute-start.2 = (bf16[1280,768]{1,0:T(8,128)(2,1)}, bf16[1280,768]{1,0:T(8,128)(2,1)}, u32[]{:S(2)}, u32[]{:S(2)}) collective-permute-start(bf16[1280,768]{1,0:T(8,128)(2,1)} %maximum_select_fusion.1.refs_19_), channel_id=1, source_target_pairs={{0,8},{4,12},{8,16},{12,20},{16,24},{20,28},{1,9},{5,13},{9,17},{1... | collective-permute-start | bytes 5898248 | tf_op jit(solution)/shard_map/ppermute | solution.py:290
  60.4 65.4 %collective-permute-start.4 = (bf16[1280,768]{1,0:T(8,128)(2,1)}, bf16[1280,768]{1,0:T(8,128)(2,1)}, u32[]{:S(2)}, u32[]{:S(2)}) collective-permute-start(bf16[1280,768]{1,0:T(8,128)(2,1)} %maximum_select_fusion.1.refs_19_), channel_id=1, source_target_pairs={{8,0},{12,4},{16,8},{20,12},{24,16},{28,20},{9,1},{13,5},{17,9},{2... | collective-permute-start | bytes 5898248 | tf_op jit(solution)/shard_map/ppermute | solution.py:290
  61.7 44.3 %collective-permute-start.28 = (bf16[384,1280]{1,0:T(8,128)(2,1)}, bf16[384,1280]{1,0:T(8,128)(2,1)}, u32[]{:S(2)}, u32[]{:S(2)}) collective-permute-start(bf16[384,1280]{1,0:T(8,128)(2,1)} %get-tuple-element.94.refs_0_), channel_id=1, source_target_pairs={{0,2},{1,3},{2,0},{3,1},{4,6},{5,7},{6,4},{7,5},{8,10},{9,11},{10,... | collective-permute-start | bytes 2949128 | tf_op jit(solution)/shard_map/ppermute | solution.py:286
  125.8 46.3 %collective-permute-start.5 = (bf16[1280,768]{1,0:T(8,128)(2,1)}, bf16[1280,768]{1,0:T(8,128)(2,1)}, u32[]{:S(2)}, u32[]{:S(2)}) collective-permute-start(bf16[1280,768]{1,0:T(8,128)(2,1)} %collective-permute-done.4.refs_20_), channel_id=1, source_target_pairs={{8,0},{12,4},{16,8},{20,12},{9,1},{13,5},{17,9},{21,13},{10,2},{14... | collective-permute-start | bytes 5898248 | tf_op jit(solution)/shard_map/ppermute | solution.py:290
  133.2 71.6 %collective-permute-start.48 = (bf16[3,256,1024]{2,1,0:T(8,128)(2,1)}, bf16[3,256,1024]{2,1,0:T(8,128)(2,1)}, u32[]{:S(2)}, u32[]{:S(2)}) collective-permute-start(bf16[3,256,1024]{2,1,0:T(8,128)(2,1)} %pad_maximum_fusion.6), channel_id=1, source_target_pairs={{16,8},{20,12},{17,9},{21,13},{18,10},{22,14},{19,11},{23,15}} | collective-permute-start | bytes 4718600 | tf_op jit(solution)/shard_map/ppermute | solution.py:290
  137.7 45.3 %collective-permute-start.29 = (bf16[384,1280]{1,0:T(8,128)(2,1)}, bf16[384,1280]{1,0:T(8,128)(2,1)}, u32[]{:S(2)}, u32[]{:S(2)}) collective-permute-start(bf16[384,1280]{1,0:T(8,128)(2,1)} %collective-permute-done.27.refs_1_), channel_id=1, source_target_pairs={{0,2},{1,3},{2,0},{3,1},{4,6},{5,7},{6,4},{7,5},{8,10},{9,11},{10,... | collective-permute-start | bytes 2949128 | tf_op jit(solution)/shard_map/ppermute | solution.py:286
  183.0 133.1 %collective-permute-start.8 = (bf16[1280,768]{1,0:T(8,128)(2,1)}, bf16[1280,768]{1,0:T(8,128)(2,1)}, u32[]{:S(2)}, u32[]{:S(2)}) collective-permute-start(bf16[1280,768]{1,0:T(8,128)(2,1)} %collective-permute-done.3.refs_17_), channel_id=1, source_target_pairs={{16,24},{20,28},{17,25},{21,29},{18,26},{22,30},{19,27},{23,31}} | collective-permute-start | bytes 5898248 | tf_op jit(solution)/shard_map/ppermute | solution.py:290
  184.9 131.7 %collective-permute-start.9 = (bf16[1280,768]{1,0:T(8,128)(2,1)}, bf16[1280,768]{1,0:T(8,128)(2,1)}, u32[]{:S(2)}, u32[]{:S(2)}) collective-permute-start(bf16[1280,768]{1,0:T(8,128)(2,1)} %collective-permute-done.5.refs_21_), channel_id=1, source_target_pairs={{8,0},{12,4},{9,1},{13,5},{10,2},{14,6},{11,3},{15,7}} | collective-permute-start | bytes 5898248 | tf_op jit(solution)/shard_map/ppermute | solution.py:290
  186.2 130.4 %collective-permute-start.6 = (bf16[1280,768]{1,0:T(8,128)(2,1)}, bf16[1280,768]{1,0:T(8,128)(2,1)}, u32[]{:S(2)}, u32[]{:S(2)}) collective-permute-start(bf16[1280,768]{1,0:T(8,128)(2,1)} %maximum_select_fusion.refs_19_), channel_id=1, source_target_pairs={{0,8},{4,12},{8,16},{12,20},{16,24},{20,28},{1,9},{5,13},{9,17},{1... | collective-permute-start | bytes 5898248 | tf_op jit(solution)/shard_map/ppermute | solution.py:290
  204.8 112.3 %collective-permute-start.7 = (bf16[1280,768]{1,0:T(8,128)(2,1)}, bf16[1280,768]{1,0:T(8,128)(2,1)}, u32[]{:S(2)}, u32[]{:S(2)}) collective-permute-start(bf16[1280,768]{1,0:T(8,128)(2,1)} %maximum_select_fusion.refs_19_), channel_id=1, source_target_pairs={{8,0},{12,4},{16,8},{20,12},{24,16},{28,20},{9,1},{13,5},{17,9},{2... | collective-permute-start | bytes 5898248 | tf_op jit(solution)/shard_map/ppermute | solution.py:290
  208.2 107.9 %collective-permute-start.49 = (bf16[3,256,1024]{2,1,0:T(8,128)(2,1)}, bf16[3,256,1024]{2,1,0:T(8,128)(2,1)}, u32[]{:S(2)}, u32[]{:S(2)}) collective-permute-start(bf16[3,256,1024]{2,1,0:T(8,128)(2,1)} %pad_maximum_fusion.7), channel_id=1, source_target_pairs={{8,0},{12,4},{9,1},{13,5},{10,2},{14,6},{11,3},{15,7}} | collective-permute-start | bytes 4718600 | tf_op jit(solution)/shard_map/ppermute | solution.py:290
  323.1 47.8 %collective-permute-start.11 = (bf16[1280,768]{1,0:T(8,128)(2,1)}, bf16[1280,768]{1,0:T(8,128)(2,1)}, u32[]{:S(2)}, u32[]{:S(2)}) collective-permute-start(bf16[1280,768]{1,0:T(8,128)(2,1)} %collective-permute-done.7.refs_20_), channel_id=1, source_target_pairs={{8,0},{12,4},{16,8},{20,12},{9,1},{13,5},{17,9},{21,13},{10,2},{14... | collective-permute-start | bytes 5898248 | tf_op jit(solution)/shard_map/ppermute | solution.py:290
  370.9 86.0 %collective-permute-start.14 = (bf16[1280,768]{1,0:T(8,128)(2,1)}, bf16[1280,768]{1,0:T(8,128)(2,1)}, u32[]{:S(2)}, u32[]{:S(2)}) collective-permute-start(bf16[1280,768]{1,0:T(8,128)(2,1)} %collective-permute-done.10.refs_17_), channel_id=1, source_target_pairs={{16,24},{20,28},{17,25},{21,29},{18,26},{22,30},{19,27},{23,31}} | collective-permute-start | bytes 5898248 | tf_op jit(solution)/shard_map/ppermute | solution.py:290
  372.8 84.1 %collective-permute-start.15 = (bf16[1280,768]{1,0:T(8,128)(2,1)}, bf16[1280,768]{1,0:T(8,128)(2,1)}, u32[]{:S(2)}, u32[]{:S(2)}) collective-permute-start(bf16[1280,768]{1,0:T(8,128)(2,1)} %collective-permute-done.11.refs_21_), channel_id=1, source_target_pairs={{8,0},{12,4},{9,1},{13,5},{10,2},{14,6},{11,3},{15,7}} | collective-permute-start | bytes 5898248 | tf_op jit(solution)/shard_map/ppermute | solution.py:290
  374.1 54.8 %collective-permute-start.12 = (bf16[512,1280]{1,0:T(8,128)(2,1)}, bf16[512,1280]{1,0:T(8,128)(2,1)}, u32[]{:S(2)}, u32[]{:S(2)}) collective-permute-start(bf16[512,1280]{1,0:T(8,128)(2,1)} %refs_6_.1), channel_id=1, source_target_pairs={{0,8},{4,12},{8,16},{12,20},{16,24},{20,28},{1,9},{5,13},{9,17},{1... | collective-permute-start | bytes 3932168 | tf_op jit(solution)/shard_map/ppermute | solution.py:290
  428.9 45.3 %collective-permute-start.66 = (bf16[768,512]{1,0:T(8,128)(2,1)S(1)}, bf16[768,512]{1,0:T(8,128)(2,1)S(1)}, u32[]{:S(2)}, u32[]{:S(2)}) collective-permute-start(bf16[768,512]{1,0:T(8,128)(2,1)S(1)} %pad_maximum_fusion.8), channel_id=1, source_target_pairs={{0,4},{4,0},{8,12},{12,8},{16,20},{20,16},{24,28},{28,24},{1,5},{5... | collective-permute-start | bytes 2359304 | tf_op jit(solution)/shard_map/ppermute | solution.py:283
  460.2 41.5 %collective-permute-start.16 = (bf16[512,1280]{1,0:T(8,128)(2,1)}, bf16[512,1280]{1,0:T(8,128)(2,1)}, u32[]{:S(2)}, u32[]{:S(2)}) collective-permute-start(bf16[512,1280]{1,0:T(8,128)(2,1)} %collective-permute-done.12.refs_4_), channel_id=1, source_target_pairs={{8,16},{12,20},{16,24},{20,28},{9,17},{13,21},{17,25},{21,29},{10,... | collective-permute-start | bytes 3932168 | tf_op jit(solution)/shard_map/ppermute | solution.py:290
  497.1 61.0 %collective-permute-start.21 = (bf16[512,1280]{1,0:T(8,128)(2,1)}, bf16[512,1280]{1,0:T(8,128)(2,1)S(1)}, u32[]{:S(2)}, u32[]{:S(2)}) collective-permute-start(bf16[512,1280]{1,0:T(8,128)(2,1)} %collective-permute-done.12.refs_4_), channel_id=1, source_target_pairs={{8,12},{12,8},{16,20},{20,16},{24,28},{28,24},{9,13},{13,9},{17,21... | collective-permute-start | bytes 3932168 | tf_op jit(solution)/shard_map/ppermute | solution.py:283
  497.9 60.8 %collective-permute-start.23 = (bf16[512,1280]{1,0:T(8,128)(2,1)}, bf16[512,1280]{1,0:T(8,128)(2,1)S(1)}, u32[]{:S(2)}, u32[]{:S(2)}) collective-permute-start(bf16[512,1280]{1,0:T(8,128)(2,1)} %collective-permute-done.13.refs_8_), channel_id=1, source_target_pairs={{0,4},{4,0},{8,12},{12,8},{16,20},{20,16},{1,5},{5,1},{9,13},{13,9... | collective-permute-start | bytes 3932168 | tf_op jit(solution)/shard_map/ppermute | solution.py:283
  512.6 50.5 %collective-permute-start.67 = (bf16[768,512]{1,0:T(8,128)(2,1)S(1)}, bf16[768,512]{1,0:T(8,128)(2,1)S(1)}, u32[]{:S(2)}, u32[]{:S(2)}) collective-permute-start(bf16[768,512]{1,0:T(8,128)(2,1)S(1)} %pad_maximum_fusion.9), channel_id=1, source_target_pairs={{0,4},{4,0},{8,12},{12,8},{16,20},{20,16},{24,28},{28,24},{1,5},{5... | collective-permute-start | bytes 2359304 | tf_op jit(solution)/shard_map/ppermute | solution.py:283
  524.0 56.5 %collective-permute-start.18 = (bf16[512,1280]{1,0:T(8,128)(2,1)}, bf16[512,1280]{1,0:T(8,128)(2,1)}, u32[]{:S(2)}, u32[]{:S(2)}) collective-permute-start(bf16[512,1280]{1,0:T(8,128)(2,1)} %collective-permute-done.16.refs_2_), channel_id=1, source_target_pairs={{16,24},{20,28},{17,25},{21,29},{18,26},{22,30},{19,27},{23,31}} | collective-permute-start | bytes 3932168 | tf_op jit(solution)/shard_map/ppermute | solution.py:290
  525.7 55.5 %collective-permute-start.25 = (bf16[512,1280]{1,0:T(8,128)(2,1)}, bf16[512,1280]{1,0:T(8,128)(2,1)}, u32[]{:S(2)}, u32[]{:S(2)}) collective-permute-start(bf16[512,1280]{1,0:T(8,128)(2,1)} %collective-permute-done.17.refs_10_), channel_id=1, source_target_pairs={{8,0},{12,4},{9,1},{13,5},{10,2},{14,6},{11,3},{15,7}} | collective-permute-start | bytes 3932168 | tf_op jit(solution)/shard_map/ppermute | solution.py:290
  581.2 54.7 %collective-permute-start.26 = (bf16[512,1280]{1,0:T(8,128)(2,1)}, bf16[512,1280]{1,0:T(8,128)(2,1)}, u32[]{:S(2)}, u32[]{:S(2)}) collective-permute-start(bf16[512,1280]{1,0:T(8,128)(2,1)} %collective-permute-done.25.refs_12_), channel_id=1, source_target_pairs={{0,4},{4,0},{1,5},{5,1},{2,6},{6,2},{3,7},{7,3}} | collective-permute-start | bytes 3932168 | tf_op jit(solution)/shard_map/ppermute | solution.py:283
  (83 other events, 1570.7 us)

commit v2 on v1

--- a/solution.py
+++ b/solution.py
@@ -28,17 +28,24 @@
     return max(t for t in range(16, most + 1, 16) if rows % t == 0)
 
 
-def qkv_kernel(planes, count, z_ref, at_ref, *refs):
-    blocks, pieces = refs[:count], refs[count : count + 2 * planes - 1]
-    out_ref, a_ref, w_ref, sems = refs[count + 2 * planes - 1 :]
+def qkv_kernel(planes, count, finish, z_ref, at_ref, *refs):
+    blocks = refs[:count]
+    pieces = refs[count : -5 if finish else -4]
+    start_ref = refs[-5] if finish else None
+    out_ref, a_ref, w_ref, sems = refs[-4:]
     z = z_ref[0]
     depth = pieces[0].shape[0]
     n, m = blocks[0].shape
     t = pl.program_id(0)
 
+    def present(plane):
+        away = jnp.abs(plane - z)
+        return away == planes - 1 if finish else away < planes - 1
+
     def each_weight(act):
         for i, piece in enumerate(pieces):
-            at = z + i - (planes - 1)
+            off = (1 - planes, planes - 1)[i] if finish else i - (planes - 2)
+            at = z + off
 
             @pl.when(jnp.logical_and(at >= 0, at < planes))
             def _():
@@ -48,8 +55,13 @@
     def each_block(act, tile):
         for i, block in enumerate(blocks):
             row, column = at_ref[i, 0], at_ref[i, 1]
-
-            @pl.when(row == tile)
+            used = row == tile
+            if finish:
+                near = column * m
+                first = jnp.logical_and(z == 0, near + m > (planes - 1) * depth)
+                used = jnp.logical_and(used, jnp.logical_or(first, jnp.logical_and(z == planes - 1, near < depth)))
+
+            @pl.when(used)
             def _():
                 to = a_ref.at[pl.ds(pl.multiple_of(row * n, n), n), pl.ds(pl.multiple_of(column * m, m), m)]
                 act(pltpu.make_async_copy(block, to, sems.at[i]))
@@ -62,11 +74,29 @@
         each_weight(lambda copy: copy.wait())
 
     each_block(lambda copy: copy.wait(), t)
-    a = a_ref[pl.ds(pl.multiple_of(t * n, n), n), :]
-    out_ref[...] = jnp.dot(a, w_ref[...], preferred_element_type=jnp.float32).astype(out_ref.dtype)
-
-
-def qkv_call(z, at, blocks, shape, pieces):
+    rows = pl.ds(pl.multiple_of(t * n, n), n)
+
+    def product(plane):
+        there = slice(plane * depth, (plane + 1) * depth)
+        return jnp.dot(a_ref[rows, there], w_ref[there, :], preferred_element_type=jnp.float32)
+
+    if finish:
+        out_ref[...] = start_ref[...].astype(out_ref.dtype)
+        for plane in (0, planes - 1):
+
+            @pl.when(present(plane))
+            def _():
+                out_ref[...] = (start_ref[...] + product(plane)).astype(out_ref.dtype)
+    else:
+        out_ref[...] = jnp.zeros(out_ref.shape, out_ref.dtype)
+        for plane in range(planes):
+
+            @pl.when(present(plane))
+            def _():
+                out_ref[...] += product(plane)
+
+
+def qkv_call(z, at, blocks, shape, pieces, start=None):
     rows, width = shape
     n, m = blocks[0].shape
     if n % 16 or m % HD:
@@ -75,16 +105,18 @@
             whole = lax.dynamic_update_slice(whole, block, (at[i, 0] * n, at[i, 1] * m))
         n, m = shape
         blocks, at = [whole], jnp.zeros((1, 2), jnp.int32)
-    planes = (len(pieces) + 1) // 2
-    columns = pieces[0].shape[1]
+    finish = start is not None
+    depth, columns = pieces[0].shape
+    planes = width // depth
+    out = pl.BlockSpec((n, columns), lambda i, *_: (i, 0))
     return pl.pallas_call(
-        functools.partial(qkv_kernel, planes, len(blocks)),
-        out_shape=jax.ShapeDtypeStruct((rows, columns), jnp.bfloat16),
+        functools.partial(qkv_kernel, planes, len(blocks), finish),
+        out_shape=jax.ShapeDtypeStruct((rows, columns), jnp.bfloat16 if finish else jnp.float32),
         grid_spec=pltpu.PrefetchScalarGridSpec(
             num_scalar_prefetch=2,
             grid=(rows // n,),
-            in_specs=[pl.BlockSpec(memory_space=pl.ANY)] * (len(blocks) + len(pieces)),
-            out_specs=pl.BlockSpec((n, columns), lambda i, *_: (i, 0)),
+            in_specs=[pl.BlockSpec(memory_space=pl.ANY)] * (len(blocks) + len(pieces)) + [out] * finish,
+            out_specs=out,
             scratch_shapes=[
                 pltpu.VMEM((rows, width), jnp.bfloat16),
                 pltpu.VMEM((width, columns), jnp.bfloat16),
@@ -93,12 +125,12 @@
         ),
         compiler_params=pltpu.CompilerParams(vmem_limit_bytes=VMEM),
         cost_estimate=pl.CostEstimate(
-            flops=2 * rows * width * columns,
+            flops=2 * rows * columns * (depth if finish else width),
             bytes_accessed=2 * (rows * width + width * columns + rows * columns),
             transcendentals=0,
         ),
-        name="qkv",
-    )(z, at, *blocks, *pieces)
+        name="qkv_end" if finish else "qkv_start",
+    )(z, at, *blocks, *pieces, *([start] if finish else []))
 
 
 def attention_kernel(heads, groups, need_ref, q_ref, own_ref, low_ref, high_ref, prefix_ref, qtag_ref, ktag_ref,
@@ -215,7 +247,7 @@
         def each(act):
             for i, piece in enumerate(columns):
                 m = piece.shape[1]
-                to = a_ref.at[:, pl.ds(pl.multiple_of(at_ref[i] * m, m), m)]
+                to = a_ref.at[:, pl.ds(pl.multiple_of(at_ref[i] * HD, HD), m)]
                 act(pltpu.make_async_copy(piece, to, sems.at[count + i]))
             for i, piece in enumerate(pieces):
                 plane = z + i // 2 - (planes - 1)
@@ -271,8 +303,9 @@
     tokens, width = hidden_in.shape
     local_heads = w_qkv.shape[1] // (3 * HD)
     heads = local_heads // 2
-    parts = 2 if heads % 2 == 0 else 1
-    hc = heads // parts
+    counts = [heads // 2] * 2 if heads % 2 == 0 else [heads]
+    firsts = [sum(counts[:i]) for i in range(len(counts))]
+    parts = len(counts)
     groups = owner.shape[0]
     requests = req_len.shape[0]
     r, c = lax.axis_index("row"), lax.axis_index("col")
@@ -289,24 +322,18 @@
         pairs = [(2 * p + i, 2 * (p + by) + i) for p in sources for i in range(2)]
         return lax.ppermute(v, "row", pairs)
 
-    under_way = []
-
-    def line_step(v, w, step):
-        if len(under_way) >= 2:
-            v, w, _, _ = lax.optimization_barrier((v, w) + under_way[-2])
-        right = z_move(v, 1, range(step - 1, planes - 1))
-        left = z_move(w, -1, range(1, planes - step + 1))
-        under_way.append((right, left))
-        return right, left
-
-    def line_gather(own):
-        lows, highs = [], []
-        low = high = own
-        for step in range(1, planes):
-            low, high = line_step(low, high, step)
-            lows.append(low)
-            highs.append(high)
-        return lows[::-1] + [own] + highs
+    def after(v, deps):
+        return lax.optimization_barrier((v, *deps))[0] if deps else v
+
+    def line_step(v, step, deps=()):
+        low, high = lax.optimization_barrier((*v, *deps))[:2] if deps else v
+        return (
+            z_move(low, 1, range(step - 1, planes - 1)),
+            z_move(high, -1, range(1, planes - step + 1)),
+        )
+
+    def in_order(own, steps):
+        return [low for low, _ in steps[::-1]] + [own] + [high for _, high in steps]
 
     def by_x(mine, other, axis):
         return jnp.where(
@@ -318,19 +345,25 @@
     def columns_of(v, start, size):
         return lax.dynamic_slice_in_dim(v, start, size, v.ndim - 1)
 
-    def plane_weights(part):
-        size = hc * 3 * HD
-        mine = columns_of(w_qkv, x * heads * 3 * HD + part * size, size)
-        other = columns_of(w_qkv, (1 - x) * heads * 3 * HD + part * size, size)
-        return by_x(mine, swap_x(other), 0)
-
-    weights = [plane_weights(part) for part in range(parts)]
+    def plane_weights(part, deps=()):
+        size = counts[part] * 3 * HD
+        at = firsts[part] * 3 * HD
+        mine = columns_of(w_qkv, x * heads * 3 * HD + at, size)
+        other = columns_of(w_qkv, (1 - x) * heads * 3 * HD + at, size)
+        return by_x(mine, swap_x(after(other, deps)), 0)
+
+    out_steps = [line_step((w_out, w_out), 1)]
+    owns = [plane_weights(0)]
+    steps = [[line_step((owns[0], owns[0]), 1, out_steps[0])]]
+    for part in range(1, parts):
+        owns.append(plane_weights(part, owns[:1]))
+        steps.append([line_step((owns[part],) * 2, 1)])
 
     kv_width = heads * 2 * HD
     slot = prefix_cache[0]
     mine = columns_of(slot, x * kv_width, kv_width)
     other = columns_of(slot, (1 - x) * kv_width, kv_width)
-    here = by_x(mine[None], swap_x(other)[None], 0)
+    here = by_x(mine[None], swap_x(after(other, owns))[None], 0)
     owner_plane = owner // 2
 
     def beyond(plane, side):
@@ -348,22 +381,25 @@
             picked.append(lax.dynamic_slice_in_dim(pool, at, 1, 0))
         return jnp.concatenate(picked, 0)
 
-    held_low = held_high = jnp.zeros((groups - 1,) + here.shape[1:], here.dtype)
-    for step in range(planes - 1):
-        came = z_move(outgoing(-1, held_low), 1, [step])
-        held_low = jnp.where(z == step + 1, came, held_low)
-        came = z_move(outgoing(1, held_high), -1, [planes - 1 - step])
-        held_high = jnp.where(z == planes - 2 - step, came, held_high)
-    pool = jnp.concatenate([here, held_low, held_high], 0)
-    low_order, high_order = beyond(z, -1)[1], beyond(z, 1)[1]
-    source = jnp.where(
-        owner_plane == z,
-        owner % 2,
-        jnp.where(owner_plane < z, 2 + low_order, 2 + groups - 1 + high_order),
-    )
-    prefix = jnp.concatenate(
-        [lax.dynamic_slice_in_dim(pool, source[g], 1, 0) for g in range(groups)], 0
-    )
+    held = [jnp.zeros((groups - 1,) + here.shape[1:], here.dtype)] * 2
+
+    def prefix_step(step, deps):
+        last = planes - 1 - step
+        low, high = lax.optimization_barrier((outgoing(-1, held[0]), outgoing(1, held[1]), *deps))[:2]
+        low, high = z_move(low, 1, [step]), z_move(high, -1, [last])
+        held[0] = jnp.where(z == step + 1, low, held[0])
+        held[1] = jnp.where(z == last - 1, high, held[1])
+        return low, high
+
+    def prefix_of_groups():
+        pool = jnp.concatenate([here] + held, 0)
+        low_order, high_order = beyond(z, -1)[1], beyond(z, 1)[1]
+        source = jnp.where(
+            owner_plane == z,
+            owner % 2,
+            jnp.where(owner_plane < z, 2 + low_order, 2 + groups - 1 + high_order),
+        )
+        return jnp.concatenate([lax.dynamic_slice_in_dim(pool, source[g], 1, 0) for g in range(groups)], 0)
 
     positions = r * tokens + jnp.arange(tokens, dtype=jnp.int32)
     request_id = request_of(positions, req_len)
@@ -381,22 +417,6 @@
     modulated = (
         (hidden_f - mean[:, None]) * lax.rsqrt(variance[:, None] + 1e-06) * (1.0 + scale) + shift
     ).astype(jnp.bfloat16)
-
-    half = tokens // 2
-    col_bits = [1 << b for b in reversed(range(cols_n.bit_length() - 1))]
-    full_pieces, full_at = [], []
-    for i in range(2):
-        pieces = [(modulated[i * half : (i + 1) * half], 0, 0)]
-        order = [0] + col_bits if i == 0 else col_bits[:-1] + [0] + col_bits[-1:]
-        for bit in order:
-            if bit == 0:
-                pieces += [(swap_x(v), 1, cb) for v, _, cb in pieces]
-            else:
-                pieces += [(swap_col(v, bit), xb, cb ^ bit) for v, xb, cb in pieces]
-        for v, xb, cb in pieces:
-            full_pieces.append(v)
-            full_at.append(jnp.stack([(x ^ xb) * 2 + i, c ^ cb]))
-    full_at = jnp.stack(full_at)
 
     rows = 2 * tokens
     key_pos = z * rows - HALO + jnp.arange(rows + 2 * HALO, dtype=jnp.int32)
@@ -419,11 +439,56 @@
     need_near = (lowest[None, :] <= tile_req[:, -1:]) & (highest[None, :] >= tile_req[:, :1])
     need = jnp.concatenate([need_group, need_near], axis=1).astype(jnp.int32)
 
+    half = tokens // 2
+    col_bits = [1 << b for b in reversed(range(cols_n.bit_length() - 1))]
+    hops = [[(modulated[i * half : (i + 1) * half], 0, 0)] for i in range(2)]
+    orders = [[0] + col_bits, col_bits[:-1] + [0] + col_bits[-1:]]
+
+    def hop(step):
+        came = []
+        for i in range(2):
+            bit = orders[i][step]
+            if bit == 0:
+                new = [(swap_x(v), 1, cb) for v, _, cb in hops[i]]
+            else:
+                new = [(swap_col(v, bit), xb, cb ^ bit) for v, xb, cb in hops[i]]
+            hops[i] += new
+            came += [v for v, _, _ in new]
+        return came
+
+    came, hops_left = hop(0) + [need, qtag, ktag], list(range(1, len(col_bits) + 1))
+    for step in range(planes - 2):
+        for part in range(parts):
+            steps[part].append(line_step(steps[part][-1], step + 2, came))
+            came = hop(hops_left.pop(0)) if hops_left else ()
+        prefix_step(step, steps[-1][step])
+    for step in hops_left:
+        hop(step)
+    prefix_step(planes - 2, steps[-1][-2])
+    full_pieces = [v for pieces in hops for v, _, _ in pieces]
+    full_at = jnp.stack(
+        [jnp.stack([(x ^ xb) * 2 + i, c ^ cb]) for i, pieces in enumerate(hops) for _, xb, cb in pieces]
+    )
+
+    def halves(piece, off, deps=()):
+        return [piece, swap_x(after(piece, deps), lambda p: 0 <= p + off < planes)]
+
+    first_out = [
+        halves(piece, off, steps[-1][-2]) for piece, off in ((out_steps[0][0], -1), (w_out, 0), (out_steps[0][1], 1))
+    ]
+    begun = [
+        qkv_call(z[None], full_at, full_pieces, (rows, width * cols_n), in_order(owns[part], steps[part][:-1]))
+        for part in range(parts)
+    ]
     keys = jnp.zeros((tokens, local_heads * HD), jnp.bfloat16)
     values = keys
     attended, attended_at = [], []
     for part in range(parts):
-        qkv = qkv_call(z[None], full_at, full_pieces, (rows, width * cols_n), line_gather(weights[part]))
+        hc = counts[part]
+        behind = [v for pair in first_out for v in pair] if part == parts - 1 else []
+        qkv = qkv_call(
+            after(z[None], behind), full_at, full_pieces, (rows, width * cols_n), steps[part][-1], begun[part]
+        )
 
         def kv_of(start, size):
             kv = lax.dynamic_slice_in_dim(qkv, start, size, 0)
@@ -431,28 +496,36 @@
 
         low = z_move(kv_of(rows - MOST, MOST), 1, range(planes - 1))
         high = z_move(kv_of(0, MOST), -1, range(1, planes))
+        if part == 0:
+            for step in range(2, planes):
+                out_steps.append(line_step(out_steps[-1], step, (low, high) if step == 2 else ()))
         own_kv = kv_of(x * tokens, tokens)
         other_kv = swap_x(kv_of((1 - x) * tokens, tokens))
         for xb, v in ((0, own_kv), (1, other_kv)):
-            at = ((x ^ xb) * heads + part * hc) * HD
+            at = ((x ^ xb) * heads + firsts[part]) * HD
             k = jnp.concatenate([v[:, 2 * j * HD : (2 * j + 1) * HD] for j in range(hc)], 1)
             v = jnp.concatenate([v[:, (2 * j + 1) * HD : (2 * j + 2) * HD] for j in range(hc)], 1)
             keys = lax.dynamic_update_slice(keys, k, (0, at))
             values = lax.dynamic_update_slice(values, v, (0, at))
-        part_prefix = prefix[:, :, part * hc * 2 * HD : (part + 1) * hc * 2 * HD]
+        if part == 0:
+            prefix = prefix_of_groups()
+        part_prefix = prefix[:, :, firsts[part] * 2 * HD : (firsts[part] + hc) * 2 * HD]
         out = attention_call(need, qkv, low, high, part_prefix, qtag, ktag)
         pieces = [(lax.dynamic_slice_in_dim(out, x * tokens, tokens, 0), 0, 0)]
-        pieces.append((swap_x(lax.dynamic_slice_in_dim(out, (1 - x) * tokens, tokens, 0)), 1, 0))
+        behind = out_steps[-1] if part == parts - 1 else out_steps[1]
+        other = lax.dynamic_slice_in_dim(out, (1 - x) * tokens, tokens, 0)
+        pieces.append((swap_x(after(other, behind)), 1, 0))
         for bit in col_bits:
             pieces += [(swap_col(v, bit), xb, cb ^ bit) for v, xb, cb in pieces]
         for v, xb, cb in pieces:
             attended.append(v)
-            attended_at.append(((c ^ cb) * 2 + (x ^ xb)) * parts + part)
-
-    out_pieces = []
-    for i, piece in enumerate(line_gather(w_out)):
-        off = i - (planes - 1)
-        out_pieces += [piece, swap_x(piece, lambda p: 0 <= p + off < planes)]
+            attended_at.append((c ^ cb) * local_heads + (x ^ xb) * heads + firsts[part])
+
+    out_pairs = first_out
+    for step in range(2, planes):
+        low, high = out_steps[step - 1]
+        out_pairs = [halves(low, -step)] + out_pairs + [halves(high, step)]
+    out_pieces = [piece for pair in out_pairs for piece in pair]
     hidden_out = out_call(
         jnp.stack([z, x]), jnp.stack(attended_at), attended, hidden_in, gate.astype(jnp.bfloat16), out_pieces
     )

time: 656 us -> 606 us (0.924)
  waiting for transfers between devices: 334 us -> 242 us
  Pallas kernels: 116 us -> 141 us
  starting transfers between devices: 115 us -> 123 us
    ppermute x28, waiting for transfers between devices: 206 us -> 79.6 us  [z_move(): return lax.ppermute(v, 'row', pairs)]
    ppermute x17, waiting for transfers between devices: 106 us -> 149 us  [swap_x(): lax.ppermute(v, 'row', [(i, i ^ 1) for i in range(rows_n) if valid(i // 2)])]
    pallas_call x2 -> x4, Pallas kernels: 38.6 us -> 54.9 us  [qkv_call(): pl.pallas_call(functools.partial(qkv_kernel, planes, len(blocks), finish)...]
    pallas_call x2, Pallas kernels: 60 us -> 68.5 us  [attention_call(): pl.pallas_call(functools.partial(attention_kernel, heads, groups), out_sh...]
    ppermute x23, waiting for transfers between devices: 21.7 us -> 14.1 us  [swap_col(): return lax.ppermute(v, 'col', [(i, i ^ bit) for i in range(cols_n)])]
  transfers between devices with their start and end apart: 68 -> 68, of which waited for: 22 -> 20; matrix products, arithmetic and copies ran while one was open for 9% -> 10% of each run, Pallas kernels for 15% -> 21%
where the time goes in v2:
time: 606 us; the launch traced here: 599 us
  waiting for transfers between devices  242 us (40%)
  Pallas kernels  141 us (23%)
  starting transfers between devices  123 us (20%)
  other arithmetic  32.8 us (5%)
  local copies, waits for them, and re-layouts  29.6 us (5%)
  between operations  20.3 us (3%)
    ppermute x17, waiting for transfers between devices, swap_x(): lax.ppermute(v, 'row', [(i, i ^ 1) for i in range(rows_n) if valid(i // 2)])  149 us
    ppermute x28, starting transfers between devices, z_move(): return lax.ppermute(v, 'row', pairs)  84.6 us
    ppermute x28, waiting for transfers between devices, z_move(): return lax.ppermute(v, 'row', pairs)  79.6 us
    pallas_call x2, Pallas kernels, attention_call(): pl.pallas_call(functools.partial(attention_kernel, heads, groups), out_sh...  68.5 us
    pallas_call x4, Pallas kernels, qkv_call(): pl.pallas_call(functools.partial(qkv_kernel, planes, len(blocks), finish)...  54.9 us
    ppermute x17, starting transfers between devices, swap_x(): lax.ppermute(v, 'row', [(i, i ^ 1) for i in range(rows_n) if valid(i // 2)])  25.9 us
    pallas_call x1, Pallas kernels, out_call(): pl.pallas_call(functools.partial(out_kernel, planes, len(columns)), out_s...  17.7 us
    ppermute x23, waiting for transfers between devices, swap_col(): return lax.ppermute(v, 'col', [(i, i ^ bit) for i in range(cols_n)])  14.1 us
  transfers between devices with their start and end apart: 68, of which 20 were waited for; matrix products, arithmetic and copies ran while one was open for 10% of the time, Pallas kernels for 21%

profile of v2, /device:TPU:0, one launch (start us, length us, event | category | flops | bytes accessed | tf_op | source)
XLA Modules:
  0.0 598.6 jit_solution(3083672612534283528)
XLA Ops:
  24.4 6.3 %collective-permute-done.16 = bf16[640,768]{1,0:T(8,128)(2,1)} collective-permute-done((bf16[640,768]{1,0:T(8,128)(2,1)}, bf16[640,768]{1,0:T(8,128)(2,1)}, u32[]{:S(2)}, u32[]{:S(2)}) %collective-permute-start.16) | collective-permute-done | bytes 983072 | tf_op jit(solution)/shard_map/ppermute | solution.py:316
  32.8 18.9 %collective-permute-done.2.refs_1_ = bf16[384,1280]{1,0:T(8,128)(2,1)S(1)} collective-permute-done((bf16[384,1280]{1,0:T(8,128)(2,1)S(1)}, bf16[384,1280]{1,0:T(8,128)(2,1)S(1)}, u32[]{:S(2)}, u32[]{:S(2)}) %collective-permute-start.2) | collective-permute-done | bytes 983072 | tf_op jit(solution)/shard_map/ppermute | solution.py:316
  59.8 13.1 %collective-permute-done.10.refs_10_ = bf16[384,1280]{1,0:T(8,128)(2,1)} collective-permute-done((bf16[384,1280]{1,0:T(8,128)(2,1)S(1)}, bf16[384,1280]{1,0:T(8,128)(2,1)}, u32[]{:S(2)}, u32[]{:S(2)}) %collective-permute-start.10) | collective-permute-done | bytes 983072 | tf_op jit(solution)/shard_map/ppermute | solution.py:316
  82.8 11.1 %collective-permute-done.29 = bf16[640,768]{1,0:T(8,128)(2,1)} collective-permute-done((bf16[640,768]{1,0:T(8,128)(2,1)}, bf16[640,768]{1,0:T(8,128)(2,1)}, u32[]{:S(2)}, u32[]{:S(2)}) %collective-permute-start.29) | collective-permute-done | bytes 983072 | tf_op jit(solution)/shard_map/ppermute | solution.py:316
  98.0 16.1 %collective-permute-done.11.refs_11_ = bf16[384,1280]{1,0:T(8,128)(2,1)} collective-permute-done((bf16[384,1280]{1,0:T(8,128)(2,1)}, bf16[384,1280]{1,0:T(8,128)(2,1)}, u32[]{:S(2)}, u32[]{:S(2)}) %collective-permute-start.11) | collective-permute-done | bytes 983072 | tf_op jit(solution)/shard_map/ppermute | solution.py:316
  131.4 7.4 %collective-permute-done.41 = bf16[256,1024]{1,0:T(8,128)(2,1)} collective-permute-done((bf16[256,1024]{1,0:T(8,128)(2,1)S(1)}, bf16[256,1024]{1,0:T(8,128)(2,1)}, u32[]{:S(2)}, u32[]{:S(2)}) %collective-permute-start.41) | collective-permute-done | bytes 524320 | tf_op jit(solution)/shard_map/ppermute | solution.py:316
  140.0 19.5 %collective-permute-done.30.refs_17_ = bf16[1280,768]{1,0:T(8,128)(2,1)} collective-permute-done((bf16[1280,768]{1,0:T(8,128)(2,1)}, bf16[1280,768]{1,0:T(8,128)(2,1)}, u32[]{:S(2)}, u32[]{:S(2)}) %collective-permute-start.30) | collective-permute-done | bytes 1966112 | tf_op jit(solution)/shard_map/ppermute | solution.py:323
  198.1 14.2 %collective-permute-done.20.refs_20_ = bf16[1280,768]{1,0:T(8,128)(2,1)} collective-permute-done((bf16[1280,768]{1,0:T(8,128)(2,1)}, bf16[1280,768]{1,0:T(8,128)(2,1)}, u32[]{:S(2)}, u32[]{:S(2)}) %collective-permute-start.20) | collective-permute-done | bytes 1966112 | tf_op jit(solution)/shard_map/ppermute | solution.py:323
  213.3 17.7 %qkv_start.2.refs_18_ = f32[1536,768]{1,0:T(8,128)} custom-call(s32[1]{0:T(128)} %bitcast.z_ref, s32[16,2]{1,0:T(8,128)} %stack.276.at_ref, bf16[384,1280]{1,0:T(8,128)(2,1)} %copy-done.3, bf16[384,1280]{1,0:T(8,128)(2,1)} %copy-done.4, bf16[384,1280]{1,0:T(8,128)(2,1)} %collective-permute-done.3.refs_2_, bf16[384,1280]{1,0:T(8,128)(2,1)} %collective-permute-done.4.refs_3_, ...), custom_call_target="tpu_custom_call" | custom-call | flops 12079595520 | bytes 25952256 | tf_op jit(solution)/shard_map/qkv_start/pallas_call | solution.py:112
  236.5 17.9 %collective-permute-done.33.refs_20_ = bf16[1280,768]{1,0:T(8,128)(2,1)} collective-permute-done((bf16[1280,768]{1,0:T(8,128)(2,1)}, bf16[1280,768]{1,0:T(8,128)(2,1)}, u32[]{:S(2)}, u32[]{:S(2)}) %collective-permute-start.33) | collective-permute-done | bytes 1966112 | tf_op jit(solution)/shard_map/ppermute | solution.py:323
  260.0 17.8 %qkv_start.3.refs_18_ = f32[1536,768]{1,0:T(8,128)} custom-call(s32[1]{0:T(128)} %bitcast.z_ref, s32[16,2]{1,0:T(8,128)} %stack.276.at_ref, bf16[384,1280]{1,0:T(8,128)(2,1)} %copy-done.3, bf16[384,1280]{1,0:T(8,128)(2,1)} %copy-done.4, bf16[384,1280]{1,0:T(8,128)(2,1)} %collective-permute-done.3.refs_2_, bf16[384,1280]{1,0:T(8,128)(2,1)} %collective-permute-done.4.refs_3_, ...), custom_call_target="tpu_custom_call" | custom-call | flops 12079595520 | bytes 25952256 | tf_op jit(solution)/shard_map/qkv_start/pallas_call | solution.py:112
  279.7 14.1 %collective-permute-done.22.refs_17_ = bf16[1280,768]{1,0:T(8,128)(2,1)S(1)} collective-permute-done((bf16[1280,768]{1,0:T(8,128)(2,1)}, bf16[1280,768]{1,0:T(8,128)(2,1)S(1)}, u32[]{:S(2)}, u32[]{:S(2)}) %collective-permute-start.22) | collective-permute-done | bytes 1966112 | tf_op jit(solution)/shard_map/ppermute | solution.py:323
  295.2 9.7 %qkv_end.2.q_ref.own_ref = bf16[1536,768]{1,0:T(8,128)(2,1)} custom-call(s32[1]{0:T(128)} %bitcast.z_ref, s32[16,2]{1,0:T(8,128)} %stack.276.at_ref, bf16[384,1280]{1,0:T(8,128)(2,1)} %copy-done.3, bf16[384,1280]{1,0:T(8,128)(2,1)} %copy-done.4, bf16[384,1280]{1,0:T(8,128)(2,1)} %collective-permute-done.3.refs_2_, ...), custom_call_target="tpu_custom_call" | custom-call | flops 3019898880 | bytes 25952256 | tf_op jit(solution)/shard_map/qkv_end/pallas_call | solution.py:112
  313.9 21.5 %collective-permute-done.35.refs_7_ = bf16[512,1280]{1,0:T(8,128)(2,1)S(1)} collective-permute-done((bf16[512,1280]{1,0:T(8,128)(2,1)}, bf16[512,1280]{1,0:T(8,128)(2,1)S(1)}, u32[]{:S(2)}, u32[]{:S(2)}) %collective-permute-start.35) | collective-permute-done | bytes 1310752 | tf_op jit(solution)/shard_map/ppermute | solution.py:316
  341.3 28.6 %collective-permute-start.23 = (bf16[672,512]{1,0:T(8,128)(2,1)}, bf16[672,512]{1,0:T(8,128)(2,1)}, u32[]{:S(2)}, u32[]{:S(2)}) collective-permute-start(bf16[672,512]{1,0:T(8,128)(2,1)} %pad_maximum_fusion.10), channel_id=1, source_target_pairs={{0,8},{4,12},{8,16},{12,20},{16,24},{20,28},{1,9},{5,13},{9,17},{1... | collective-permute-start | bytes 2064392 | tf_op jit(solution)/shard_map/ppermute | solution.py:323
  369.9 9.7 %qkv_end.3.q_ref.own_ref = bf16[1536,768]{1,0:T(8,128)(2,1)} custom-call(s32[1]{0:T(128)} %bitcast.z_ref, s32[16,2]{1,0:T(8,128)} %stack.276.at_ref, bf16[384,1280]{1,0:T(8,128)(2,1)} %copy-done.3, bf16[384,1280]{1,0:T(8,128)(2,1)} %copy-done.4, bf16[384,1280]{1,0:T(8,128)(2,1)} %collective-permute-done.3.refs_2_, ...), custom_call_target="tpu_custom_call" | custom-call | flops 3019898880 | bytes 25952256 | tf_op jit(solution)/shard_map/qkv_end/pallas_call | solution.py:112
  399.9 7.1 %collective-permute-done.58.high_ref = bf16[672,512]{1,0:T(8,128)(2,1)S(1)} collective-permute-done((bf16[672,512]{1,0:T(8,128)(2,1)S(1)}, bf16[672,512]{1,0:T(8,128)(2,1)S(1)}, u32[]{:S(2)}, u32[]{:S(2)}) %collective-permute-start.58) | collective-permute-done | bytes 688160 | tf_op jit(solution)/shard_map/ppermute | solution.py:323
  409.4 34.3 %attention.3 = bf16[1536,256]{1,0:T(8,128)(2,1)} custom-call(s32[6,16]{1,0:T(8,128)} %add_convert_fusion.need_ref, bf16[1536,768]{1,0:T(8,128)(2,1)} %qkv_end.3.q_ref.own_ref, bf16[1536,768]{1,0:T(8,128)(2,1)} %qkv_end.3.q_ref.own_ref, bf16[672,512]{1,0:T(8,128)(2,1)} %copy-done.36, bf16[672,512]{1,0:T(8,128)(2,1)} %copy-done.35, ...), custom_call_target="tpu_custom_call" | custom-call | flops 3221225472 | bytes 6291456 | tf_op jit(solution)/shard_map/attention/pallas_call | solution.py:203
  448.6 34.3 %attention.2 = bf16[1536,256]{1,0:T(8,128)(2,1)} custom-call(s32[6,16]{1,0:T(8,128)} %add_convert_fusion.need_ref, bf16[1536,768]{1,0:T(8,128)(2,1)} %qkv_end.2.q_ref.own_ref, bf16[1536,768]{1,0:T(8,128)(2,1)} %qkv_end.2.q_ref.own_ref, bf16[672,512]{1,0:T(8,128)(2,1)} %collective-permute-done.23.low_ref, bf16[672,512]{1,0:T(8,128)(2,1)} %collective-permute-done.24.high_ref, ...), custom_call_target="tpu_custom_call" | custom-call | flops 3221225472 | bytes 6291456 | tf_op jit(solution)/shard_map/attention/pallas_call | solution.py:203
  486.3 9.5 %collective-permute-done.48.refs_15_ = bf16[768,256]{1,0:T(8,128)(2,1)} collective-permute-done((bf16[768,256]{1,0:T(8,128)(2,1)S(1)}, bf16[768,256]{1,0:T(8,128)(2,1)}, u32[]{:S(2)}, u32[]{:S(2)}) %collective-permute-start.48) | collective-permute-done | bytes 393248 | tf_op jit(solution)/shard_map/ppermute | solution.py:316
  526.0 8.8 %collective-permute-done.61.refs_25_ = bf16[768,256]{1,0:T(8,128)(2,1)S(1)} collective-permute-done((bf16[768,256]{1,0:T(8,128)(2,1)S(1)}, bf16[768,256]{1,0:T(8,128)(2,1)S(1)}, u32[]{:S(2)}, u32[]{:S(2)}) %collective-permute-start.61) | collective-permute-done | bytes 393248 | tf_op jit(solution)/shard_map/ppermute | solution.py:319
  535.6 17.0 %collective-permute-done.38.refs_11_ = bf16[512,1280]{1,0:T(8,128)(2,1)S(1)} collective-permute-done((bf16[512,1280]{1,0:T(8,128)(2,1)S(1)}, bf16[512,1280]{1,0:T(8,128)(2,1)S(1)}, u32[]{:S(2)}, u32[]{:S(2)}) %collective-permute-start.38) | collective-permute-done | bytes 1310752 | tf_op jit(solution)/shard_map/ppermute | solution.py:316
  554.9 25.5 %collective-permute-done.40.refs_13_ = bf16[512,1280]{1,0:T(8,128)(2,1)} collective-permute-done((bf16[512,1280]{1,0:T(8,128)(2,1)S(1)}, bf16[512,1280]{1,0:T(8,128)(2,1)}, u32[]{:S(2)}, u32[]{:S(2)}) %collective-permute-start.40) | collective-permute-done | bytes 1310752 | tf_op jit(solution)/shard_map/ppermute | solution.py:316
  580.4 17.7 %project.1 = bf16[768,1280]{1,0:T(8,128)(2,1)} custom-call(s32[2]{0:T(128)} %pad_add_fusion.2.where_ref, s32[16]{0:T(128)} %stack.235.at_ref, bf16[768,1280]{1,0:T(8,128)(2,1)} %hidden_ref.1, bf16[768,1280]{1,0:T(8,128)(2,1)} %convolution_convert_fusion.gate_ref, bf16[512,1280]{1,0:T(8,128)(2,1)} %copy-done.16, bf16[512,1280]{1,0:T(8,128)(2,1)} %copy-done.21, ...), custom_call_target="tpu_custom_call" | custom-call | flops 8053063680 | bytes 22675456 | tf_op jit(solution)/shard_map/project/pallas_call | solution.py:277
  (307 shorter events, 180.3 us)
Async XLA Ops:
  72.9 48.8 %collective-permute-start.17 = (bf16[1280,768]{1,0:T(8,128)(2,1)}, bf16[1280,768]{1,0:T(8,128)(2,1)}, u32[]{:S(2)}, u32[]{:S(2)}) collective-permute-start(bf16[1280,768]{1,0:T(8,128)(2,1)} %maximum_select_fusion.refs_18_), channel_id=1, source_target_pairs={{0,8},{4,12},{8,16},{12,20},{16,24},{20,28},{1,9},{5,13},{9,17},{1... | collective-permute-start | bytes 5898248 | tf_op jit(solution)/shard_map/ppermute | solution.py:323
  119.2 51.4 %collective-permute-start.31 = (bf16[1280,768]{1,0:T(8,128)(2,1)}, bf16[1280,768]{1,0:T(8,128)(2,1)}, u32[]{:S(2)}, u32[]{:S(2)}) collective-permute-start(bf16[1280,768]{1,0:T(8,128)(2,1)} %maximum_select_fusion.1.refs_18_), channel_id=1, source_target_pairs={{8,0},{12,4},{16,8},{20,12},{24,16},{28,20},{9,1},{13,5},{17,9},{2... | collective-permute-start | bytes 5898248 | tf_op jit(solution)/shard_map/ppermute | solution.py:323
  128.1 68.6 %collective-permute-start.19 = (bf16[1280,768]{1,0:T(8,128)(2,1)}, bf16[1280,768]{1,0:T(8,128)(2,1)}, u32[]{:S(2)}, u32[]{:S(2)}) collective-permute-start(bf16[1280,768]{1,0:T(8,128)(2,1)} %collective-permute-done.17.refs_17_), channel_id=1, source_target_pairs={{8,16},{12,20},{16,24},{20,28},{9,17},{13,21},{17,25},{21,29},{10,... | collective-permute-start | bytes 5898248 | tf_op jit(solution)/shard_map/ppermute | solution.py:323
  130.1 82.2 %collective-permute-start.20 = (bf16[1280,768]{1,0:T(8,128)(2,1)}, bf16[1280,768]{1,0:T(8,128)(2,1)}, u32[]{:S(2)}, u32[]{:S(2)}) collective-permute-start(bf16[1280,768]{1,0:T(8,128)(2,1)} %collective-permute-done.18.refs_19_), channel_id=1, source_target_pairs={{8,0},{12,4},{16,8},{20,12},{9,1},{13,5},{17,9},{21,13},{10,2},{14... | collective-permute-start | bytes 5898248 | tf_op jit(solution)/shard_map/ppermute | solution.py:323
  176.1 54.9 %collective-permute-start.42 = (bf16[3,256,1024]{2,1,0:T(8,128)(2,1)}, bf16[3,256,1024]{2,1,0:T(8,128)(2,1)S(1)}, u32[]{:S(2)}, u32[]{:S(2)}) collective-permute-start(bf16[3,256,1024]{2,1,0:T(8,128)(2,1)} %pad_maximum_fusion.2), channel_id=1, source_target_pairs={{0,8},{4,12},{1,9},{5,13},{2,10},{6,14},{3,11},{7,15}} | collective-permute-start | bytes 4718600 | tf_op jit(solution)/shard_map/ppermute | solution.py:323
  182.5 49.9 %collective-permute-start.43 = (bf16[3,256,1024]{2,1,0:T(8,128)(2,1)}, bf16[3,256,1024]{2,1,0:T(8,128)(2,1)}, u32[]{:S(2)}, u32[]{:S(2)}) collective-permute-start(bf16[3,256,1024]{2,1,0:T(8,128)(2,1)} %pad_maximum_fusion.3), channel_id=1, source_target_pairs={{24,16},{28,20},{25,17},{29,21},{26,18},{30,22},{27,19},{31,23}} | collective-permute-start | bytes 4718600 | tf_op jit(solution)/shard_map/ppermute | solution.py:323
  196.8 57.7 %collective-permute-start.33 = (bf16[1280,768]{1,0:T(8,128)(2,1)}, bf16[1280,768]{1,0:T(8,128)(2,1)}, u32[]{:S(2)}, u32[]{:S(2)}) collective-permute-start(bf16[1280,768]{1,0:T(8,128)(2,1)} %collective-permute-done.31.refs_19_), channel_id=1, source_target_pairs={{8,0},{12,4},{16,8},{20,12},{9,1},{13,5},{17,9},{21,13},{10,2},{14... | collective-permute-start | bytes 5898248 | tf_op jit(solution)/shard_map/ppermute | solution.py:323
  212.3 65.5 %collective-permute-start.21 = (bf16[1280,768]{1,0:T(8,128)(2,1)}, bf16[1280,768]{1,0:T(8,128)(2,1)S(1)}, u32[]{:S(2)}, u32[]{:S(2)}) collective-permute-start(bf16[1280,768]{1,0:T(8,128)(2,1)} %collective-permute-done.19.refs_16_), channel_id=1, source_target_pairs={{16,24},{20,28},{17,25},{21,29},{18,26},{22,30},{19,27},{23,31}} | collective-permute-start | bytes 5898248 | tf_op jit(solution)/shard_map/ppermute | solution.py:323
  231.0 62.9 %collective-permute-start.22 = (bf16[1280,768]{1,0:T(8,128)(2,1)}, bf16[1280,768]{1,0:T(8,128)(2,1)S(1)}, u32[]{:S(2)}, u32[]{:S(2)}) collective-permute-start(bf16[1280,768]{1,0:T(8,128)(2,1)} %collective-permute-done.20.refs_20_), channel_id=1, source_target_pairs={{8,0},{12,4},{9,1},{13,5},{10,2},{14,6},{11,3},{15,7}} | collective-permute-start | bytes 5898248 | tf_op jit(solution)/shard_map/ppermute | solution.py:323
  254.4 58.4 %collective-permute-start.36 = (bf16[512,1280]{1,0:T(8,128)(2,1)}, bf16[512,1280]{1,0:T(8,128)(2,1)}, u32[]{:S(2)}, u32[]{:S(2)}) collective-permute-start(bf16[512,1280]{1,0:T(8,128)(2,1)} %collective-permute-done.1.refs_8_), channel_id=1, source_target_pairs={{0,4},{4,0},{8,12},{12,8},{16,20},{20,16},{1,5},{5,1},{9,13},{13,9... | collective-permute-start | bytes 3932168 | tf_op jit(solution)/shard_map/ppermute | solution.py:316
  256.4 50.7 %collective-permute-start.44 = (bf16[3,256,1024]{2,1,0:T(8,128)(2,1)}, bf16[3,256,1024]{2,1,0:T(8,128)(2,1)}, u32[]{:S(2)}, u32[]{:S(2)}) collective-permute-start(bf16[3,256,1024]{2,1,0:T(8,128)(2,1)} %pad_maximum_fusion.4), channel_id=1, source_target_pairs={{8,16},{12,20},{9,17},{13,21},{10,18},{14,22},{11,19},{15,23}} | collective-permute-start | bytes 4718600 | tf_op jit(solution)/shard_map/ppermute | solution.py:323
  258.2 49.4 %collective-permute-start.45 = (bf16[3,256,1024]{2,1,0:T(8,128)(2,1)}, bf16[3,256,1024]{2,1,0:T(8,128)(2,1)}, u32[]{:S(2)}, u32[]{:S(2)}) collective-permute-start(bf16[3,256,1024]{2,1,0:T(8,128)(2,1)} %pad_maximum_fusion.5), channel_id=1, source_target_pairs={{16,8},{20,12},{17,9},{21,13},{18,10},{22,14},{19,11},{23,15}} | collective-permute-start | bytes 4718600 | tf_op jit(solution)/shard_map/ppermute | solution.py:323
  277.8 62.2 %collective-permute-start.55 = (bf16[1280,768]{1,0:T(8,128)(2,1)}, bf16[1280,768]{1,0:T(8,128)(2,1)}, u32[]{:S(2)}, u32[]{:S(2)}) collective-permute-start(bf16[1280,768]{1,0:T(8,128)(2,1)} %collective-permute-done.32.refs_16_), channel_id=1, source_target_pairs={{16,24},{20,28},{17,25},{21,29},{18,26},{22,30},{19,27},{23,31}} | collective-permute-start | bytes 5898248 | tf_op jit(solution)/shard_map/ppermute | solution.py:323
  293.8 47.5 %collective-permute-start.56 = (bf16[1280,768]{1,0:T(8,128)(2,1)}, bf16[1280,768]{1,0:T(8,128)(2,1)}, u32[]{:S(2)}, u32[]{:S(2)}) collective-permute-start(bf16[1280,768]{1,0:T(8,128)(2,1)} %collective-permute-done.33.refs_20_), channel_id=1, source_target_pairs={{8,0},{12,4},{9,1},{13,5},{10,2},{14,6},{11,3},{15,7}} | collective-permute-start | bytes 5898248 | tf_op jit(solution)/shard_map/ppermute | solution.py:323
  312.9 79.8 %collective-permute-start.46 = (bf16[3,256,1024]{2,1,0:T(8,128)(2,1)}, bf16[3,256,1024]{2,1,0:T(8,128)(2,1)S(1)}, u32[]{:S(2)}, u32[]{:S(2)}) collective-permute-start(bf16[3,256,1024]{2,1,0:T(8,128)(2,1)} %pad_maximum_fusion.6), channel_id=1, source_target_pairs={{16,24},{20,28},{17,25},{21,29},{18,26},{22,30},{19,27},{23,31}} | collective-permute-start | bytes 4718600 | tf_op jit(solution)/shard_map/ppermute | solution.py:323
  335.4 59.1 %collective-permute-start.47 = (bf16[3,256,1024]{2,1,0:T(8,128)(2,1)}, bf16[3,256,1024]{2,1,0:T(8,128)(2,1)}, u32[]{:S(2)}, u32[]{:S(2)}) collective-permute-start(bf16[3,256,1024]{2,1,0:T(8,128)(2,1)} %pad_maximum_fusion.7), channel_id=1, source_target_pairs={{8,0},{12,4},{9,1},{13,5},{10,2},{14,6},{11,3},{15,7}} | collective-permute-start | bytes 4718600 | tf_op jit(solution)/shard_map/ppermute | solution.py:323
  337.6 146.5 %collective-permute-start.66 = (bf16[768,512]{1,0:T(8,128)(2,1)}, bf16[768,512]{1,0:T(8,128)(2,1)S(1)}, u32[]{:S(2)}, u32[]{:S(2)}) collective-permute-start(bf16[768,512]{1,0:T(8,128)(2,1)} %pad_maximum_fusion.8), channel_id=1, source_target_pairs={{0,4},{4,0},{8,12},{12,8},{16,20},{20,16},{24,28},{28,24},{1,5},{5... | collective-permute-start | bytes 2359304 | tf_op jit(solution)/shard_map/ppermute | solution.py:316
  340.0 46.7 %collective-permute-start.24 = (bf16[672,512]{1,0:T(8,128)(2,1)}, bf16[672,512]{1,0:T(8,128)(2,1)}, u32[]{:S(2)}, u32[]{:S(2)}) collective-permute-start(bf16[672,512]{1,0:T(8,128)(2,1)} %pad_maximum_fusion.11), channel_id=1, source_target_pairs={{8,0},{12,4},{16,8},{20,12},{24,16},{28,20},{9,1},{13,5},{17,9},{2... | collective-permute-start | bytes 2064392 | tf_op jit(solution)/shard_map/ppermute | solution.py:323
  392.6 51.1 %collective-permute-start.25 = (bf16[512,1280]{1,0:T(8,128)(2,1)}, bf16[512,1280]{1,0:T(8,128)(2,1)}, u32[]{:S(2)}, u32[]{:S(2)}) collective-permute-start(bf16[512,1280]{1,0:T(8,128)(2,1)} %collective-permute-done.refs_4_), channel_id=1, source_target_pairs={{8,16},{12,20},{16,24},{20,28},{9,17},{13,21},{17,25},{21,29},{10,... | collective-permute-start | bytes 3932168 | tf_op jit(solution)/shard_map/ppermute | solution.py:323
  394.5 49.9 %collective-permute-start.37 = (bf16[512,1280]{1,0:T(8,128)(2,1)}, bf16[512,1280]{1,0:T(8,128)(2,1)S(1)}, u32[]{:S(2)}, u32[]{:S(2)}) collective-permute-start(bf16[512,1280]{1,0:T(8,128)(2,1)} %collective-permute-done.1.refs_8_), channel_id=1, source_target_pairs={{8,0},{12,4},{16,8},{20,12},{9,1},{13,5},{17,9},{21,13},{10,2},{14... | collective-permute-start | bytes 3932168 | tf_op jit(solution)/shard_map/ppermute | solution.py:323
  407.0 77.2 %collective-permute-start.67 = (bf16[768,512]{1,0:T(8,128)(2,1)}, bf16[768,512]{1,0:T(8,128)(2,1)S(1)}, u32[]{:S(2)}, u32[]{:S(2)}) collective-permute-start(bf16[768,512]{1,0:T(8,128)(2,1)} %pad_maximum_fusion.9), channel_id=1, source_target_pairs={{0,4},{4,0},{8,12},{12,8},{16,20},{20,16},{24,28},{28,24},{1,5},{5... | collective-permute-start | bytes 2359304 | tf_op jit(solution)/shard_map/ppermute | solution.py:316
  443.7 63.1 %collective-permute-start.26 = (bf16[512,1280]{1,0:T(8,128)(2,1)}, bf16[512,1280]{1,0:T(8,128)(2,1)S(1)}, u32[]{:S(2)}, u32[]{:S(2)}) collective-permute-start(bf16[512,1280]{1,0:T(8,128)(2,1)} %collective-permute-done.25.refs_2_), channel_id=1, source_target_pairs={{16,24},{20,28},{17,25},{21,29},{18,26},{22,30},{19,27},{23,31}} | collective-permute-start | bytes 3932168 | tf_op jit(solution)/shard_map/ppermute | solution.py:323
  444.4 62.9 %collective-permute-start.39 = (bf16[512,1280]{1,0:T(8,128)(2,1)S(1)}, bf16[512,1280]{1,0:T(8,128)(2,1)S(1)}, u32[]{:S(2)}, u32[]{:S(2)}) collective-permute-start(bf16[512,1280]{1,0:T(8,128)(2,1)S(1)} %collective-permute-done.37.refs_10_), channel_id=1, source_target_pairs={{8,0},{12,4},{9,1},{13,5},{10,2},{14,6},{11,3},{15,7}} | collective-permute-start | bytes 3932168 | tf_op jit(solution)/shard_map/ppermute | solution.py:323
  517.9 62.5 %collective-permute-start.40 = (bf16[512,1280]{1,0:T(8,128)(2,1)S(1)}, bf16[512,1280]{1,0:T(8,128)(2,1)}, u32[]{:S(2)}, u32[]{:S(2)}) collective-permute-start(bf16[512,1280]{1,0:T(8,128)(2,1)S(1)} %copy-done.19), channel_id=1, source_target_pairs={{0,4},{4,0},{1,5},{5,1},{2,6},{6,2},{3,7},{7,3}} | collective-permute-start | bytes 3932168 | tf_op jit(solution)/shard_map/ppermute | solution.py:316
  (81 other events, 1849.9 us)

commit v3 on v2

--- a/solution.py
+++ b/solution.py
@@ -482,7 +482,7 @@
     ]
     keys = jnp.zeros((tokens, local_heads * HD), jnp.bfloat16)
     values = keys
-    attended, attended_at = [], []
+    attended, attended_at, later_out = [], [], []
     for part in range(parts):
         hc = counts[part]
         behind = [v for pair in first_out for v in pair] if part == parts - 1 else []
@@ -499,6 +499,7 @@
         if part == 0:
             for step in range(2, planes):
                 out_steps.append(line_step(out_steps[-1], step, (low, high) if step == 2 else ()))
+                later_out.append([halves(out_steps[-1][0], -step), halves(out_steps[-1][1], step)])
         own_kv = kv_of(x * tokens, tokens)
         other_kv = swap_x(kv_of((1 - x) * tokens, tokens))
         for xb, v in ((0, own_kv), (1, other_kv)):
@@ -512,7 +513,9 @@
         part_prefix = prefix[:, :, firsts[part] * 2 * HD : (firsts[part] + hc) * 2 * HD]
         out = attention_call(need, qkv, low, high, part_prefix, qtag, ktag)
         pieces = [(lax.dynamic_slice_in_dim(out, x * tokens, tokens, 0), 0, 0)]
-        behind = out_steps[-1] if part == parts - 1 else out_steps[1]
+        behind = out_steps[1]
+        if part == parts - 1:
+            behind = [*out_steps[-1], *(piece for pairs in later_out[:-1] for _, piece in pairs)]
         other = lax.dynamic_slice_in_dim(out, (1 - x) * tokens, tokens, 0)
         pieces.append((swap_x(after(other, behind)), 1, 0))
         for bit in col_bits:
@@ -522,9 +525,8 @@
             attended_at.append((c ^ cb) * local_heads + (x ^ xb) * heads + firsts[part])
 
     out_pairs = first_out
-    for step in range(2, planes):
-        low, high = out_steps[step - 1]
-        out_pairs = [halves(low, -step)] + out_pairs + [halves(high, step)]
+    for low, high in later_out:
+        out_pairs = [low] + out_pairs + [high]
     out_pieces = [piece for pair in out_pairs for piece in pair]
     hidden_out = out_call(
         jnp.stack([z, x]), jnp.stack(attended_at), attended, hidden_in, gate.astype(jnp.bfloat16), out_pieces

time: 606 us -> 591 us (0.975)
  waiting for transfers between devices: 242 us -> 230 us
    ppermute x17, waiting for transfers between devices: 149 us -> 106 us  [swap_x(): lax.ppermute(v, 'row', [(i, i ^ 1) for i in range(rows_n) if valid(i // 2)])]
    ppermute x28, waiting for transfers between devices: 79.6 us -> 104 us  [z_move(): return lax.ppermute(v, 'row', pairs)]
  transfers between devices with their start and end apart: 68 -> 68, of which waited for: 20 -> 21; matrix products, arithmetic and copies ran while one was open for 10% -> 10% of each run, Pallas kernels for 21% -> 20%
where the time goes in v3:
time: 591 us; the launch traced here: 583 us
  waiting for transfers between devices  230 us (39%)
  Pallas kernels  137 us (23%)
  starting transfers between devices  125 us (21%)
  other arithmetic  31.8 us (5%)
  local copies, waits for them, and re-layouts  29.2 us (5%)
  between operations  20.4 us (3%)
    ppermute x17, waiting for transfers between devices, swap_x(): lax.ppermute(v, 'row', [(i, i ^ 1) for i in range(rows_n) if valid(i // 2)])  106 us
    ppermute x28, waiting for transfers between devices, z_move(): return lax.ppermute(v, 'row', pairs)  104 us
    ppermute x28, starting transfers between devices, z_move(): return lax.ppermute(v, 'row', pairs)  86.1 us
    pallas_call x2, Pallas kernels, attention_call(): pl.pallas_call(functools.partial(attention_kernel, heads, groups), out_sh...  64.2 us
    pallas_call x4, Pallas kernels, qkv_call(): pl.pallas_call(functools.partial(qkv_kernel, planes, len(blocks), finish)...  54.9 us
    ppermute x17, starting transfers between devices, swap_x(): lax.ppermute(v, 'row', [(i, i ^ 1) for i in range(rows_n) if valid(i // 2)])  25 us
    ppermute x23, waiting for transfers between devices, swap_col(): return lax.ppermute(v, 'col', [(i, i ^ bit) for i in range(cols_n)])  20.1 us
    pallas_call x1, Pallas kernels, out_call(): pl.pallas_call(functools.partial(out_kernel, planes, len(columns)), out_s...  17.7 us
  transfers between devices with their start and end apart: 68, of which 21 were waited for; matrix products, arithmetic and copies ran while one was open for 10% of the time, Pallas kernels for 20%

profile of v3, /device:TPU:0, one launch (start us, length us, event | category | flops | bytes accessed | tf_op | source)
XLA Modules:
  0.0 582.8 jit_solution(3165796159077558645)
XLA Ops:
  24.4 6.3 %collective-permute-done.16 = bf16[640,768]{1,0:T(8,128)(2,1)} collective-permute-done((bf16[640,768]{1,0:T(8,128)(2,1)}, bf16[640,768]{1,0:T(8,128)(2,1)}, u32[]{:S(2)}, u32[]{:S(2)}) %collective-permute-start.16) | collective-permute-done | bytes 983072 | tf_op jit(solution)/shard_map/ppermute | solution.py:316
  32.8 18.9 %collective-permute-done.2.refs_1_ = bf16[384,1280]{1,0:T(8,128)(2,1)S(1)} collective-permute-done((bf16[384,1280]{1,0:T(8,128)(2,1)S(1)}, bf16[384,1280]{1,0:T(8,128)(2,1)S(1)}, u32[]{:S(2)}, u32[]{:S(2)}) %collective-permute-start.2) | collective-permute-done | bytes 983072 | tf_op jit(solution)/shard_map/ppermute | solution.py:316
  59.8 13.1 %collective-permute-done.10.refs_10_ = bf16[384,1280]{1,0:T(8,128)(2,1)} collective-permute-done((bf16[384,1280]{1,0:T(8,128)(2,1)S(1)}, bf16[384,1280]{1,0:T(8,128)(2,1)}, u32[]{:S(2)}, u32[]{:S(2)}) %collective-permute-start.10) | collective-permute-done | bytes 983072 | tf_op jit(solution)/shard_map/ppermute | solution.py:316
  82.8 11.1 %collective-permute-done.29 = bf16[640,768]{1,0:T(8,128)(2,1)} collective-permute-done((bf16[640,768]{1,0:T(8,128)(2,1)}, bf16[640,768]{1,0:T(8,128)(2,1)}, u32[]{:S(2)}, u32[]{:S(2)}) %collective-permute-start.29) | collective-permute-done | bytes 983072 | tf_op jit(solution)/shard_map/ppermute | solution.py:316
  98.0 16.1 %collective-permute-done.11.refs_11_ = bf16[384,1280]{1,0:T(8,128)(2,1)} collective-permute-done((bf16[384,1280]{1,0:T(8,128)(2,1)}, bf16[384,1280]{1,0:T(8,128)(2,1)}, u32[]{:S(2)}, u32[]{:S(2)}) %collective-permute-start.11) | collective-permute-done | bytes 983072 | tf_op jit(solution)/shard_map/ppermute | solution.py:316
  131.4 7.4 %collective-permute-done.41 = bf16[256,1024]{1,0:T(8,128)(2,1)} collective-permute-done((bf16[256,1024]{1,0:T(8,128)(2,1)S(1)}, bf16[256,1024]{1,0:T(8,128)(2,1)}, u32[]{:S(2)}, u32[]{:S(2)}) %collective-permute-start.41) | collective-permute-done | bytes 524320 | tf_op jit(solution)/shard_map/ppermute | solution.py:316
  140.0 19.5 %collective-permute-done.30.refs_17_ = bf16[1280,768]{1,0:T(8,128)(2,1)} collective-permute-done((bf16[1280,768]{1,0:T(8,128)(2,1)}, bf16[1280,768]{1,0:T(8,128)(2,1)}, u32[]{:S(2)}, u32[]{:S(2)}) %collective-permute-start.30) | collective-permute-done | bytes 1966112 | tf_op jit(solution)/shard_map/ppermute | solution.py:323
  198.1 14.2 %collective-permute-done.20.refs_20_ = bf16[1280,768]{1,0:T(8,128)(2,1)} collective-permute-done((bf16[1280,768]{1,0:T(8,128)(2,1)}, bf16[1280,768]{1,0:T(8,128)(2,1)}, u32[]{:S(2)}, u32[]{:S(2)}) %collective-permute-start.20) | collective-permute-done | bytes 1966112 | tf_op jit(solution)/shard_map/ppermute | solution.py:323
  213.3 17.7 %qkv_start.2.refs_18_ = f32[1536,768]{1,0:T(8,128)} custom-call(s32[1]{0:T(128)} %bitcast.z_ref, s32[16,2]{1,0:T(8,128)} %stack.276.at_ref, bf16[384,1280]{1,0:T(8,128)(2,1)} %copy-done.3, bf16[384,1280]{1,0:T(8,128)(2,1)} %copy-done.4, bf16[384,1280]{1,0:T(8,128)(2,1)} %collective-permute-done.3.refs_2_, bf16[384,1280]{1,0:T(8,128)(2,1)} %collective-permute-done.4.refs_3_, ...), custom_call_target="tpu_custom_call" | custom-call | flops 12079595520 | bytes 25952256 | tf_op jit(solution)/shard_map/qkv_start/pallas_call | solution.py:112
  236.5 17.9 %collective-permute-done.33.refs_20_ = bf16[1280,768]{1,0:T(8,128)(2,1)} collective-permute-done((bf16[1280,768]{1,0:T(8,128)(2,1)}, bf16[1280,768]{1,0:T(8,128)(2,1)}, u32[]{:S(2)}, u32[]{:S(2)}) %collective-permute-start.33) | collective-permute-done | bytes 1966112 | tf_op jit(solution)/shard_map/ppermute | solution.py:323
  260.0 17.8 %qkv_start.3.refs_18_ = f32[1536,768]{1,0:T(8,128)} custom-call(s32[1]{0:T(128)} %bitcast.z_ref, s32[16,2]{1,0:T(8,128)} %stack.276.at_ref, bf16[384,1280]{1,0:T(8,128)(2,1)} %copy-done.3, bf16[384,1280]{1,0:T(8,128)(2,1)} %copy-done.4, bf16[384,1280]{1,0:T(8,128)(2,1)} %collective-permute-done.3.refs_2_, bf16[384,1280]{1,0:T(8,128)(2,1)} %collective-permute-done.4.refs_3_, ...), custom_call_target="tpu_custom_call" | custom-call | flops 12079595520 | bytes 25952256 | tf_op jit(solution)/shard_map/qkv_start/pallas_call | solution.py:112
  279.7 14.1 %collective-permute-done.22.refs_17_ = bf16[1280,768]{1,0:T(8,128)(2,1)S(1)} collective-permute-done((bf16[1280,768]{1,0:T(8,128)(2,1)}, bf16[1280,768]{1,0:T(8,128)(2,1)S(1)}, u32[]{:S(2)}, u32[]{:S(2)}) %collective-permute-start.22) | collective-permute-done | bytes 1966112 | tf_op jit(solution)/shard_map/ppermute | solution.py:323
  295.2 9.7 %qkv_end.2.q_ref.own_ref = bf16[1536,768]{1,0:T(8,128)(2,1)} custom-call(s32[1]{0:T(128)} %bitcast.z_ref, s32[16,2]{1,0:T(8,128)} %stack.276.at_ref, bf16[384,1280]{1,0:T(8,128)(2,1)} %copy-done.3, bf16[384,1280]{1,0:T(8,128)(2,1)} %copy-done.4, bf16[384,1280]{1,0:T(8,128)(2,1)} %collective-permute-done.3.refs_2_, ...), custom_call_target="tpu_custom_call" | custom-call | flops 3019898880 | bytes 25952256 | tf_op jit(solution)/shard_map/qkv_end/pallas_call | solution.py:112
  313.1 21.5 %collective-permute-done.35.refs_7_ = bf16[512,1280]{1,0:T(8,128)(2,1)S(1)} collective-permute-done((bf16[512,1280]{1,0:T(8,128)(2,1)}, bf16[512,1280]{1,0:T(8,128)(2,1)S(1)}, u32[]{:S(2)}, u32[]{:S(2)}) %collective-permute-start.35) | collective-permute-done | bytes 1310752 | tf_op jit(solution)/shard_map/ppermute | solution.py:316
  340.5 28.7 %collective-permute-start.23 = (bf16[672,512]{1,0:T(8,128)(2,1)}, bf16[672,512]{1,0:T(8,128)(2,1)}, u32[]{:S(2)}, u32[]{:S(2)}) collective-permute-start(bf16[672,512]{1,0:T(8,128)(2,1)} %pad_maximum_fusion.10), channel_id=1, source_target_pairs={{0,8},{4,12},{8,16},{12,20},{16,24},{20,28},{1,9},{5,13},{9,17},{1... | collective-permute-start | bytes 2064392 | tf_op jit(solution)/shard_map/ppermute | solution.py:323
  369.2 9.7 %qkv_end.3.q_ref.own_ref = bf16[1536,768]{1,0:T(8,128)(2,1)} custom-call(s32[1]{0:T(128)} %bitcast.z_ref, s32[16,2]{1,0:T(8,128)} %stack.276.at_ref, bf16[384,1280]{1,0:T(8,128)(2,1)} %copy-done.3, bf16[384,1280]{1,0:T(8,128)(2,1)} %copy-done.4, bf16[384,1280]{1,0:T(8,128)(2,1)} %collective-permute-done.3.refs_2_, ...), custom_call_target="tpu_custom_call" | custom-call | flops 3019898880 | bytes 25952256 | tf_op jit(solution)/shard_map/qkv_end/pallas_call | solution.py:112
  392.2 6.0 %collective-permute-start.57 = (bf16[672,512]{1,0:T(8,128)(2,1)S(1)}, bf16[672,512]{1,0:T(8,128)(2,1)S(1)}, u32[]{:S(2)}, u32[]{:S(2)}) collective-permute-start(bf16[672,512]{1,0:T(8,128)(2,1)S(1)} %pad_maximum_fusion.12), channel_id=1, source_target_pairs={{0,8},{4,12},{8,16},{12,20},{16,24},{20,28},{1,9},{5,13},{9,17},{1... | collective-permute-start | bytes 2064392 | tf_op jit(solution)/shard_map/ppermute | solution.py:323
  402.3 29.2 %collective-permute-done.37.refs_10_ = bf16[512,1280]{1,0:T(8,128)(2,1)} collective-permute-done((bf16[512,1280]{1,0:T(8,128)(2,1)}, bf16[512,1280]{1,0:T(8,128)(2,1)}, u32[]{:S(2)}, u32[]{:S(2)}) %collective-permute-start.37) | collective-permute-done | bytes 1310752 | tf_op jit(solution)/shard_map/ppermute | solution.py:323
  439.3 32.1 %attention.3 = bf16[1536,256]{1,0:T(8,128)(2,1)} custom-call(s32[6,16]{1,0:T(8,128)} %add_convert_fusion.need_ref, bf16[1536,768]{1,0:T(8,128)(2,1)} %qkv_end.3.q_ref.own_ref, bf16[1536,768]{1,0:T(8,128)(2,1)} %qkv_end.3.q_ref.own_ref, bf16[672,512]{1,0:T(8,128)(2,1)} %copy-done.36, bf16[672,512]{1,0:T(8,128)(2,1)} %copy-done.35, ...), custom_call_target="tpu_custom_call" | custom-call | flops 3221225472 | bytes 6291456 | tf_op jit(solution)/shard_map/attention/pallas_call | solution.py:203
  473.3 32.1 %attention.2 = bf16[1536,256]{1,0:T(8,128)(2,1)} custom-call(s32[6,16]{1,0:T(8,128)} %add_convert_fusion.need_ref, bf16[1536,768]{1,0:T(8,128)(2,1)} %qkv_end.2.q_ref.own_ref, bf16[1536,768]{1,0:T(8,128)(2,1)} %qkv_end.2.q_ref.own_ref, bf16[672,512]{1,0:T(8,128)(2,1)} %collective-permute-done.23.low_ref, bf16[672,512]{1,0:T(8,128)(2,1)} %collective-permute-done.24.high_ref, ...), custom_call_target="tpu_custom_call" | custom-call | flops 3221225472 | bytes 6291456 | tf_op jit(solution)/shard_map/attention/pallas_call | solution.py:203
  538.0 5.9 %collective-permute-done.50.refs_17_ = bf16[768,256]{1,0:T(8,128)(2,1)S(1)} collective-permute-done((bf16[768,256]{1,0:T(8,128)(2,1)}, bf16[768,256]{1,0:T(8,128)(2,1)S(1)}, u32[]{:S(2)}, u32[]{:S(2)}) %collective-permute-start.50) | collective-permute-done | bytes 393248 | tf_op jit(solution)/shard_map/ppermute | solution.py:319
  544.5 7.1 %collective-permute-done.61.refs_25_ = bf16[768,256]{1,0:T(8,128)(2,1)S(1)} collective-permute-done((bf16[768,256]{1,0:T(8,128)(2,1)S(1)}, bf16[768,256]{1,0:T(8,128)(2,1)S(1)}, u32[]{:S(2)}, u32[]{:S(2)}) %collective-permute-start.61) | collective-permute-done | bytes 393248 | tf_op jit(solution)/shard_map/ppermute | solution.py:319
  554.0 9.6 %collective-permute-done.40.refs_13_ = bf16[512,1280]{1,0:T(8,128)(2,1)S(1)} collective-permute-done((bf16[512,1280]{1,0:T(8,128)(2,1)}, bf16[512,1280]{1,0:T(8,128)(2,1)S(1)}, u32[]{:S(2)}, u32[]{:S(2)}) %collective-permute-start.40) | collective-permute-done | bytes 1310752 | tf_op jit(solution)/shard_map/ppermute | solution.py:316
  564.6 17.7 %project.1 = bf16[768,1280]{1,0:T(8,128)(2,1)} custom-call(s32[2]{0:T(128)} %pad_add_fusion.2.where_ref, s32[16]{0:T(128)} %stack.235.at_ref, bf16[768,1280]{1,0:T(8,128)(2,1)} %hidden_ref.1, bf16[768,1280]{1,0:T(8,128)(2,1)} %convolution_convert_fusion.gate_ref, bf16[512,1280]{1,0:T(8,128)(2,1)} %copy-done.15, bf16[512,1280]{1,0:T(8,128)(2,1)} %copy-done.17, ...), custom_call_target="tpu_custom_call" | custom-call | flops 8053063680 | bytes 22675456 | tf_op jit(solution)/shard_map/project/pallas_call | solution.py:277
  (307 shorter events, 179.0 us)
Async XLA Ops:
  72.9 48.8 %collective-permute-start.17 = (bf16[1280,768]{1,0:T(8,128)(2,1)}, bf16[1280,768]{1,0:T(8,128)(2,1)}, u32[]{:S(2)}, u32[]{:S(2)}) collective-permute-start(bf16[1280,768]{1,0:T(8,128)(2,1)} %maximum_select_fusion.refs_18_), channel_id=1, source_target_pairs={{0,8},{4,12},{8,16},{12,20},{16,24},{20,28},{1,9},{5,13},{9,17},{1... | collective-permute-start | bytes 5898248 | tf_op jit(solution)/shard_map/ppermute | solution.py:323
  119.2 51.4 %collective-permute-start.31 = (bf16[1280,768]{1,0:T(8,128)(2,1)}, bf16[1280,768]{1,0:T(8,128)(2,1)}, u32[]{:S(2)}, u32[]{:S(2)}) collective-permute-start(bf16[1280,768]{1,0:T(8,128)(2,1)} %maximum_select_fusion.1.refs_18_), channel_id=1, source_target_pairs={{8,0},{12,4},{16,8},{20,12},{24,16},{28,20},{9,1},{13,5},{17,9},{2... | collective-permute-start | bytes 5898248 | tf_op jit(solution)/shard_map/ppermute | solution.py:323
  128.1 68.6 %collective-permute-start.19 = (bf16[1280,768]{1,0:T(8,128)(2,1)}, bf16[1280,768]{1,0:T(8,128)(2,1)}, u32[]{:S(2)}, u32[]{:S(2)}) collective-permute-start(bf16[1280,768]{1,0:T(8,128)(2,1)} %collective-permute-done.17.refs_17_), channel_id=1, source_target_pairs={{8,16},{12,20},{16,24},{20,28},{9,17},{13,21},{17,25},{21,29},{10,... | collective-permute-start | bytes 5898248 | tf_op jit(solution)/shard_map/ppermute | solution.py:323
  130.1 82.2 %collective-permute-start.20 = (bf16[1280,768]{1,0:T(8,128)(2,1)}, bf16[1280,768]{1,0:T(8,128)(2,1)}, u32[]{:S(2)}, u32[]{:S(2)}) collective-permute-start(bf16[1280,768]{1,0:T(8,128)(2,1)} %collective-permute-done.18.refs_19_), channel_id=1, source_target_pairs={{8,0},{12,4},{16,8},{20,12},{9,1},{13,5},{17,9},{21,13},{10,2},{14... | collective-permute-start | bytes 5898248 | tf_op jit(solution)/shard_map/ppermute | solution.py:323
  176.1 54.9 %collective-permute-start.42 = (bf16[3,256,1024]{2,1,0:T(8,128)(2,1)}, bf16[3,256,1024]{2,1,0:T(8,128)(2,1)S(1)}, u32[]{:S(2)}, u32[]{:S(2)}) collective-permute-start(bf16[3,256,1024]{2,1,0:T(8,128)(2,1)} %pad_maximum_fusion.2), channel_id=1, source_target_pairs={{0,8},{4,12},{1,9},{5,13},{2,10},{6,14},{3,11},{7,15}} | collective-permute-start | bytes 4718600 | tf_op jit(solution)/shard_map/ppermute | solution.py:323
  182.5 49.9 %collective-permute-start.43 = (bf16[3,256,1024]{2,1,0:T(8,128)(2,1)}, bf16[3,256,1024]{2,1,0:T(8,128)(2,1)}, u32[]{:S(2)}, u32[]{:S(2)}) collective-permute-start(bf16[3,256,1024]{2,1,0:T(8,128)(2,1)} %pad_maximum_fusion.3), channel_id=1, source_target_pairs={{24,16},{28,20},{25,17},{29,21},{26,18},{30,22},{27,19},{31,23}} | collective-permute-start | bytes 4718600 | tf_op jit(solution)/shard_map/ppermute | solution.py:323
  196.8 57.7 %collective-permute-start.33 = (bf16[1280,768]{1,0:T(8,128)(2,1)}, bf16[1280,768]{1,0:T(8,128)(2,1)}, u32[]{:S(2)}, u32[]{:S(2)}) collective-permute-start(bf16[1280,768]{1,0:T(8,128)(2,1)} %collective-permute-done.31.refs_19_), channel_id=1, source_target_pairs={{8,0},{12,4},{16,8},{20,12},{9,1},{13,5},{17,9},{21,13},{10,2},{14... | collective-permute-start | bytes 5898248 | tf_op jit(solution)/shard_map/ppermute | solution.py:323
  212.3 65.5 %collective-permute-start.21 = (bf16[1280,768]{1,0:T(8,128)(2,1)}, bf16[1280,768]{1,0:T(8,128)(2,1)S(1)}, u32[]{:S(2)}, u32[]{:S(2)}) collective-permute-start(bf16[1280,768]{1,0:T(8,128)(2,1)} %collective-permute-done.19.refs_16_), channel_id=1, source_target_pairs={{16,24},{20,28},{17,25},{21,29},{18,26},{22,30},{19,27},{23,31}} | collective-permute-start | bytes 5898248 | tf_op jit(solution)/shard_map/ppermute | solution.py:323
  231.0 62.9 %collective-permute-start.22 = (bf16[1280,768]{1,0:T(8,128)(2,1)}, bf16[1280,768]{1,0:T(8,128)(2,1)S(1)}, u32[]{:S(2)}, u32[]{:S(2)}) collective-permute-start(bf16[1280,768]{1,0:T(8,128)(2,1)} %collective-permute-done.20.refs_20_), channel_id=1, source_target_pairs={{8,0},{12,4},{9,1},{13,5},{10,2},{14,6},{11,3},{15,7}} | collective-permute-start | bytes 5898248 | tf_op jit(solution)/shard_map/ppermute | solution.py:323
  254.4 57.6 %collective-permute-start.36 = (bf16[512,1280]{1,0:T(8,128)(2,1)}, bf16[512,1280]{1,0:T(8,128)(2,1)}, u32[]{:S(2)}, u32[]{:S(2)}) collective-permute-start(bf16[512,1280]{1,0:T(8,128)(2,1)} %collective-permute-done.1.refs_8_), channel_id=1, source_target_pairs={{0,4},{4,0},{8,12},{12,8},{16,20},{20,16},{1,5},{5,1},{9,13},{13,9... | collective-permute-start | bytes 3932168 | tf_op jit(solution)/shard_map/ppermute | solution.py:316
  256.4 49.8 %collective-permute-start.44 = (bf16[3,256,1024]{2,1,0:T(8,128)(2,1)}, bf16[3,256,1024]{2,1,0:T(8,128)(2,1)}, u32[]{:S(2)}, u32[]{:S(2)}) collective-permute-start(bf16[3,256,1024]{2,1,0:T(8,128)(2,1)} %pad_maximum_fusion.4), channel_id=1, source_target_pairs={{8,16},{12,20},{9,17},{13,21},{10,18},{14,22},{11,19},{15,23}} | collective-permute-start | bytes 4718600 | tf_op jit(solution)/shard_map/ppermute | solution.py:323
  258.2 48.6 %collective-permute-start.45 = (bf16[3,256,1024]{2,1,0:T(8,128)(2,1)}, bf16[3,256,1024]{2,1,0:T(8,128)(2,1)}, u32[]{:S(2)}, u32[]{:S(2)}) collective-permute-start(bf16[3,256,1024]{2,1,0:T(8,128)(2,1)} %pad_maximum_fusion.5), channel_id=1, source_target_pairs={{16,8},{20,12},{17,9},{21,13},{18,10},{22,14},{19,11},{23,15}} | collective-permute-start | bytes 4718600 | tf_op jit(solution)/shard_map/ppermute | solution.py:323
  277.8 61.4 %collective-permute-start.55 = (bf16[1280,768]{1,0:T(8,128)(2,1)}, bf16[1280,768]{1,0:T(8,128)(2,1)}, u32[]{:S(2)}, u32[]{:S(2)}) collective-permute-start(bf16[1280,768]{1,0:T(8,128)(2,1)} %collective-permute-done.32.refs_16_), channel_id=1, source_target_pairs={{16,24},{20,28},{17,25},{21,29},{18,26},{22,30},{19,27},{23,31}} | collective-permute-start | bytes 5898248 | tf_op jit(solution)/shard_map/ppermute | solution.py:323
  312.1 78.7 %collective-permute-start.46 = (bf16[3,256,1024]{2,1,0:T(8,128)(2,1)}, bf16[3,256,1024]{2,1,0:T(8,128)(2,1)S(1)}, u32[]{:S(2)}, u32[]{:S(2)}) collective-permute-start(bf16[3,256,1024]{2,1,0:T(8,128)(2,1)} %pad_maximum_fusion.6), channel_id=1, source_target_pairs={{16,24},{20,28},{17,25},{21,29},{18,26},{22,30},{19,27},{23,31}} | collective-permute-start | bytes 4718600 | tf_op jit(solution)/shard_map/ppermute | solution.py:323
  334.6 57.6 %collective-permute-start.47 = (bf16[3,256,1024]{2,1,0:T(8,128)(2,1)}, bf16[3,256,1024]{2,1,0:T(8,128)(2,1)}, u32[]{:S(2)}, u32[]{:S(2)}) collective-permute-start(bf16[3,256,1024]{2,1,0:T(8,128)(2,1)} %pad_maximum_fusion.7), channel_id=1, source_target_pairs={{8,0},{12,4},{9,1},{13,5},{10,2},{14,6},{11,3},{15,7}} | collective-permute-start | bytes 4718600 | tf_op jit(solution)/shard_map/ppermute | solution.py:323
  336.8 64.5 %collective-permute-start.66 = (bf16[768,512]{1,0:T(8,128)(2,1)S(1)}, bf16[768,512]{1,0:T(8,128)(2,1)}, u32[]{:S(2)}, u32[]{:S(2)}) collective-permute-start(bf16[768,512]{1,0:T(8,128)(2,1)S(1)} %pad_maximum_fusion.8), channel_id=1, source_target_pairs={{0,4},{4,0},{8,12},{12,8},{16,20},{20,16},{24,28},{28,24},{1,5},{5... | collective-permute-start | bytes 2359304 | tf_op jit(solution)/shard_map/ppermute | solution.py:316
  339.2 47.5 %collective-permute-start.24 = (bf16[672,512]{1,0:T(8,128)(2,1)}, bf16[672,512]{1,0:T(8,128)(2,1)}, u32[]{:S(2)}, u32[]{:S(2)}) collective-permute-start(bf16[672,512]{1,0:T(8,128)(2,1)} %pad_maximum_fusion.11), channel_id=1, source_target_pairs={{8,0},{12,4},{16,8},{20,12},{24,16},{28,20},{9,1},{13,5},{17,9},{2... | collective-permute-start | bytes 2064392 | tf_op jit(solution)/shard_map/ppermute | solution.py:323
  340.5 47.5 %collective-permute-start.23 = (bf16[672,512]{1,0:T(8,128)(2,1)}, bf16[672,512]{1,0:T(8,128)(2,1)}, u32[]{:S(2)}, u32[]{:S(2)}) collective-permute-start(bf16[672,512]{1,0:T(8,128)(2,1)} %pad_maximum_fusion.10), channel_id=1, source_target_pairs={{0,8},{4,12},{8,16},{12,20},{16,24},{20,28},{1,9},{5,13},{9,17},{1... | collective-permute-start | bytes 2064392 | tf_op jit(solution)/shard_map/ppermute | solution.py:323
  386.7 48.8 %collective-permute-start.58 = (bf16[672,512]{1,0:T(8,128)(2,1)S(1)}, bf16[672,512]{1,0:T(8,128)(2,1)S(1)}, u32[]{:S(2)}, u32[]{:S(2)}) collective-permute-start(bf16[672,512]{1,0:T(8,128)(2,1)S(1)} %pad_maximum_fusion.13), channel_id=1, source_target_pairs={{8,0},{12,4},{16,8},{20,12},{24,16},{28,20},{9,1},{13,5},{17,9},{2... | collective-permute-start | bytes 2064392 | tf_op jit(solution)/shard_map/ppermute | solution.py:323
  400.6 108.8 %collective-permute-start.26 = (bf16[512,1280]{1,0:T(8,128)(2,1)}, bf16[512,1280]{1,0:T(8,128)(2,1)S(1)}, u32[]{:S(2)}, u32[]{:S(2)}) collective-permute-start(bf16[512,1280]{1,0:T(8,128)(2,1)} %collective-permute-done.25.refs_2_), channel_id=1, source_target_pairs={{16,24},{20,28},{17,25},{21,29},{18,26},{22,30},{19,27},{23,31}} | collective-permute-start | bytes 3932168 | tf_op jit(solution)/shard_map/ppermute | solution.py:323
  401.3 108.2 %collective-permute-start.28 = (bf16[512,1280]{1,0:T(8,128)(2,1)}, bf16[512,1280]{1,0:T(8,128)(2,1)S(1)}, u32[]{:S(2)}, u32[]{:S(2)}) collective-permute-start(bf16[512,1280]{1,0:T(8,128)(2,1)} %collective-permute-done.25.refs_2_), channel_id=1, source_target_pairs={{16,20},{20,16},{24,28},{28,24},{17,21},{21,17},{25,29},{29,25},{1... | collective-permute-start | bytes 3932168 | tf_op jit(solution)/shard_map/ppermute | solution.py:316
  431.6 81.0 %collective-permute-start.38 = (bf16[512,1280]{1,0:T(8,128)(2,1)}, bf16[512,1280]{1,0:T(8,128)(2,1)}, u32[]{:S(2)}, u32[]{:S(2)}) collective-permute-start(bf16[512,1280]{1,0:T(8,128)(2,1)} %collective-permute-done.37.refs_10_), channel_id=1, source_target_pairs={{0,4},{4,0},{8,12},{12,8},{1,5},{5,1},{9,13},{13,9},{2,6},{6,2},{1... | collective-permute-start | bytes 3932168 | tf_op jit(solution)/shard_map/ppermute | solution.py:316
  435.5 77.5 %collective-permute-start.39 = (bf16[512,1280]{1,0:T(8,128)(2,1)}, bf16[512,1280]{1,0:T(8,128)(2,1)}, u32[]{:S(2)}, u32[]{:S(2)}) collective-permute-start(bf16[512,1280]{1,0:T(8,128)(2,1)} %collective-permute-done.37.refs_10_), channel_id=1, source_target_pairs={{8,0},{12,4},{9,1},{13,5},{10,2},{14,6},{11,3},{15,7}} | collective-permute-start | bytes 3932168 | tf_op jit(solution)/shard_map/ppermute | solution.py:323
  439.3 68.1 %collective-permute-start.67 = (bf16[768,512]{1,0:T(8,128)(2,1)}, bf16[768,512]{1,0:T(8,128)(2,1)S(1)}, u32[]{:S(2)}, u32[]{:S(2)}) collective-permute-start(bf16[768,512]{1,0:T(8,128)(2,1)} %pad_maximum_fusion.9), channel_id=1, source_target_pairs={{0,4},{4,0},{8,12},{12,8},{16,20},{20,16},{24,28},{28,24},{1,5},{5... | collective-permute-start | bytes 2359304 | tf_op jit(solution)/shard_map/ppermute | solution.py:316
  (81 other events, 1668.3 us)

commit v4 on v3

--- a/solution.py
+++ b/solution.py
@@ -497,9 +497,7 @@
         low = z_move(kv_of(rows - MOST, MOST), 1, range(planes - 1))
         high = z_move(kv_of(0, MOST), -1, range(1, planes))
         if part == 0:
-            for step in range(2, planes):
-                out_steps.append(line_step(out_steps[-1], step, (low, high) if step == 2 else ()))
-                later_out.append([halves(out_steps[-1][0], -step), halves(out_steps[-1][1], step)])
+            out_steps.append(line_step(out_steps[-1], 2, (low, high)))
         own_kv = kv_of(x * tokens, tokens)
         other_kv = swap_x(kv_of((1 - x) * tokens, tokens))
         for xb, v in ((0, own_kv), (1, other_kv)):
@@ -512,6 +510,11 @@
             prefix = prefix_of_groups()
         part_prefix = prefix[:, :, firsts[part] * 2 * HD : (firsts[part] + hc) * 2 * HD]
         out = attention_call(need, qkv, low, high, part_prefix, qtag, ktag)
+        if part == 0:
+            for step in range(2, planes):
+                if step > 2:
+                    out_steps.append(line_step(out_steps[-1], step, [out]))
+                later_out.append([halves(out_steps[-1][0], -step, [out]), halves(out_steps[-1][1], step, [out])])
         pieces = [(lax.dynamic_slice_in_dim(out, x * tokens, tokens, 0), 0, 0)]
         behind = out_steps[1]
         if part == parts - 1:

time: 591 us -> 593 us (level)
    ppermute x28, waiting for transfers between devices: 104 us -> 110 us  [z_move(): return lax.ppermute(v, 'row', pairs)]
  transfers between devices with their start and end apart: 68 -> 68, of which waited for: 21 -> 20; matrix products, arithmetic and copies ran while one was open for 10% -> 11% of each run, Pallas kernels for 20% -> 21%
where the time goes in v4:
time: 593 us; the launch traced here: 587 us
  waiting for transfers between devices  235 us (40%)
  Pallas kernels  138 us (23%)
  starting transfers between devices  121 us (20%)
  other arithmetic  34.6 us (6%)
  local copies, waits for them, and re-layouts  27.7 us (5%)
  between operations  21.1 us (4%)
    ppermute x28, waiting for transfers between devices, z_move(): return lax.ppermute(v, 'row', pairs)  110 us
    ppermute x17, waiting for transfers between devices, swap_x(): lax.ppermute(v, 'row', [(i, i ^ 1) for i in range(rows_n) if valid(i // 2)])  105 us
    ppermute x28, starting transfers between devices, z_move(): return lax.ppermute(v, 'row', pairs)  81.3 us
    pallas_call x2, Pallas kernels, attention_call(): pl.pallas_call(functools.partial(attention_kernel, heads, groups), out_sh...  65.6 us
    pallas_call x4, Pallas kernels, qkv_call(): pl.pallas_call(functools.partial(qkv_kernel, planes, len(blocks), finish)...  55 us
    ppermute x17, starting transfers between devices, swap_x(): lax.ppermute(v, 'row', [(i, i ^ 1) for i in range(rows_n) if valid(i // 2)])  28.2 us
    ppermute x23, waiting for transfers between devices, swap_col(): return lax.ppermute(v, 'col', [(i, i ^ bit) for i in range(cols_n)])  19 us
    pallas_call x1, Pallas kernels, out_call(): pl.pallas_call(functools.partial(out_kernel, planes, len(columns)), out_s...  17.7 us
  transfers between devices with their start and end apart: 68, of which 20 were waited for; matrix products, arithmetic and copies ran while one was open for 11% of the time, Pallas kernels for 21%

profile of v4, /device:TPU:0, one launch (start us, length us, event | category | flops | bytes accessed | tf_op | source)
XLA Modules:
  0.0 587.0 jit_solution(3925660253283153143)
XLA Ops:
  0.6 6.0 %collective-permute-start = (bf16[512,1280]{1,0:T(8,128)(2,1)}, bf16[512,1280]{1,0:T(8,128)(2,1)}, u32[]{:S(2)}, u32[]{:S(2)}) collective-permute-start(bf16[512,1280]{1,0:T(8,128)(2,1)} %refs_6_.1), channel_id=1, source_target_pairs={{0,8},{4,12},{8,16},{12,20},{16,24},{20,28},{1,9},{5,13},{9,17},{1... | collective-permute-start | bytes 3932168 | tf_op jit(solution)/shard_map/ppermute | solution.py:323
  24.4 12.8 %collective-permute-done.16 = bf16[640,768]{1,0:T(8,128)(2,1)} collective-permute-done((bf16[640,768]{1,0:T(8,128)(2,1)}, bf16[640,768]{1,0:T(8,128)(2,1)}, u32[]{:S(2)}, u32[]{:S(2)}) %collective-permute-start.16) | collective-permute-done | bytes 983072 | tf_op jit(solution)/shard_map/ppermute | solution.py:316
  38.7 19.5 %collective-permute-done.2.refs_1_ = bf16[384,1280]{1,0:T(8,128)(2,1)S(1)} collective-permute-done((bf16[384,1280]{1,0:T(8,128)(2,1)S(1)}, bf16[384,1280]{1,0:T(8,128)(2,1)S(1)}, u32[]{:S(2)}, u32[]{:S(2)}) %collective-permute-start.2) | collective-permute-done | bytes 983072 | tf_op jit(solution)/shard_map/ppermute | solution.py:316
  70.9 8.4 %collective-permute-done.10.refs_10_ = bf16[384,1280]{1,0:T(8,128)(2,1)} collective-permute-done((bf16[384,1280]{1,0:T(8,128)(2,1)S(1)}, bf16[384,1280]{1,0:T(8,128)(2,1)}, u32[]{:S(2)}, u32[]{:S(2)}) %collective-permute-start.10) | collective-permute-done | bytes 983072 | tf_op jit(solution)/shard_map/ppermute | solution.py:316
  82.5 17.9 %collective-permute-done.27 = bf16[640,768]{1,0:T(8,128)(2,1)} collective-permute-done((bf16[640,768]{1,0:T(8,128)(2,1)}, bf16[640,768]{1,0:T(8,128)(2,1)}, u32[]{:S(2)}, u32[]{:S(2)}) %collective-permute-start.27) | collective-permute-done | bytes 983072 | tf_op jit(solution)/shard_map/ppermute | solution.py:316
  106.3 5.9 collective-permute-start.29
  112.1 7.9 %collective-permute-done.11.refs_11_ = bf16[384,1280]{1,0:T(8,128)(2,1)} collective-permute-done((bf16[384,1280]{1,0:T(8,128)(2,1)}, bf16[384,1280]{1,0:T(8,128)(2,1)}, u32[]{:S(2)}, u32[]{:S(2)}) %collective-permute-start.11) | collective-permute-done | bytes 983072 | tf_op jit(solution)/shard_map/ppermute | solution.py:316
  131.5 9.4 %collective-permute-done.28 = bf16[256,1024]{1,0:T(8,128)(2,1)S(1)} collective-permute-done((bf16[256,1024]{1,0:T(8,128)(2,1)}, bf16[256,1024]{1,0:T(8,128)(2,1)S(1)}, u32[]{:S(2)}, u32[]{:S(2)}) %collective-permute-start.28) | collective-permute-done | bytes 524320 | tf_op jit(solution)/shard_map/ppermute | solution.py:316
  154.6 11.3 %collective-permute-done.30.refs_19_ = bf16[1280,768]{1,0:T(8,128)(2,1)} collective-permute-done((bf16[1280,768]{1,0:T(8,128)(2,1)}, bf16[1280,768]{1,0:T(8,128)(2,1)}, u32[]{:S(2)}, u32[]{:S(2)}) %collective-permute-start.30) | collective-permute-done | bytes 1966112 | tf_op jit(solution)/shard_map/ppermute | solution.py:323
  192.6 21.3 %collective-permute-done.20.refs_20_ = bf16[1280,768]{1,0:T(8,128)(2,1)} collective-permute-done((bf16[1280,768]{1,0:T(8,128)(2,1)}, bf16[1280,768]{1,0:T(8,128)(2,1)}, u32[]{:S(2)}, u32[]{:S(2)}) %collective-permute-start.20) | collective-permute-done | bytes 1966112 | tf_op jit(solution)/shard_map/ppermute | solution.py:323
  220.4 35.6 %collective-permute-done.34.refs_20_ = bf16[1280,768]{1,0:T(8,128)(2,1)} collective-permute-done((bf16[1280,768]{1,0:T(8,128)(2,1)}, bf16[1280,768]{1,0:T(8,128)(2,1)}, u32[]{:S(2)}, u32[]{:S(2)}) %collective-permute-start.34) | collective-permute-done | bytes 1966112 | tf_op jit(solution)/shard_map/ppermute | solution.py:323
  259.6 17.8 %qkv_start.2.refs_18_ = f32[1536,768]{1,0:T(8,128)} custom-call(s32[1]{0:T(128)} %bitcast.z_ref, s32[16,2]{1,0:T(8,128)} %stack.276.at_ref, bf16[384,1280]{1,0:T(8,128)(2,1)} %copy-done.3, bf16[384,1280]{1,0:T(8,128)(2,1)} %copy-done.4, bf16[384,1280]{1,0:T(8,128)(2,1)} %collective-permute-done.3.refs_2_, bf16[384,1280]{1,0:T(8,128)(2,1)} %collective-permute-done.4.refs_3_, ...), custom_call_target="tpu_custom_call" | custom-call | flops 12079595520 | bytes 25952256 | tf_op jit(solution)/shard_map/qkv_start/pallas_call | solution.py:112
  280.7 17.8 %qkv_start.3.refs_18_ = f32[1536,768]{1,0:T(8,128)} custom-call(s32[1]{0:T(128)} %bitcast.z_ref, s32[16,2]{1,0:T(8,128)} %stack.276.at_ref, bf16[384,1280]{1,0:T(8,128)(2,1)} %copy-done.3, bf16[384,1280]{1,0:T(8,128)(2,1)} %copy-done.4, bf16[384,1280]{1,0:T(8,128)(2,1)} %collective-permute-done.3.refs_2_, bf16[384,1280]{1,0:T(8,128)(2,1)} %collective-permute-done.4.refs_3_, ...), custom_call_target="tpu_custom_call" | custom-call | flops 12079595520 | bytes 25952256 | tf_op jit(solution)/shard_map/qkv_start/pallas_call | solution.py:112
  301.1 9.7 %qkv_end.2.q_ref.own_ref = bf16[1536,768]{1,0:T(8,128)(2,1)} custom-call(s32[1]{0:T(128)} %bitcast.z_ref, s32[16,2]{1,0:T(8,128)} %stack.276.at_ref, bf16[384,1280]{1,0:T(8,128)(2,1)} %copy-done.3, bf16[384,1280]{1,0:T(8,128)(2,1)} %copy-done.4, bf16[384,1280]{1,0:T(8,128)(2,1)} %collective-permute-done.3.refs_2_, ...), custom_call_target="tpu_custom_call" | custom-call | flops 3019898880 | bytes 25952256 | tf_op jit(solution)/shard_map/qkv_end/pallas_call | solution.py:112
  320.6 15.7 %collective-permute-done.43.refs_7_ = bf16[512,1280]{1,0:T(8,128)(2,1)} collective-permute-done((bf16[512,1280]{1,0:T(8,128)(2,1)}, bf16[512,1280]{1,0:T(8,128)(2,1)}, u32[]{:S(2)}, u32[]{:S(2)}) %collective-permute-start.43) | collective-permute-done | bytes 1310752 | tf_op jit(solution)/shard_map/ppermute | solution.py:316
  342.2 14.8 %collective-permute-done.56.refs_17_ = bf16[1280,768]{1,0:T(8,128)(2,1)} collective-permute-done((bf16[1280,768]{1,0:T(8,128)(2,1)}, bf16[1280,768]{1,0:T(8,128)(2,1)}, u32[]{:S(2)}, u32[]{:S(2)}) %collective-permute-start.56) | collective-permute-done | bytes 1966112 | tf_op jit(solution)/shard_map/ppermute | solution.py:323
  357.1 22.3 %collective-permute-start.23 = (bf16[672,512]{1,0:T(8,128)(2,1)}, bf16[672,512]{1,0:T(8,128)(2,1)}, u32[]{:S(2)}, u32[]{:S(2)}) collective-permute-start(bf16[672,512]{1,0:T(8,128)(2,1)} %pad_maximum_fusion.10), channel_id=1, source_target_pairs={{0,8},{4,12},{8,16},{12,20},{16,24},{20,28},{1,9},{5,13},{9,17},{1... | collective-permute-start | bytes 2064392 | tf_op jit(solution)/shard_map/ppermute | solution.py:323
  379.3 9.7 %qkv_end.3.q_ref.own_ref = bf16[1536,768]{1,0:T(8,128)(2,1)} custom-call(s32[1]{0:T(128)} %bitcast.z_ref, s32[16,2]{1,0:T(8,128)} %stack.276.at_ref, bf16[384,1280]{1,0:T(8,128)(2,1)} %copy-done.3, bf16[384,1280]{1,0:T(8,128)(2,1)} %copy-done.4, bf16[384,1280]{1,0:T(8,128)(2,1)} %collective-permute-done.3.refs_2_, ...), custom_call_target="tpu_custom_call" | custom-call | flops 3019898880 | bytes 25952256 | tf_op jit(solution)/shard_map/qkv_end/pallas_call | solution.py:112
  392.2 24.7 %collective-permute-done.24.high_ref = bf16[672,512]{1,0:T(8,128)(2,1)} collective-permute-done((bf16[672,512]{1,0:T(8,128)(2,1)}, bf16[672,512]{1,0:T(8,128)(2,1)}, u32[]{:S(2)}, u32[]{:S(2)}) %collective-permute-start.24) | collective-permute-done | bytes 688160 | tf_op jit(solution)/shard_map/ppermute | solution.py:323
  430.0 32.8 %attention.2 = bf16[1536,256]{1,0:T(8,128)(2,1)} custom-call(s32[6,16]{1,0:T(8,128)} %add_convert_fusion.need_ref, bf16[1536,768]{1,0:T(8,128)(2,1)} %qkv_end.2.q_ref.own_ref, bf16[1536,768]{1,0:T(8,128)(2,1)} %qkv_end.2.q_ref.own_ref, bf16[672,512]{1,0:T(8,128)(2,1)} %collective-permute-done.23.low_ref, bf16[672,512]{1,0:T(8,128)(2,1)} %collective-permute-done.24.high_ref, ...), custom_call_target="tpu_custom_call" | custom-call | flops 3221225472 | bytes 6291456 | tf_op jit(solution)/shard_map/attention/pallas_call | solution.py:203
  475.7 32.8 %attention.3 = bf16[1536,256]{1,0:T(8,128)(2,1)} custom-call(s32[6,16]{1,0:T(8,128)} %add_convert_fusion.need_ref, bf16[1536,768]{1,0:T(8,128)(2,1)} %qkv_end.3.q_ref.own_ref, bf16[1536,768]{1,0:T(8,128)(2,1)} %qkv_end.3.q_ref.own_ref, bf16[672,512]{1,0:T(8,128)(2,1)} %collective-permute-done.57.low_ref, bf16[672,512]{1,0:T(8,128)(2,1)} %collective-permute-done.58.high_ref, ...), custom_call_target="tpu_custom_call" | custom-call | flops 3221225472 | bytes 6291456 | tf_op jit(solution)/shard_map/attention/pallas_call | solution.py:203
  547.0 7.1 %collective-permute-done.61.refs_25_ = bf16[768,256]{1,0:T(8,128)(2,1)S(1)} collective-permute-done((bf16[768,256]{1,0:T(8,128)(2,1)S(1)}, bf16[768,256]{1,0:T(8,128)(2,1)S(1)}, u32[]{:S(2)}, u32[]{:S(2)}) %collective-permute-start.61) | collective-permute-done | bytes 393248 | tf_op jit(solution)/shard_map/ppermute | solution.py:319
  555.8 10.9 %collective-permute-done.47.refs_13_ = bf16[512,1280]{1,0:T(8,128)(2,1)S(1)} collective-permute-done((bf16[512,1280]{1,0:T(8,128)(2,1)}, bf16[512,1280]{1,0:T(8,128)(2,1)S(1)}, u32[]{:S(2)}, u32[]{:S(2)}) %collective-permute-start.47) | collective-permute-done | bytes 1310752 | tf_op jit(solution)/shard_map/ppermute | solution.py:316
  568.8 17.7 %project.1 = bf16[768,1280]{1,0:T(8,128)(2,1)} custom-call(s32[2]{0:T(128)} %pad_add_fusion.2.where_ref, s32[16]{0:T(128)} %stack.235.at_ref, bf16[768,1280]{1,0:T(8,128)(2,1)} %hidden_ref.1, bf16[768,1280]{1,0:T(8,128)(2,1)} %convolution_convert_fusion.gate_ref, bf16[512,1280]{1,0:T(8,128)(2,1)} %collective-permute-done.39.refs_0_, ...), custom_call_target="tpu_custom_call" | custom-call | flops 8053063680 | bytes 22675456 | tf_op jit(solution)/shard_map/project/pallas_call | solution.py:277
  (305 shorter events, 176.0 us)
Async XLA Ops:
  0.6 59.1 %collective-permute-start = (bf16[512,1280]{1,0:T(8,128)(2,1)}, bf16[512,1280]{1,0:T(8,128)(2,1)}, u32[]{:S(2)}, u32[]{:S(2)}) collective-permute-start(bf16[512,1280]{1,0:T(8,128)(2,1)} %refs_6_.1), channel_id=1, source_target_pairs={{0,8},{4,12},{8,16},{12,20},{16,24},{20,28},{1,9},{5,13},{9,17},{1... | collective-permute-start | bytes 3932168 | tf_op jit(solution)/shard_map/ppermute | solution.py:323
  6.6 57.0 %collective-permute-start.1 = (bf16[512,1280]{1,0:T(8,128)(2,1)}, bf16[512,1280]{1,0:T(8,128)(2,1)}, u32[]{:S(2)}, u32[]{:S(2)}) collective-permute-start(bf16[512,1280]{1,0:T(8,128)(2,1)} %refs_6_.1), channel_id=1, source_target_pairs={{8,0},{12,4},{16,8},{20,12},{24,16},{28,20},{9,1},{13,5},{17,9},{2... | collective-permute-start | bytes 3932168 | tf_op jit(solution)/shard_map/ppermute | solution.py:323
  65.1 56.9 %collective-permute-start.17 = (bf16[1280,768]{1,0:T(8,128)(2,1)}, bf16[1280,768]{1,0:T(8,128)(2,1)}, u32[]{:S(2)}, u32[]{:S(2)}) collective-permute-start(bf16[1280,768]{1,0:T(8,128)(2,1)} %maximum_select_fusion.refs_18_), channel_id=1, source_target_pairs={{0,8},{4,12},{8,16},{12,20},{16,24},{20,28},{1,9},{5,13},{9,17},{1... | collective-permute-start | bytes 5898248 | tf_op jit(solution)/shard_map/ppermute | solution.py:323
  79.3 44.4 %collective-permute-start.18 = (bf16[1280,768]{1,0:T(8,128)(2,1)}, bf16[1280,768]{1,0:T(8,128)(2,1)}, u32[]{:S(2)}, u32[]{:S(2)}) collective-permute-start(bf16[1280,768]{1,0:T(8,128)(2,1)} %maximum_select_fusion.refs_18_), channel_id=1, source_target_pairs={{8,0},{12,4},{16,8},{20,12},{24,16},{28,20},{9,1},{13,5},{17,9},{2... | collective-permute-start | bytes 5898248 | tf_op jit(solution)/shard_map/ppermute | solution.py:323
  106.3 48.3 %collective-permute-start.29 = (bf16[1280,768]{1,0:T(8,128)(2,1)}, bf16[1280,768]{1,0:T(8,128)(2,1)}, u32[]{:S(2)}, u32[]{:S(2)}) collective-permute-start(bf16[1280,768]{1,0:T(8,128)(2,1)} %maximum_select_fusion.1.refs_18_), channel_id=1, source_target_pairs={{0,8},{4,12},{8,16},{12,20},{16,24},{20,28},{1,9},{5,13},{9,17},{1... | collective-permute-start | bytes 5898248 | tf_op jit(solution)/shard_map/ppermute | solution.py:323
  120.0 45.9 %collective-permute-start.30 = (bf16[1280,768]{1,0:T(8,128)(2,1)}, bf16[1280,768]{1,0:T(8,128)(2,1)}, u32[]{:S(2)}, u32[]{:S(2)}) collective-permute-start(bf16[1280,768]{1,0:T(8,128)(2,1)} %maximum_select_fusion.1.refs_18_), channel_id=1, source_target_pairs={{8,0},{12,4},{16,8},{20,12},{24,16},{28,20},{9,1},{13,5},{17,9},{2... | collective-permute-start | bytes 5898248 | tf_op jit(solution)/shard_map/ppermute | solution.py:323
  127.9 61.6 %collective-permute-start.19 = (bf16[1280,768]{1,0:T(8,128)(2,1)}, bf16[1280,768]{1,0:T(8,128)(2,1)}, u32[]{:S(2)}, u32[]{:S(2)}) collective-permute-start(bf16[1280,768]{1,0:T(8,128)(2,1)} %collective-permute-done.17.refs_17_), channel_id=1, source_target_pairs={{8,16},{12,20},{16,24},{20,28},{9,17},{13,21},{17,25},{21,29},{10,... | collective-permute-start | bytes 5898248 | tf_op jit(solution)/shard_map/ppermute | solution.py:323
  165.9 48.0 %collective-permute-start.20 = (bf16[1280,768]{1,0:T(8,128)(2,1)}, bf16[1280,768]{1,0:T(8,128)(2,1)}, u32[]{:S(2)}, u32[]{:S(2)}) collective-permute-start(bf16[1280,768]{1,0:T(8,128)(2,1)} %collective-permute-done.18.refs_19_), channel_id=1, source_target_pairs={{8,0},{12,4},{16,8},{20,12},{9,1},{13,5},{17,9},{21,13},{10,2},{14... | collective-permute-start | bytes 5898248 | tf_op jit(solution)/shard_map/ppermute | solution.py:323
  189.4 66.6 %collective-permute-start.34 = (bf16[1280,768]{1,0:T(8,128)(2,1)}, bf16[1280,768]{1,0:T(8,128)(2,1)}, u32[]{:S(2)}, u32[]{:S(2)}) collective-permute-start(bf16[1280,768]{1,0:T(8,128)(2,1)} %collective-permute-done.30.refs_19_), channel_id=1, source_target_pairs={{8,0},{12,4},{16,8},{20,12},{9,1},{13,5},{17,9},{21,13},{10,2},{14... | collective-permute-start | bytes 5898248 | tf_op jit(solution)/shard_map/ppermute | solution.py:323
  213.9 84.7 %collective-permute-start.21 = (bf16[1280,768]{1,0:T(8,128)(2,1)}, bf16[1280,768]{1,0:T(8,128)(2,1)S(1)}, u32[]{:S(2)}, u32[]{:S(2)}) collective-permute-start(bf16[1280,768]{1,0:T(8,128)(2,1)} %collective-permute-done.19.refs_16_), channel_id=1, source_target_pairs={{16,24},{20,28},{17,25},{21,29},{18,26},{22,30},{19,27},{23,31}} | collective-permute-start | bytes 5898248 | tf_op jit(solution)/shard_map/ppermute | solution.py:323
  214.7 84.7 %collective-permute-start.22 = (bf16[1280,768]{1,0:T(8,128)(2,1)}, bf16[1280,768]{1,0:T(8,128)(2,1)S(1)}, u32[]{:S(2)}, u32[]{:S(2)}) collective-permute-start(bf16[1280,768]{1,0:T(8,128)(2,1)} %collective-permute-done.20.refs_20_), channel_id=1, source_target_pairs={{8,0},{12,4},{9,1},{13,5},{10,2},{14,6},{11,3},{15,7}} | collective-permute-start | bytes 5898248 | tf_op jit(solution)/shard_map/ppermute | solution.py:323
  256.0 54.8 %collective-permute-start.35 = (bf16[3,256,1024]{2,1,0:T(8,128)(2,1)}, bf16[3,256,1024]{2,1,0:T(8,128)(2,1)}, u32[]{:S(2)}, u32[]{:S(2)}) collective-permute-start(bf16[3,256,1024]{2,1,0:T(8,128)(2,1)} %pad_maximum_fusion.4), channel_id=1, source_target_pairs={{8,16},{12,20},{9,17},{13,21},{10,18},{14,22},{11,19},{15,23}} | collective-permute-start | bytes 4718600 | tf_op jit(solution)/shard_map/ppermute | solution.py:323
  257.8 55.0 %collective-permute-start.36 = (bf16[3,256,1024]{2,1,0:T(8,128)(2,1)}, bf16[3,256,1024]{2,1,0:T(8,128)(2,1)}, u32[]{:S(2)}, u32[]{:S(2)}) collective-permute-start(bf16[3,256,1024]{2,1,0:T(8,128)(2,1)} %pad_maximum_fusion.5), channel_id=1, source_target_pairs={{16,8},{20,12},{17,9},{21,13},{18,10},{22,14},{19,11},{23,15}} | collective-permute-start | bytes 4718600 | tf_op jit(solution)/shard_map/ppermute | solution.py:323
  318.7 105.0 %collective-permute-start.37 = (bf16[3,256,1024]{2,1,0:T(8,128)(2,1)}, bf16[3,256,1024]{2,1,0:T(8,128)(2,1)S(1)}, u32[]{:S(2)}, u32[]{:S(2)}) collective-permute-start(bf16[3,256,1024]{2,1,0:T(8,128)(2,1)} %pad_maximum_fusion.6), channel_id=1, source_target_pairs={{16,24},{20,28},{17,25},{21,29},{18,26},{22,30},{19,27},{23,31}} | collective-permute-start | bytes 4718600 | tf_op jit(solution)/shard_map/ppermute | solution.py:323
  336.4 132.2 %collective-permute-start.66 = (bf16[768,512]{1,0:T(8,128)(2,1)}, bf16[768,512]{1,0:T(8,128)(2,1)S(1)}, u32[]{:S(2)}, u32[]{:S(2)}) collective-permute-start(bf16[768,512]{1,0:T(8,128)(2,1)} %pad_maximum_fusion.8), channel_id=1, source_target_pairs={{0,4},{4,0},{8,12},{12,8},{16,20},{20,16},{24,28},{28,24},{1,5},{5... | collective-permute-start | bytes 2359304 | tf_op jit(solution)/shard_map/ppermute | solution.py:316
  337.8 87.4 %collective-permute-start.38 = (bf16[3,256,1024]{2,1,0:T(8,128)(2,1)}, bf16[3,256,1024]{2,1,0:T(8,128)(2,1)}, u32[]{:S(2)}, u32[]{:S(2)}) collective-permute-start(bf16[3,256,1024]{2,1,0:T(8,128)(2,1)} %pad_maximum_fusion.7), channel_id=1, source_target_pairs={{8,0},{12,4},{9,1},{13,5},{10,2},{14,6},{11,3},{15,7}} | collective-permute-start | bytes 4718600 | tf_op jit(solution)/shard_map/ppermute | solution.py:323
  340.9 76.0 %collective-permute-start.24 = (bf16[672,512]{1,0:T(8,128)(2,1)}, bf16[672,512]{1,0:T(8,128)(2,1)}, u32[]{:S(2)}, u32[]{:S(2)}) collective-permute-start(bf16[672,512]{1,0:T(8,128)(2,1)} %pad_maximum_fusion.11), channel_id=1, source_target_pairs={{8,0},{12,4},{16,8},{20,12},{24,16},{28,20},{9,1},{13,5},{17,9},{2... | collective-permute-start | bytes 2064392 | tf_op jit(solution)/shard_map/ppermute | solution.py:323
  357.1 61.2 %collective-permute-start.23 = (bf16[672,512]{1,0:T(8,128)(2,1)}, bf16[672,512]{1,0:T(8,128)(2,1)}, u32[]{:S(2)}, u32[]{:S(2)}) collective-permute-start(bf16[672,512]{1,0:T(8,128)(2,1)} %pad_maximum_fusion.10), channel_id=1, source_target_pairs={{0,8},{4,12},{8,16},{12,20},{16,24},{20,28},{1,9},{5,13},{9,17},{1... | collective-permute-start | bytes 2064392 | tf_op jit(solution)/shard_map/ppermute | solution.py:323
  417.0 53.4 %collective-permute-start.58 = (bf16[672,512]{1,0:T(8,128)(2,1)}, bf16[672,512]{1,0:T(8,128)(2,1)}, u32[]{:S(2)}, u32[]{:S(2)}) collective-permute-start(bf16[672,512]{1,0:T(8,128)(2,1)} %pad_maximum_fusion.13), channel_id=1, source_target_pairs={{8,0},{12,4},{16,8},{20,12},{24,16},{28,20},{9,1},{13,5},{17,9},{2... | collective-permute-start | bytes 2064392 | tf_op jit(solution)/shard_map/ppermute | solution.py:323
  418.3 55.5 %collective-permute-start.57 = (bf16[672,512]{1,0:T(8,128)(2,1)}, bf16[672,512]{1,0:T(8,128)(2,1)}, u32[]{:S(2)}, u32[]{:S(2)}) collective-permute-start(bf16[672,512]{1,0:T(8,128)(2,1)} %pad_maximum_fusion.12), channel_id=1, source_target_pairs={{0,8},{4,12},{8,16},{12,20},{16,24},{20,28},{1,9},{5,13},{9,17},{1... | collective-permute-start | bytes 2064392 | tf_op jit(solution)/shard_map/ppermute | solution.py:323
  462.8 49.1 %collective-permute-start.45 = (bf16[512,1280]{1,0:T(8,128)(2,1)}, bf16[512,1280]{1,0:T(8,128)(2,1)}, u32[]{:S(2)}, u32[]{:S(2)}) collective-permute-start(bf16[512,1280]{1,0:T(8,128)(2,1)} %collective-permute-done.26.refs_10_), channel_id=1, source_target_pairs={{0,4},{4,0},{8,12},{12,8},{1,5},{5,1},{9,13},{13,9},{2,6},{6,2},{1... | collective-permute-start | bytes 3932168 | tf_op jit(solution)/shard_map/ppermute | solution.py:316
  466.9 45.1 %collective-permute-start.41 = (bf16[512,1280]{1,0:T(8,128)(2,1)S(1)}, bf16[512,1280]{1,0:T(8,128)(2,1)}, u32[]{:S(2)}, u32[]{:S(2)}) collective-permute-start(bf16[512,1280]{1,0:T(8,128)(2,1)S(1)} %collective-permute-done.25.refs_2_), channel_id=1, source_target_pairs={{16,20},{20,16},{24,28},{28,24},{17,21},{21,17},{25,29},{29,25},{1... | collective-permute-start | bytes 3932168 | tf_op jit(solution)/shard_map/ppermute | solution.py:316
  468.6 46.8 %collective-permute-start.39 = (bf16[512,1280]{1,0:T(8,128)(2,1)S(1)}, bf16[512,1280]{1,0:T(8,128)(2,1)}, u32[]{:S(2)}, u32[]{:S(2)}) collective-permute-start(bf16[512,1280]{1,0:T(8,128)(2,1)S(1)} %collective-permute-done.25.refs_2_), channel_id=1, source_target_pairs={{16,24},{20,28},{17,25},{21,29},{18,26},{22,30},{19,27},{23,31}} | collective-permute-start | bytes 3932168 | tf_op jit(solution)/shard_map/ppermute | solution.py:323
  470.3 45.3 %collective-permute-start.46 = (bf16[512,1280]{1,0:T(8,128)(2,1)}, bf16[512,1280]{1,0:T(8,128)(2,1)}, u32[]{:S(2)}, u32[]{:S(2)}) collective-permute-start(bf16[512,1280]{1,0:T(8,128)(2,1)} %collective-permute-done.26.refs_10_), channel_id=1, source_target_pairs={{8,0},{12,4},{9,1},{13,5},{10,2},{14,6},{11,3},{15,7}} | collective-permute-start | bytes 3932168 | tf_op jit(solution)/shard_map/ppermute | solution.py:323
  (80 other events, 1595.5 us)

commit v5 on v3

--- a/solution.py
+++ b/solution.py
@@ -429,7 +429,7 @@
     group_tag = jnp.repeat(jnp.arange(groups, dtype=jnp.int32), KT)
     ktag = jnp.concatenate([group_tag, key_req]).reshape(-1, KT, 1)
     qtag = jnp.stack([plane_group, plane_req])[:, None, :]
-    tile = tile_rows(rows, 256)
+    tile = tile_rows(rows, 512)
     tile_group = plane_group.reshape(-1, tile)
     tile_req = plane_req.reshape(-1, tile)
     need_group = jnp.any(tile_group[:, None, :] == jnp.arange(groups, dtype=jnp.int32)[None, :, None], axis=2)

time: 591 us -> 580 us (0.981)
  Pallas kernels: 137 us -> 124 us
    pallas_call x2, Pallas kernels: 64.2 us -> 51.6 us  [attention_call(): pl.pallas_call(functools.partial(attention_kernel, heads, groups), out_sh...]
  transfers between devices with their start and end apart: 68 -> 68, of which waited for: 21 -> 21; matrix products, arithmetic and copies ran while one was open for 10% -> 10% of each run, Pallas kernels for 20% -> 19%
where the time goes in v5:
time: 580 us; the launch traced here: 570 us
  waiting for transfers between devices  230 us (40%)
  starting transfers between devices  125 us (22%)
  Pallas kernels  124 us (21%)
  other arithmetic  31.8 us (5%)
  local copies, waits for them, and re-layouts  29.2 us (5%)
  between operations  20.4 us (4%)
    ppermute x17, waiting for transfers between devices, swap_x(): lax.ppermute(v, 'row', [(i, i ^ 1) for i in range(rows_n) if valid(i // 2)])  106 us
    ppermute x28, waiting for transfers between devices, z_move(): return lax.ppermute(v, 'row', pairs)  103 us
    ppermute x28, starting transfers between devices, z_move(): return lax.ppermute(v, 'row', pairs)  86.1 us
    pallas_call x4, Pallas kernels, qkv_call(): pl.pallas_call(functools.partial(qkv_kernel, planes, len(blocks), finish)...  54.9 us
    pallas_call x2, Pallas kernels, attention_call(): pl.pallas_call(functools.partial(attention_kernel, heads, groups), out_sh...  51.6 us
    ppermute x17, starting transfers between devices, swap_x(): lax.ppermute(v, 'row', [(i, i ^ 1) for i in range(rows_n) if valid(i // 2)])  25 us
    ppermute x23, waiting for transfers between devices, swap_col(): return lax.ppermute(v, 'col', [(i, i ^ bit) for i in range(cols_n)])  20.1 us
    pallas_call x1, Pallas kernels, out_call(): pl.pallas_call(functools.partial(out_kernel, planes, len(columns)), out_s...  17.7 us
  transfers between devices with their start and end apart: 68, of which 21 were waited for; matrix products, arithmetic and copies ran while one was open for 10% of the time, Pallas kernels for 19%

profile of v5, /device:TPU:0, one launch (start us, length us, event | category | flops | bytes accessed | tf_op | source)
XLA Modules:
  0.0 570.3 jit_solution(4847956490974376657)
XLA Ops:
  24.4 6.3 %collective-permute-done.16 = bf16[640,768]{1,0:T(8,128)(2,1)} collective-permute-done((bf16[640,768]{1,0:T(8,128)(2,1)}, bf16[640,768]{1,0:T(8,128)(2,1)}, u32[]{:S(2)}, u32[]{:S(2)}) %collective-permute-start.16) | collective-permute-done | bytes 983072 | tf_op jit(solution)/shard_map/ppermute | solution.py:316
  32.8 18.9 %collective-permute-done.2.refs_1_ = bf16[384,1280]{1,0:T(8,128)(2,1)S(1)} collective-permute-done((bf16[384,1280]{1,0:T(8,128)(2,1)S(1)}, bf16[384,1280]{1,0:T(8,128)(2,1)S(1)}, u32[]{:S(2)}, u32[]{:S(2)}) %collective-permute-start.2) | collective-permute-done | bytes 983072 | tf_op jit(solution)/shard_map/ppermute | solution.py:316
  59.8 13.1 %collective-permute-done.10.refs_10_ = bf16[384,1280]{1,0:T(8,128)(2,1)} collective-permute-done((bf16[384,1280]{1,0:T(8,128)(2,1)S(1)}, bf16[384,1280]{1,0:T(8,128)(2,1)}, u32[]{:S(2)}, u32[]{:S(2)}) %collective-permute-start.10) | collective-permute-done | bytes 983072 | tf_op jit(solution)/shard_map/ppermute | solution.py:316
  83.0 11.0 %collective-permute-done.29 = bf16[640,768]{1,0:T(8,128)(2,1)} collective-permute-done((bf16[640,768]{1,0:T(8,128)(2,1)}, bf16[640,768]{1,0:T(8,128)(2,1)}, u32[]{:S(2)}, u32[]{:S(2)}) %collective-permute-start.29) | collective-permute-done | bytes 983072 | tf_op jit(solution)/shard_map/ppermute | solution.py:316
  97.9 16.3 %collective-permute-done.11.refs_11_ = bf16[384,1280]{1,0:T(8,128)(2,1)} collective-permute-done((bf16[384,1280]{1,0:T(8,128)(2,1)}, bf16[384,1280]{1,0:T(8,128)(2,1)}, u32[]{:S(2)}, u32[]{:S(2)}) %collective-permute-start.11) | collective-permute-done | bytes 983072 | tf_op jit(solution)/shard_map/ppermute | solution.py:316
  131.4 7.4 %collective-permute-done.41 = bf16[256,1024]{1,0:T(8,128)(2,1)} collective-permute-done((bf16[256,1024]{1,0:T(8,128)(2,1)S(1)}, bf16[256,1024]{1,0:T(8,128)(2,1)}, u32[]{:S(2)}, u32[]{:S(2)}) %collective-permute-start.41) | collective-permute-done | bytes 524320 | tf_op jit(solution)/shard_map/ppermute | solution.py:316
  140.0 19.4 %collective-permute-done.30.refs_17_ = bf16[1280,768]{1,0:T(8,128)(2,1)} collective-permute-done((bf16[1280,768]{1,0:T(8,128)(2,1)}, bf16[1280,768]{1,0:T(8,128)(2,1)}, u32[]{:S(2)}, u32[]{:S(2)}) %collective-permute-start.30) | collective-permute-done | bytes 1966112 | tf_op jit(solution)/shard_map/ppermute | solution.py:323
  198.1 14.3 %collective-permute-done.20.refs_20_ = bf16[1280,768]{1,0:T(8,128)(2,1)} collective-permute-done((bf16[1280,768]{1,0:T(8,128)(2,1)}, bf16[1280,768]{1,0:T(8,128)(2,1)}, u32[]{:S(2)}, u32[]{:S(2)}) %collective-permute-start.20) | collective-permute-done | bytes 1966112 | tf_op jit(solution)/shard_map/ppermute | solution.py:323
  213.3 17.7 %qkv_start.2.refs_18_ = f32[1536,768]{1,0:T(8,128)} custom-call(s32[1]{0:T(128)} %bitcast.z_ref, s32[16,2]{1,0:T(8,128)} %stack.276.at_ref, bf16[384,1280]{1,0:T(8,128)(2,1)} %copy-done.3, bf16[384,1280]{1,0:T(8,128)(2,1)} %copy-done.4, bf16[384,1280]{1,0:T(8,128)(2,1)} %collective-permute-done.3.refs_2_, bf16[384,1280]{1,0:T(8,128)(2,1)} %collective-permute-done.4.refs_3_, ...), custom_call_target="tpu_custom_call" | custom-call | flops 12079595520 | bytes 25952256 | tf_op jit(solution)/shard_map/qkv_start/pallas_call | solution.py:112
  236.5 17.9 %collective-permute-done.33.refs_20_ = bf16[1280,768]{1,0:T(8,128)(2,1)} collective-permute-done((bf16[1280,768]{1,0:T(8,128)(2,1)}, bf16[1280,768]{1,0:T(8,128)(2,1)}, u32[]{:S(2)}, u32[]{:S(2)}) %collective-permute-start.33) | collective-permute-done | bytes 1966112 | tf_op jit(solution)/shard_map/ppermute | solution.py:323
  260.0 17.8 %qkv_start.3.refs_18_ = f32[1536,768]{1,0:T(8,128)} custom-call(s32[1]{0:T(128)} %bitcast.z_ref, s32[16,2]{1,0:T(8,128)} %stack.276.at_ref, bf16[384,1280]{1,0:T(8,128)(2,1)} %copy-done.3, bf16[384,1280]{1,0:T(8,128)(2,1)} %copy-done.4, bf16[384,1280]{1,0:T(8,128)(2,1)} %collective-permute-done.3.refs_2_, bf16[384,1280]{1,0:T(8,128)(2,1)} %collective-permute-done.4.refs_3_, ...), custom_call_target="tpu_custom_call" | custom-call | flops 12079595520 | bytes 25952256 | tf_op jit(solution)/shard_map/qkv_start/pallas_call | solution.py:112
  279.7 14.1 %collective-permute-done.22.refs_17_ = bf16[1280,768]{1,0:T(8,128)(2,1)S(1)} collective-permute-done((bf16[1280,768]{1,0:T(8,128)(2,1)}, bf16[1280,768]{1,0:T(8,128)(2,1)S(1)}, u32[]{:S(2)}, u32[]{:S(2)}) %collective-permute-start.22) | collective-permute-done | bytes 1966112 | tf_op jit(solution)/shard_map/ppermute | solution.py:323
  295.2 9.7 %qkv_end.2.q_ref.own_ref = bf16[1536,768]{1,0:T(8,128)(2,1)} custom-call(s32[1]{0:T(128)} %bitcast.z_ref, s32[16,2]{1,0:T(8,128)} %stack.276.at_ref, bf16[384,1280]{1,0:T(8,128)(2,1)} %copy-done.3, bf16[384,1280]{1,0:T(8,128)(2,1)} %copy-done.4, bf16[384,1280]{1,0:T(8,128)(2,1)} %collective-permute-done.3.refs_2_, ...), custom_call_target="tpu_custom_call" | custom-call | flops 3019898880 | bytes 25952256 | tf_op jit(solution)/shard_map/qkv_end/pallas_call | solution.py:112
  313.1 21.5 %collective-permute-done.35.refs_7_ = bf16[512,1280]{1,0:T(8,128)(2,1)S(1)} collective-permute-done((bf16[512,1280]{1,0:T(8,128)(2,1)}, bf16[512,1280]{1,0:T(8,128)(2,1)S(1)}, u32[]{:S(2)}, u32[]{:S(2)}) %collective-permute-start.35) | collective-permute-done | bytes 1310752 | tf_op jit(solution)/shard_map/ppermute | solution.py:316
  340.5 28.7 %collective-permute-start.23 = (bf16[672,512]{1,0:T(8,128)(2,1)}, bf16[672,512]{1,0:T(8,128)(2,1)}, u32[]{:S(2)}, u32[]{:S(2)}) collective-permute-start(bf16[672,512]{1,0:T(8,128)(2,1)} %pad_maximum_fusion.10), channel_id=1, source_target_pairs={{0,8},{4,12},{8,16},{12,20},{16,24},{20,28},{1,9},{5,13},{9,17},{1... | collective-permute-start | bytes 2064392 | tf_op jit(solution)/shard_map/ppermute | solution.py:323
  369.2 9.7 %qkv_end.3.q_ref.own_ref = bf16[1536,768]{1,0:T(8,128)(2,1)} custom-call(s32[1]{0:T(128)} %bitcast.z_ref, s32[16,2]{1,0:T(8,128)} %stack.276.at_ref, bf16[384,1280]{1,0:T(8,128)(2,1)} %copy-done.3, bf16[384,1280]{1,0:T(8,128)(2,1)} %copy-done.4, bf16[384,1280]{1,0:T(8,128)(2,1)} %collective-permute-done.3.refs_2_, ...), custom_call_target="tpu_custom_call" | custom-call | flops 3019898880 | bytes 25952256 | tf_op jit(solution)/shard_map/qkv_end/pallas_call | solution.py:112
  392.2 6.0 %collective-permute-start.57 = (bf16[672,512]{1,0:T(8,128)(2,1)S(1)}, bf16[672,512]{1,0:T(8,128)(2,1)S(1)}, u32[]{:S(2)}, u32[]{:S(2)}) collective-permute-start(bf16[672,512]{1,0:T(8,128)(2,1)S(1)} %pad_maximum_fusion.12), channel_id=1, source_target_pairs={{0,8},{4,12},{8,16},{12,20},{16,24},{20,28},{1,9},{5,13},{9,17},{1... | collective-permute-start | bytes 2064392 | tf_op jit(solution)/shard_map/ppermute | solution.py:323
  402.3 29.2 %collective-permute-done.37.refs_10_ = bf16[512,1280]{1,0:T(8,128)(2,1)} collective-permute-done((bf16[512,1280]{1,0:T(8,128)(2,1)}, bf16[512,1280]{1,0:T(8,128)(2,1)}, u32[]{:S(2)}, u32[]{:S(2)}) %collective-permute-start.37) | collective-permute-done | bytes 1310752 | tf_op jit(solution)/shard_map/ppermute | solution.py:323
  439.3 25.8 %attention.3 = bf16[1536,256]{1,0:T(8,128)(2,1)} custom-call(s32[3,16]{1,0:T(4,128)} %add_convert_fusion.need_ref, bf16[1536,768]{1,0:T(8,128)(2,1)} %qkv_end.3.q_ref.own_ref, bf16[1536,768]{1,0:T(8,128)(2,1)} %qkv_end.3.q_ref.own_ref, bf16[672,512]{1,0:T(8,128)(2,1)} %copy-done.36, bf16[672,512]{1,0:T(8,128)(2,1)} %copy-done.35, ...), custom_call_target="tpu_custom_call" | custom-call | flops 3221225472 | bytes 6291456 | tf_op jit(solution)/shard_map/attention/pallas_call | solution.py:203
  467.0 25.8 %attention.2 = bf16[1536,256]{1,0:T(8,128)(2,1)} custom-call(s32[3,16]{1,0:T(4,128)} %add_convert_fusion.need_ref, bf16[1536,768]{1,0:T(8,128)(2,1)} %qkv_end.2.q_ref.own_ref, bf16[1536,768]{1,0:T(8,128)(2,1)} %qkv_end.2.q_ref.own_ref, bf16[672,512]{1,0:T(8,128)(2,1)} %collective-permute-done.23.low_ref, bf16[672,512]{1,0:T(8,128)(2,1)} %collective-permute-done.24.high_ref, ...), custom_call_target="tpu_custom_call" | custom-call | flops 3221225472 | bytes 6291456 | tf_op jit(solution)/shard_map/attention/pallas_call | solution.py:203
  525.4 5.9 %collective-permute-done.50.refs_17_ = bf16[768,256]{1,0:T(8,128)(2,1)S(1)} collective-permute-done((bf16[768,256]{1,0:T(8,128)(2,1)}, bf16[768,256]{1,0:T(8,128)(2,1)S(1)}, u32[]{:S(2)}, u32[]{:S(2)}) %collective-permute-start.50) | collective-permute-done | bytes 393248 | tf_op jit(solution)/shard_map/ppermute | solution.py:319
  531.9 7.1 %collective-permute-done.61.refs_25_ = bf16[768,256]{1,0:T(8,128)(2,1)S(1)} collective-permute-done((bf16[768,256]{1,0:T(8,128)(2,1)S(1)}, bf16[768,256]{1,0:T(8,128)(2,1)S(1)}, u32[]{:S(2)}, u32[]{:S(2)}) %collective-permute-start.61) | collective-permute-done | bytes 393248 | tf_op jit(solution)/shard_map/ppermute | solution.py:319
  541.4 9.6 %collective-permute-done.40.refs_13_ = bf16[512,1280]{1,0:T(8,128)(2,1)S(1)} collective-permute-done((bf16[512,1280]{1,0:T(8,128)(2,1)}, bf16[512,1280]{1,0:T(8,128)(2,1)S(1)}, u32[]{:S(2)}, u32[]{:S(2)}) %collective-permute-start.40) | collective-permute-done | bytes 1310752 | tf_op jit(solution)/shard_map/ppermute | solution.py:316
  552.1 17.7 %project.1 = bf16[768,1280]{1,0:T(8,128)(2,1)} custom-call(s32[2]{0:T(128)} %pad_add_fusion.2.where_ref, s32[16]{0:T(128)} %stack.235.at_ref, bf16[768,1280]{1,0:T(8,128)(2,1)} %hidden_ref.1, bf16[768,1280]{1,0:T(8,128)(2,1)} %convolution_convert_fusion.gate_ref, bf16[512,1280]{1,0:T(8,128)(2,1)} %copy-done.15, bf16[512,1280]{1,0:T(8,128)(2,1)} %copy-done.17, ...), custom_call_target="tpu_custom_call" | custom-call | flops 8053063680 | bytes 22675456 | tf_op jit(solution)/shard_map/project/pallas_call | solution.py:277
  (308 shorter events, 178.9 us)
Async XLA Ops:
  72.9 48.8 %collective-permute-start.17 = (bf16[1280,768]{1,0:T(8,128)(2,1)}, bf16[1280,768]{1,0:T(8,128)(2,1)}, u32[]{:S(2)}, u32[]{:S(2)}) collective-permute-start(bf16[1280,768]{1,0:T(8,128)(2,1)} %maximum_select_fusion.refs_18_), channel_id=1, source_target_pairs={{0,8},{4,12},{8,16},{12,20},{16,24},{20,28},{1,9},{5,13},{9,17},{1... | collective-permute-start | bytes 5898248 | tf_op jit(solution)/shard_map/ppermute | solution.py:323
  119.2 51.4 %collective-permute-start.31 = (bf16[1280,768]{1,0:T(8,128)(2,1)}, bf16[1280,768]{1,0:T(8,128)(2,1)}, u32[]{:S(2)}, u32[]{:S(2)}) collective-permute-start(bf16[1280,768]{1,0:T(8,128)(2,1)} %maximum_select_fusion.1.refs_18_), channel_id=1, source_target_pairs={{8,0},{12,4},{16,8},{20,12},{24,16},{28,20},{9,1},{13,5},{17,9},{2... | collective-permute-start | bytes 5898248 | tf_op jit(solution)/shard_map/ppermute | solution.py:323
  128.1 68.6 %collective-permute-start.19 = (bf16[1280,768]{1,0:T(8,128)(2,1)}, bf16[1280,768]{1,0:T(8,128)(2,1)}, u32[]{:S(2)}, u32[]{:S(2)}) collective-permute-start(bf16[1280,768]{1,0:T(8,128)(2,1)} %collective-permute-done.17.refs_17_), channel_id=1, source_target_pairs={{8,16},{12,20},{16,24},{20,28},{9,17},{13,21},{17,25},{21,29},{10,... | collective-permute-start | bytes 5898248 | tf_op jit(solution)/shard_map/ppermute | solution.py:323
  130.1 82.2 %collective-permute-start.20 = (bf16[1280,768]{1,0:T(8,128)(2,1)}, bf16[1280,768]{1,0:T(8,128)(2,1)}, u32[]{:S(2)}, u32[]{:S(2)}) collective-permute-start(bf16[1280,768]{1,0:T(8,128)(2,1)} %collective-permute-done.18.refs_19_), channel_id=1, source_target_pairs={{8,0},{12,4},{16,8},{20,12},{9,1},{13,5},{17,9},{21,13},{10,2},{14... | collective-permute-start | bytes 5898248 | tf_op jit(solution)/shard_map/ppermute | solution.py:323
  176.1 54.9 %collective-permute-start.42 = (bf16[3,256,1024]{2,1,0:T(8,128)(2,1)}, bf16[3,256,1024]{2,1,0:T(8,128)(2,1)S(1)}, u32[]{:S(2)}, u32[]{:S(2)}) collective-permute-start(bf16[3,256,1024]{2,1,0:T(8,128)(2,1)} %pad_maximum_fusion.2), channel_id=1, source_target_pairs={{0,8},{4,12},{1,9},{5,13},{2,10},{6,14},{3,11},{7,15}} | collective-permute-start | bytes 4718600 | tf_op jit(solution)/shard_map/ppermute | solution.py:323
  182.5 49.9 %collective-permute-start.43 = (bf16[3,256,1024]{2,1,0:T(8,128)(2,1)}, bf16[3,256,1024]{2,1,0:T(8,128)(2,1)}, u32[]{:S(2)}, u32[]{:S(2)}) collective-permute-start(bf16[3,256,1024]{2,1,0:T(8,128)(2,1)} %pad_maximum_fusion.3), channel_id=1, source_target_pairs={{24,16},{28,20},{25,17},{29,21},{26,18},{30,22},{27,19},{31,23}} | collective-permute-start | bytes 4718600 | tf_op jit(solution)/shard_map/ppermute | solution.py:323
  196.8 57.7 %collective-permute-start.33 = (bf16[1280,768]{1,0:T(8,128)(2,1)}, bf16[1280,768]{1,0:T(8,128)(2,1)}, u32[]{:S(2)}, u32[]{:S(2)}) collective-permute-start(bf16[1280,768]{1,0:T(8,128)(2,1)} %collective-permute-done.31.refs_19_), channel_id=1, source_target_pairs={{8,0},{12,4},{16,8},{20,12},{9,1},{13,5},{17,9},{21,13},{10,2},{14... | collective-permute-start | bytes 5898248 | tf_op jit(solution)/shard_map/ppermute | solution.py:323
  212.3 65.5 %collective-permute-start.21 = (bf16[1280,768]{1,0:T(8,128)(2,1)}, bf16[1280,768]{1,0:T(8,128)(2,1)S(1)}, u32[]{:S(2)}, u32[]{:S(2)}) collective-permute-start(bf16[1280,768]{1,0:T(8,128)(2,1)} %collective-permute-done.19.refs_16_), channel_id=1, source_target_pairs={{16,24},{20,28},{17,25},{21,29},{18,26},{22,30},{19,27},{23,31}} | collective-permute-start | bytes 5898248 | tf_op jit(solution)/shard_map/ppermute | solution.py:323
  231.0 62.8 %collective-permute-start.22 = (bf16[1280,768]{1,0:T(8,128)(2,1)}, bf16[1280,768]{1,0:T(8,128)(2,1)S(1)}, u32[]{:S(2)}, u32[]{:S(2)}) collective-permute-start(bf16[1280,768]{1,0:T(8,128)(2,1)} %collective-permute-done.20.refs_20_), channel_id=1, source_target_pairs={{8,0},{12,4},{9,1},{13,5},{10,2},{14,6},{11,3},{15,7}} | collective-permute-start | bytes 5898248 | tf_op jit(solution)/shard_map/ppermute | solution.py:323
  254.5 57.6 %collective-permute-start.36 = (bf16[512,1280]{1,0:T(8,128)(2,1)}, bf16[512,1280]{1,0:T(8,128)(2,1)}, u32[]{:S(2)}, u32[]{:S(2)}) collective-permute-start(bf16[512,1280]{1,0:T(8,128)(2,1)} %collective-permute-done.1.refs_8_), channel_id=1, source_target_pairs={{0,4},{4,0},{8,12},{12,8},{16,20},{20,16},{1,5},{5,1},{9,13},{13,9... | collective-permute-start | bytes 3932168 | tf_op jit(solution)/shard_map/ppermute | solution.py:316
  256.4 49.8 %collective-permute-start.44 = (bf16[3,256,1024]{2,1,0:T(8,128)(2,1)}, bf16[3,256,1024]{2,1,0:T(8,128)(2,1)}, u32[]{:S(2)}, u32[]{:S(2)}) collective-permute-start(bf16[3,256,1024]{2,1,0:T(8,128)(2,1)} %pad_maximum_fusion.4), channel_id=1, source_target_pairs={{8,16},{12,20},{9,17},{13,21},{10,18},{14,22},{11,19},{15,23}} | collective-permute-start | bytes 4718600 | tf_op jit(solution)/shard_map/ppermute | solution.py:323
  258.2 48.5 %collective-permute-start.45 = (bf16[3,256,1024]{2,1,0:T(8,128)(2,1)}, bf16[3,256,1024]{2,1,0:T(8,128)(2,1)}, u32[]{:S(2)}, u32[]{:S(2)}) collective-permute-start(bf16[3,256,1024]{2,1,0:T(8,128)(2,1)} %pad_maximum_fusion.5), channel_id=1, source_target_pairs={{16,8},{20,12},{17,9},{21,13},{18,10},{22,14},{19,11},{23,15}} | collective-permute-start | bytes 4718600 | tf_op jit(solution)/shard_map/ppermute | solution.py:323
  277.8 61.4 %collective-permute-start.55 = (bf16[1280,768]{1,0:T(8,128)(2,1)}, bf16[1280,768]{1,0:T(8,128)(2,1)}, u32[]{:S(2)}, u32[]{:S(2)}) collective-permute-start(bf16[1280,768]{1,0:T(8,128)(2,1)} %collective-permute-done.32.refs_16_), channel_id=1, source_target_pairs={{16,24},{20,28},{17,25},{21,29},{18,26},{22,30},{19,27},{23,31}} | collective-permute-start | bytes 5898248 | tf_op jit(solution)/shard_map/ppermute | solution.py:323
  312.1 78.7 %collective-permute-start.46 = (bf16[3,256,1024]{2,1,0:T(8,128)(2,1)}, bf16[3,256,1024]{2,1,0:T(8,128)(2,1)S(1)}, u32[]{:S(2)}, u32[]{:S(2)}) collective-permute-start(bf16[3,256,1024]{2,1,0:T(8,128)(2,1)} %pad_maximum_fusion.6), channel_id=1, source_target_pairs={{16,24},{20,28},{17,25},{21,29},{18,26},{22,30},{19,27},{23,31}} | collective-permute-start | bytes 4718600 | tf_op jit(solution)/shard_map/ppermute | solution.py:323
  334.6 57.6 %collective-permute-start.47 = (bf16[3,256,1024]{2,1,0:T(8,128)(2,1)}, bf16[3,256,1024]{2,1,0:T(8,128)(2,1)}, u32[]{:S(2)}, u32[]{:S(2)}) collective-permute-start(bf16[3,256,1024]{2,1,0:T(8,128)(2,1)} %pad_maximum_fusion.7), channel_id=1, source_target_pairs={{8,0},{12,4},{9,1},{13,5},{10,2},{14,6},{11,3},{15,7}} | collective-permute-start | bytes 4718600 | tf_op jit(solution)/shard_map/ppermute | solution.py:323
  336.8 64.5 %collective-permute-start.66 = (bf16[768,512]{1,0:T(8,128)(2,1)S(1)}, bf16[768,512]{1,0:T(8,128)(2,1)}, u32[]{:S(2)}, u32[]{:S(2)}) collective-permute-start(bf16[768,512]{1,0:T(8,128)(2,1)S(1)} %pad_maximum_fusion.8), channel_id=1, source_target_pairs={{0,4},{4,0},{8,12},{12,8},{16,20},{20,16},{24,28},{28,24},{1,5},{5... | collective-permute-start | bytes 2359304 | tf_op jit(solution)/shard_map/ppermute | solution.py:316
  339.2 47.5 %collective-permute-start.24 = (bf16[672,512]{1,0:T(8,128)(2,1)}, bf16[672,512]{1,0:T(8,128)(2,1)}, u32[]{:S(2)}, u32[]{:S(2)}) collective-permute-start(bf16[672,512]{1,0:T(8,128)(2,1)} %pad_maximum_fusion.11), channel_id=1, source_target_pairs={{8,0},{12,4},{16,8},{20,12},{24,16},{28,20},{9,1},{13,5},{17,9},{2... | collective-permute-start | bytes 2064392 | tf_op jit(solution)/shard_map/ppermute | solution.py:323
  340.5 47.5 %collective-permute-start.23 = (bf16[672,512]{1,0:T(8,128)(2,1)}, bf16[672,512]{1,0:T(8,128)(2,1)}, u32[]{:S(2)}, u32[]{:S(2)}) collective-permute-start(bf16[672,512]{1,0:T(8,128)(2,1)} %pad_maximum_fusion.10), channel_id=1, source_target_pairs={{0,8},{4,12},{8,16},{12,20},{16,24},{20,28},{1,9},{5,13},{9,17},{1... | collective-permute-start | bytes 2064392 | tf_op jit(solution)/shard_map/ppermute | solution.py:323
  386.7 48.8 %collective-permute-start.58 = (bf16[672,512]{1,0:T(8,128)(2,1)S(1)}, bf16[672,512]{1,0:T(8,128)(2,1)S(1)}, u32[]{:S(2)}, u32[]{:S(2)}) collective-permute-start(bf16[672,512]{1,0:T(8,128)(2,1)S(1)} %pad_maximum_fusion.13), channel_id=1, source_target_pairs={{8,0},{12,4},{16,8},{20,12},{24,16},{28,20},{9,1},{13,5},{17,9},{2... | collective-permute-start | bytes 2064392 | tf_op jit(solution)/shard_map/ppermute | solution.py:323
  400.5 96.3 %collective-permute-start.26 = (bf16[512,1280]{1,0:T(8,128)(2,1)}, bf16[512,1280]{1,0:T(8,128)(2,1)S(1)}, u32[]{:S(2)}, u32[]{:S(2)}) collective-permute-start(bf16[512,1280]{1,0:T(8,128)(2,1)} %collective-permute-done.25.refs_2_), channel_id=1, source_target_pairs={{16,24},{20,28},{17,25},{21,29},{18,26},{22,30},{19,27},{23,31}} | collective-permute-start | bytes 3932168 | tf_op jit(solution)/shard_map/ppermute | solution.py:323
  401.3 95.6 %collective-permute-start.28 = (bf16[512,1280]{1,0:T(8,128)(2,1)}, bf16[512,1280]{1,0:T(8,128)(2,1)S(1)}, u32[]{:S(2)}, u32[]{:S(2)}) collective-permute-start(bf16[512,1280]{1,0:T(8,128)(2,1)} %collective-permute-done.25.refs_2_), channel_id=1, source_target_pairs={{16,20},{20,16},{24,28},{28,24},{17,21},{21,17},{25,29},{29,25},{1... | collective-permute-start | bytes 3932168 | tf_op jit(solution)/shard_map/ppermute | solution.py:316
  431.6 68.5 %collective-permute-start.38 = (bf16[512,1280]{1,0:T(8,128)(2,1)}, bf16[512,1280]{1,0:T(8,128)(2,1)}, u32[]{:S(2)}, u32[]{:S(2)}) collective-permute-start(bf16[512,1280]{1,0:T(8,128)(2,1)} %collective-permute-done.37.refs_10_), channel_id=1, source_target_pairs={{0,4},{4,0},{8,12},{12,8},{1,5},{5,1},{9,13},{13,9},{2,6},{6,2},{1... | collective-permute-start | bytes 3932168 | tf_op jit(solution)/shard_map/ppermute | solution.py:316
  435.5 64.9 %collective-permute-start.39 = (bf16[512,1280]{1,0:T(8,128)(2,1)}, bf16[512,1280]{1,0:T(8,128)(2,1)}, u32[]{:S(2)}, u32[]{:S(2)}) collective-permute-start(bf16[512,1280]{1,0:T(8,128)(2,1)} %collective-permute-done.37.refs_10_), channel_id=1, source_target_pairs={{8,0},{12,4},{9,1},{13,5},{10,2},{14,6},{11,3},{15,7}} | collective-permute-start | bytes 3932168 | tf_op jit(solution)/shard_map/ppermute | solution.py:323
  439.3 55.5 %collective-permute-start.67 = (bf16[768,512]{1,0:T(8,128)(2,1)}, bf16[768,512]{1,0:T(8,128)(2,1)S(1)}, u32[]{:S(2)}, u32[]{:S(2)}) collective-permute-start(bf16[768,512]{1,0:T(8,128)(2,1)} %pad_maximum_fusion.9), channel_id=1, source_target_pairs={{0,4},{4,0},{8,12},{12,8},{16,20},{20,16},{24,28},{28,24},{1,5},{5... | collective-permute-start | bytes 2359304 | tf_op jit(solution)/shard_map/ppermute | solution.py:316
  (81 other events, 1651.0 us)
